TPU v7x, 32 devices: a whole 2x2x4 slice. The times are simulated.
32 devices in a mesh: dp: 8 (over y, x, core), head: 4 (over z).
Axes of the slice: x: 2, y: 2, z: 4, core: 2. Of those that a mesh axis runs over, the one named last changes fastest.
Arguments:
- image_tokens: bfloat16 [96, 196, 768], P(('dp', 'head')), may hold values from -6 to 6
- cotangent: bfloat16 [96, 196, 768], P(('dp', 'head')), may hold values from -6 to 6
- weights: float32 [24, 768, 768], P('head', 'dp'), may hold values from -4 to 4
- weights_ema: float32 [24, 768, 768], P('head', 'dp'), may hold values from -0.21875 to 0.21875
- left_stats: float32 [24, 768, 768], P('head', 'dp'), may hold values from -28901376 to 28901376
- right_stats: float32 [24, 768, 768], P('head', 'dp'), may hold values from -28901376 to 28901376
- left_root: float32 [24, 768, 768], P('head', 'dp'), may hold values from -1 to 8
- right_root: float32 [24, 768, 768], P('head', 'dp'), may hold values from -1 to 8
- vectors: float32 [2, 4736], replicated, may hold values from -2 to 3
- vec_first: float32 [2, 4736], replicated, may hold values from -18816 to 18816
- vec_second: float32 [2, 4736], replicated, may hold values from 0 to 18816
Outputs:
- block_out: bfloat16 [96, 196, 768], P(('dp', 'head'))
- input_grad: float32 [96, 196, 768], P(('dp', 'head'))
- weight_grad: float32 [24, 768, 768], P('head', 'dp')
- left_new: float32 [24, 768, 768], P('head', 'dp')
- right_new: float32 [24, 768, 768], P('head', 'dp')
- weight_new: float32 [24, 768, 768], P('head', 'dp')
- ema_new: float32 [24, 768, 768], P('head', 'dp')
- vec_first_new: float32 [2, 4736], replicated
- vec_second_new: float32 [2, 4736], replicated
- vec_new: float32 [2, 4736], replicated
All inputs are finite; a program needn't handle non-finite values.
Results may differ from a plain program's by a relative error of at most 0.014.
Values may be sent and summed in bfloat16 or wider, within the bound.
No kernel may reach another device: no remote copies, remote signals or barrier semaphores. Data moves between devices by JAX's collectives and lax.ppermute only.
A program may use at most 384 MiB of HBM per device.

v0:
```python
import jax
import jax.numpy as jnp
from jax import lax
from jax.sharding import PartitionSpec as P

D = 768
HEADS = 12
HEAD_DIM = 64
FF = 3072
SEQ = 196
LAYERS = 2
STEP = 10


PRECISE = lax.Precision.HIGHEST
EPS_NORM = 1e-06
BETA_ONE = 0.9
BETA_TWO = 0.95
ADAM_EPS = 1e-08
RATE_VEC = 0.3
RATE_MAT = 0.003
DECAY_MAT = 0.1
STAT_DECAY = 0.5
EMA_DECAY = 0.8


def norm_parts(values):
    average = jnp.mean(values, axis=-1, keepdims=True)
    centred = values - average
    inverse = lax.rsqrt(jnp.mean(centred * centred, axis=-1, keepdims=True) + EPS_NORM)
    return (centred * inverse, inverse)


def norm_back(grad_hat, unit, inverse):
    return inverse * (
        grad_hat
        - jnp.mean(grad_hat, axis=-1, keepdims=True)
        - unit * jnp.mean(grad_hat * unit, axis=-1, keepdims=True)
    )


def gelu_exact(values):
    return jax.nn.gelu(values, approximate=False)


def split_vector(row_vec):
    ln_gain = row_vec[:D]
    q_gain = row_vec[D : D + HEAD_DIM]
    k_gain = row_vec[D + HEAD_DIM : D + 2 * HEAD_DIM]
    mlp_bias = row_vec[D + 2 * HEAD_DIM : D + 2 * HEAD_DIM + FF]
    out_bias = row_vec[D + 2 * HEAD_DIM + FF :]
    return (ln_gain, q_gain, k_gain, mlp_bias, out_bias)


def on_device(
    image_tokens,
    cotangent,
    weights,
    weights_ema,
    left_stats,
    right_stats,
    left_root,
    right_root,
    vectors,
    vec_first,
    vec_second,
):
    mlp_ratio = FF // D
    per_layer = 4 + 2 * mlp_ratio
    in_count = 3 + mlp_ratio
    score_scale = HEAD_DIM ** (-0.5)
    heads_local = HEADS // lax.axis_size("head")
    block_rows = lax.all_gather(weights.astype(jnp.bfloat16), "head", axis=0, tiled=True)
    full_blocks = lax.all_gather(block_rows, "dp", axis=1, tiled=True)
    stream = image_tokens.astype(jnp.float32)
    image_count = stream.shape[0]
    group_images = image_count * lax.axis_size("head")
    head_shape = (group_images, SEQ, heads_local, HEAD_DIM)
    merged_shape = (group_images, SEQ, heads_local * HEAD_DIM)
    saved = []
    for depth in range(LAYERS):
        in_blocks = full_blocks[depth * per_layer : depth * per_layer + in_count]
        out_blocks = full_blocks[depth * per_layer + in_count : (depth + 1) * per_layer]
        ln_gain, q_gain, k_gain, mlp_bias, out_bias = split_vector(vectors[depth])
        unit, inverse = norm_parts(stream)
        normed = (unit * ln_gain).astype(jnp.bfloat16)
        mixed_all = jnp.einsum(
            "isk,bkn->isbn", normed, in_blocks, preferred_element_type=jnp.float32
        )
        q_unit, q_inverse = norm_parts(
            mixed_all[:, :, 0].reshape(image_count, SEQ, HEADS, HEAD_DIM)
        )
        k_unit, k_inverse = norm_parts(
            mixed_all[:, :, 1].reshape(image_count, SEQ, HEADS, HEAD_DIM)
        )
        queries = (q_unit * q_gain).astype(jnp.bfloat16).reshape(image_count, SEQ, D)
        key_vecs = (k_unit * k_gain).astype(jnp.bfloat16).reshape(image_count, SEQ, D)
        value_vecs = mixed_all[:, :, 2].astype(jnp.bfloat16)
        pre_act = mixed_all[:, :, 3:].reshape(image_count, SEQ, FF) + mlp_bias
        hidden = gelu_exact(pre_act).astype(jnp.bfloat16)
        q_heads, k_heads, v_heads = (
            lax.all_to_all(queries, "head", split_axis=2, concat_axis=0, tiled=True),
            lax.all_to_all(key_vecs, "head", split_axis=2, concat_axis=0, tiled=True),
            lax.all_to_all(value_vecs, "head", split_axis=2, concat_axis=0, tiled=True),
        )
        q_heads = q_heads.reshape(head_shape)
        k_heads = k_heads.reshape(head_shape)
        v_heads = v_heads.reshape(head_shape)
        scores = (
            jnp.einsum("ishd,ijhd->ihsj", q_heads, k_heads, preferred_element_type=jnp.float32)
            * score_scale
        )
        row_top = jnp.max(scores, axis=-1, keepdims=True)
        log_total = row_top + jnp.log(jnp.sum(jnp.exp(scores - row_top), axis=-1, keepdims=True))
        soft_probs = jnp.exp(scores - log_total).astype(jnp.bfloat16)
        attended = jnp.einsum(
            "ihsj,ijhd->ishd", soft_probs, v_heads, preferred_element_type=jnp.float32
        )
        attended = attended.astype(jnp.bfloat16).reshape(merged_shape)
        attended = lax.all_to_all(attended, "head", split_axis=0, concat_axis=2, tiled=True)
        joined = jnp.concatenate(
            [attended[:, :, None], hidden.reshape(image_count, SEQ, mlp_ratio, D)], axis=2
        )
        branch = (
            jnp.einsum("isbk,bkn->isn", joined, out_blocks, preferred_element_type=jnp.float32)
            + out_bias
        )
        saved.append(
            (
                unit,
                inverse,
                normed,
                q_unit,
                q_inverse,
                k_unit,
                k_inverse,
                pre_act,
                q_heads,
                k_heads,
                v_heads,
                log_total,
                joined,
            )
        )
        stream = stream + branch
    block_out = stream.astype(jnp.bfloat16)
    grad_stream = cotangent.astype(jnp.float32)
    weight_parts = [None] * LAYERS
    vector_parts = [None] * LAYERS
    for depth in reversed(range(LAYERS)):
        (
            unit,
            inverse,
            normed,
            q_unit,
            q_inverse,
            k_unit,
            k_inverse,
            pre_act,
            q_heads,
            k_heads,
            v_heads,
            log_total,
            joined,
        ) = saved[depth]
        in_blocks = full_blocks[depth * per_layer : depth * per_layer + in_count]
        out_blocks = full_blocks[depth * per_layer + in_count : (depth + 1) * per_layer]
        ln_gain, q_gain, k_gain, mlp_bias, out_bias = split_vector(vectors[depth])
        grad_branch = grad_stream.astype(jnp.bfloat16)
        out_bias_grad = jnp.sum(grad_branch.astype(jnp.float32), axis=(0, 1))
        grad_joined = jnp.einsum(
            "isn,bkn->isbk", grad_branch, out_blocks, preferred_element_type=jnp.float32
        )
        grad_att = grad_joined[:, :, 0].astype(jnp.bfloat16)
        gelu_pull = jax.vjp(gelu_exact, pre_act)[1]
        grad_pre = gelu_pull(grad_joined[:, :, 1:].reshape(image_count, SEQ, FF))[0].astype(
            jnp.bfloat16
        )
        mlp_bias_grad = jnp.sum(grad_pre.astype(jnp.float32), axis=(0, 1))
        grad_heads = lax.all_to_all(
            grad_att, "head", split_axis=2, concat_axis=0, tiled=True
        ).reshape(head_shape)
        scores = (
            jnp.einsum("ishd,ijhd->ihsj", q_heads, k_heads, preferred_element_type=jnp.float32)
            * score_scale
        )
        exact_probs = jnp.exp(scores - log_total)
        soft_probs = exact_probs.astype(jnp.bfloat16)
        grad_value = jnp.einsum(
            "ihsj,ishd->ijhd", soft_probs, grad_heads, preferred_element_type=jnp.float32
        ).astype(jnp.bfloat16)
        grad_probs = jnp.einsum(
            "ishd,ijhd->ihsj", grad_heads, v_heads, preferred_element_type=jnp.float32
        )
        row_dot = jnp.sum(exact_probs * grad_probs, axis=-1, keepdims=True)
        grad_scores = (exact_probs * (grad_probs - row_dot)).astype(jnp.bfloat16)
        grad_query = (
            jnp.einsum("ihsj,ijhd->ishd", grad_scores, k_heads, preferred_element_type=jnp.float32)
            * score_scale
        ).astype(jnp.bfloat16)
        grad_key = (
            jnp.einsum("ihsj,ishd->ijhd", grad_scores, q_heads, preferred_element_type=jnp.float32)
            * score_scale
        ).astype(jnp.bfloat16)
        grad_q_tok, grad_k_tok, grad_v_tok = (
            lax.all_to_all(
                grad_query.reshape(merged_shape), "head", split_axis=0, concat_axis=2, tiled=True
            ),
            lax.all_to_all(
                grad_key.reshape(merged_shape), "head", split_axis=0, concat_axis=2, tiled=True
            ),
            lax.all_to_all(
                grad_value.reshape(merged_shape), "head", split_axis=0, concat_axis=2, tiled=True
            ),
        )
        grad_qn = grad_q_tok.astype(jnp.float32).reshape(image_count, SEQ, HEADS, HEAD_DIM)
        grad_kn = grad_k_tok.astype(jnp.float32).reshape(image_count, SEQ, HEADS, HEAD_DIM)
        q_gain_grad = jnp.sum(grad_qn * q_unit, axis=(0, 1, 2))
        k_gain_grad = jnp.sum(grad_kn * k_unit, axis=(0, 1, 2))
        grad_q_raw = (
            norm_back(grad_qn * q_gain, q_unit, q_inverse)
            .astype(jnp.bfloat16)
            .reshape(image_count, SEQ, D)
        )
        grad_k_raw = (
            norm_back(grad_kn * k_gain, k_unit, k_inverse)
            .astype(jnp.bfloat16)
            .reshape(image_count, SEQ, D)
        )
        grad_mixed = jnp.concatenate(
            [
                grad_q_raw[:, :, None],
                grad_k_raw[:, :, None],
                grad_v_tok[:, :, None],
                grad_pre.reshape(image_count, SEQ, mlp_ratio, D),
            ],
            axis=2,
        )
        grad_out_w = jnp.einsum(
            "isbk,isn->bkn", joined, grad_branch, preferred_element_type=jnp.float32
        )
        grad_in_w = jnp.einsum(
            "isk,isbn->bkn", normed, grad_mixed, preferred_element_type=jnp.float32
        )
        weight_parts[depth] = jnp.concatenate([grad_in_w, grad_out_w], axis=0)
        grad_normed = jnp.einsum(
            "isbn,bkn->isk", grad_mixed, in_blocks, preferred_element_type=jnp.float32
        )
        ln_gain_grad = jnp.sum(grad_normed * unit, axis=(0, 1))
        grad_stream = grad_stream + norm_back(grad_normed * ln_gain, unit, inverse)
        vector_parts[depth] = jnp.concatenate(
            [ln_gain_grad, q_gain_grad, k_gain_grad, mlp_bias_grad, out_bias_grad]
        )
    partial_grad = jnp.concatenate(weight_parts, axis=0)
    rows_part = lax.psum_scatter(partial_grad, "dp", scatter_dimension=1, tiled=True)
    weight_grad = lax.psum_scatter(
        rows_part.astype(jnp.bfloat16), "head", scatter_dimension=0, tiled=True
    ).astype(jnp.float32)
    vector_grad = lax.psum(jnp.stack(vector_parts), ("dp", "head"))
    rows_dev = weight_grad.shape[1]
    own_start = lax.axis_index("dp") * rows_dev
    zero_rows = jnp.zeros_like(weight_grad)
    piece = lax.all_gather(weight_grad.astype(jnp.bfloat16), "dp", axis=1, tiled=True).astype(
        jnp.float32
    )
    left_cols = zero_rows
    right_rows = zero_rows
    add_lifted = zero_rows
    gram_piece = jnp.einsum("brk,bck->brc", weight_grad, piece, precision=PRECISE)
    left_cols = lax.dynamic_update_slice_in_dim(left_cols, gram_piece, jnp.int32(0), 2)
    own_cols = lax.dynamic_slice_in_dim(piece, own_start, rows_dev, 2)
    right_rows = right_rows + jnp.einsum("bcr,bck->brk", own_cols, piece, precision=PRECISE)
    add_lifted = add_lifted + jnp.einsum("brc,bck->brk", left_root, piece, precision=PRECISE)
    precond = zero_rows + jnp.einsum(
        "brc,bck->brk",
        add_lifted,
        lax.all_gather(right_root.astype(jnp.bfloat16), "dp", axis=1, tiled=True).astype(
            jnp.float32
        ),
        precision=PRECISE,
    )
    left_new = STAT_DECAY * left_stats + (1.0 - STAT_DECAY) * left_cols
    right_new = STAT_DECAY * right_stats + (1.0 - STAT_DECAY) * right_rows
    weight_new = weights * (1.0 - RATE_MAT * DECAY_MAT) - RATE_MAT * precond
    ema_new = EMA_DECAY * weights_ema + (1.0 - EMA_DECAY) * weight_new
    first_new = BETA_ONE * vec_first + (1.0 - BETA_ONE) * vector_grad
    second_new = BETA_TWO * vec_second + (1.0 - BETA_TWO) * vector_grad * vector_grad
    first_hat = first_new / (1.0 - BETA_ONE**STEP)
    second_hat = second_new / (1.0 - BETA_TWO**STEP)
    vec_new = vectors - RATE_VEC * first_hat / (jnp.sqrt(second_hat) + ADAM_EPS)
    return (
        block_out,
        grad_stream,
        weight_grad,
        left_new,
        right_new,
        weight_new,
        ema_new,
        first_new,
        second_new,
        vec_new,
    )


def solution(mesh):
    placed = (
        P(("dp", "head"), None, None),
        P(("dp", "head"), None, None),
        P("head", "dp", None),
        P("head", "dp", None),
        P("head", "dp", None),
        P("head", "dp", None),
        P("head", "dp", None),
        P("head", "dp", None),
        P(),
        P(),
        P(),
    )
    return jax.shard_map(
        on_device,
        mesh=mesh,
        in_specs=placed,
        out_specs=(
            P(("dp", "head"), None, None),
            P(("dp", "head"), None, None),
            P("head", "dp", None),
            P("head", "dp", None),
            P("head", "dp", None),
            P("head", "dp", None),
            P("head", "dp", None),
            P(),
            P(),
            P(),
        ),
        check_vma=False,
    )
```

profile of v0, /device:TPU:0, one launch (start us, length us, event | category | flops | bytes accessed | tf_op | source)
XLA Modules:
  0.0 1650.0 jit_solution(10066525692378146445)
XLA Ops:
  9.9 73.0 %all-gather.5.cloned.1.call-done = bf16[24,96,768]{2,1,0:T(8,128)(2,1)} async-done(((bf16[6,96,768]{2,1,0:T(8,128)(2,1)}), bf16[24,96,768]{2,1,0:T(8,128)(2,1)}) %all-gather.5.cloned.1.call-update) | async-done | bytes 3538960 | tf_op jit(solution)/shard_map/all_gather | solution.py:73
  84.5 137.6 %all-gather.7.cloned.1.call-done = bf16[24,768,768]{2,1,0:T(8,128)(2,1)} async-done(((bf16[24,96,768]{2,1,0:T(8,128)(2,1)}), bf16[24,768,768]{2,1,0:T(8,128)(2,1)}) %all-gather.7.cloned.1.call-update) | async-done | bytes 28311568 | tf_op jit(solution)/shard_map/all_gather | solution.py:74
  295.5 33.5 %all-to-all-done.1 = bf16[3,196,768]{1,0,2:T(4,128)(2,1)} async-done(((bf16[3,196,768]{1,0,2:T(4,128)(2,1)}), bf16[3,196,768]{1,0,2:T(4,128)(2,1)}, u32[]{:S(2)}, u32[]{:S(2)}) %all-to-all-start.1) | async-done | bytes 903200 | tf_op jit(solution)/shard_map/all_to_all | solution.py:102
  339.3 31.0 %all-to-all-done.2 = bf16[3,196,768]{1,0,2:T(4,128)(2,1)} async-done(((bf16[3,196,768]{1,0,2:T(4,128)(2,1)}), bf16[3,196,768]{1,0,2:T(4,128)(2,1)}, u32[]{:S(2)}, u32[]{:S(2)}) %all-to-all-start.2) | async-done | bytes 903200 | tf_op jit(solution)/shard_map/all_to_all | solution.py:103
  382.4 18.6 %multiply_convert_fusion.3 = (bf16[3,196,4,768]{3,1,2,0:T(8,128)(2,1)}, f32[3,196,4,768]{3,1,2,0:T(8,128)}) fusion(f32[3,196,7,768]{3,1,2,0:T(8,128)} %copy-done.4, f32[4,768]{1,0:T(4,128)S(1)} %add.158), kind=kLoop, calls=%fused_computation.34 | loop fusion | flops 119218176 | bytes 18075648 | tf_op jit(solution)/shard_map/convert_element_type | solution.py:100
  428.5 7.9 fusion.116
  436.8 8.0 fusion.15
  511.7 32.9 %all-to-all-done.5 = bf16[3,196,768]{1,0,2:T(4,128)(2,1)} async-done(((bf16[3,196,768]{1,0,2:T(4,128)(2,1)}), bf16[3,196,768]{1,0,2:T(4,128)(2,1)}, u32[]{:S(2)}, u32[]{:S(2)}) %all-to-all-start.5) | async-done | bytes 903200 | tf_op jit(solution)/shard_map/all_to_all | solution.py:102
  554.5 31.0 %all-to-all-done.6 = bf16[3,196,768]{1,0,2:T(4,128)(2,1)} async-done(((bf16[3,196,768]{1,0,2:T(4,128)(2,1)}), bf16[3,196,768]{1,0,2:T(4,128)(2,1)}, u32[]{:S(2)}, u32[]{:S(2)}) %all-to-all-start.6) | async-done | bytes 903200 | tf_op jit(solution)/shard_map/all_to_all | solution.py:103
  605.9 23.4 %all-to-all-done.9 = bf16[12,196,192]{1,2,0:T(8,128)(2,1)} async-done(((bf16[12,196,192]{1,2,0:T(8,128)(2,1)}), bf16[12,196,192]{1,2,0:T(8,128)(2,1)}, u32[]{:S(2)}, u32[]{:S(2)}) %all-to-all-start.9) | async-done | bytes 903200 | tf_op jit(solution)/shard_map/all_to_all | solution.py:206
  639.7 22.1 %all-to-all-done.10 = bf16[12,196,192]{1,2,0:T(8,128)(2,1)} async-done(((bf16[12,196,192]{1,2,0:T(8,128)(2,1)}), bf16[12,196,192]{1,2,0:T(8,128)(2,1)}, u32[]{:S(2)}, u32[]{:S(2)}) %all-to-all-start.10) | async-done | bytes 903200 | tf_op jit(solution)/shard_map/all_to_all | solution.py:209
  666.2 21.6 %convert_reduce_fusion = (f32[4,768]{1,0:T(4,128)}, bf16[3,196,4,768]{3,1,2,0:T(8,128)(2,1)}, f32[3,196,4,768]{3,1,2,0:T(8,128)}) fusion(f32[3,196,5,768]{3,1,2,0:T(8,128)} %copy-done.34, f32[4,768]{1,0:T(4,128)S(1)} %add.169, f32[3,196,7,768]{3,1,2,0:T(8,128)} %copy-done.5), kind=kLoop, calls=%fused_computation.11 | loop fusion | flops 135472128 | bytes 25313280 | tf_op jit(solution)/shard_map/reduce_sum | solution.py:179
  766.8 9.0 fusion.59
  775.9 11.3 fusion.51
  818.9 8.2 multiply_convert_fusion.2
  833.9 8.4 all-to-all-done.12
  857.9 13.6 convolution_bitcast_fusion
  873.3 12.5 all-to-all-done.14
  890.2 11.9 convert_reduce_fusion.1
  907.7 10.6 all-to-all-done.13
  922.6 11.9 convolution_bitcast_fusion.2
  934.6 8.1 convolution_bitcast_fusion.3
  997.1 10.2 fusion.50
  1007.4 9.2 convolution_bitcast_fusion.1
  1016.6 34.3 %pad_maximum_fusion = f32[24,768,768]{1,2,0:T(8,128)} fusion(f32[5,768,768]{1,2,0:T(8,128)} %convolution_bitcast_fusion.2, f32[7,768,768]{1,2,0:T(8,128)} %convolution_bitcast_fusion, f32[5,768,768]{1,2,0:T(8,128)} %convolution_bitcast_fusion.3, f32[7,768,768]{1,2,0:T(8,128)S(1)} %convolution_bitcast_fusion.1), kind=kLoop, calls=%fused_computation | loop fusion | flops 42467328 | bytes 113246208 | tf_op jit(solution)/shard_map/concatenate | solution.py:254
  1050.9 56.4 %copy.427 = f32[24,768,768]{2,0,1:T(8,128)} copy(f32[24,768,768]{1,2,0:T(8,128)} %pad_maximum_fusion) | data formatting | bytes 113246208 | tf_op jit(solution)/shard_map/concatenate | solution.py:254
  1107.8 318.5 %reduce-scatter.3.cloned.1.call-done = f32[24,96,768]{2,0,1:T(8,128)} async-done(((f32[24,768,768]{2,0,1:T(8,128)}), f32[24,96,768]{2,0,1:T(8,128)}) %reduce-scatter.3.cloned.1.call-update) | async-done | bytes 7077904 | tf_op jit(solution)/shard_map/reduce_scatter | solution.py:255
  1432.3 66.4 %reduce-scatter.5.cloned.1.call-done = bf16[6,96,768]{2,1,0:T(8,128)(2,1)} async-done(((bf16[24,96,768]{2,1,0:T(8,128)(2,1)}), bf16[6,96,768]{2,1,0:T(8,128)(2,1)}) %reduce-scatter.5.cloned.1.call-update) | async-done | bytes 884752 | tf_op jit(solution)/shard_map/reduce_scatter | solution.py:256
  1542.3 9.2 fusion.61
  1557.3 13.0 fusion.41
  1570.5 41.8 %psum.7 = f32[2,4736]{1,0:T(2,128)} all-reduce(f32[2,4736]{1,0:T(2,128)S(1)} %pad_maximum_fusion.17), channel_id=1, replica_groups=mesh['dp'=8,'head'=4] {'dp','head'}, use_global_device_ids=true, to_apply=%region_46.47 | all-reduce | flops 9472 | bytes 75776 | tf_op jit(solution)/shard_map/psum | solution.py:259
  1633.5 9.4 multiply_add_fusion
  (454 shorter events, 519.2 us)
Async XLA Ops:
  7.2 1618.0 %copy-start = (f32[6,96,768]{2,1,0:T(8,128)S(1)}, f32[6,96,768]{2,1,0:T(8,128)}, u32[]{:S(2)}) copy-start(f32[6,96,768]{2,1,0:T(8,128)} %param.17) | copy-start | bytes 5308420
  7.2 75.7 %all-gather.5.cloned.1.call-start = ((), (), s32[]{:S(2)}) async-start(), calls=%async_computation.18 | async-start | bytes 4423680 | tf_op jit(solution)/shard_map/all_gather | solution.py:73
  9.9 212.2 %all-gather.7.cloned.1.call-start = ((), (), s32[]{:S(2)}) async-start(), calls=%async_computation.19 | async-start | bytes 31850496 | tf_op jit(solution)/shard_map/all_gather | solution.py:74
  83.0 146.9 %copy-start.97 = (f32[64]{0:T(128)}, f32[64]{0:T(128)S(1)}, u32[]{:S(2)}) copy-start(f32[64]{0:T(128)S(1)} %get-tuple-element.87) | copy-start | bytes 772
  83.0 250.9 %copy-start.99 = (f32[64]{0:T(128)}, f32[64]{0:T(128)S(1)}, u32[]{:S(2)}) copy-start(f32[64]{0:T(128)S(1)} %get-tuple-element.85) | copy-start | bytes 772
  83.0 251.0 %copy-start.101 = (f32[64]{0:T(128)}, f32[64]{0:T(128)S(1)}, u32[]{:S(2)}) copy-start(f32[64]{0:T(128)S(1)} %get-tuple-element.88) | copy-start | bytes 772
  83.1 194.1 %copy-start.76 = (f32[768]{0:T(1024)}, f32[768]{0:T(1024)S(1)}, u32[]{:S(2)}) copy-start(f32[768]{0:T(1024)S(1)} %mul.671) | copy-start | bytes 9220
  83.2 194.1 %copy-start.78 = (f32[768]{0:T(1024)}, f32[768]{0:T(1024)S(1)}, u32[]{:S(2)}) copy-start(f32[768]{0:T(1024)S(1)} %mul.662) | copy-start | bytes 9220
  83.8 146.1 %copy-start.85 = (f32[768]{0:T(1024)}, f32[768]{0:T(1024)S(1)}, u32[]{:S(2)}) copy-start(f32[768]{0:T(1024)S(1)} %get-tuple-element.57) | copy-start | bytes 9220
  83.8 353.0 %copy-start.87 = (f32[768]{0:T(1024)}, f32[768]{0:T(1024)S(1)}, u32[]{:S(2)}) copy-start(f32[768]{0:T(1024)S(1)} %get-tuple-element.55) | copy-start | bytes 9220
  84.0 145.9 %copy-start.81 = (f32[3,196]{1,0:T(4,128)}, f32[3,196]{1,0:T(4,128)S(1)}, u32[]{:S(2)}) copy-start(f32[3,196]{1,0:T(4,128)S(1)} %broadcast_multiply_fusion.17) | copy-start | bytes 7060
  84.5 145.5 %copy-start.89 = (f32[3,196]{1,0:T(4,128)}, f32[3,196]{1,0:T(4,128)S(1)}, u32[]{:S(2)}) copy-start(f32[3,196]{1,0:T(4,128)S(1)} %add_rsqrt_fusion.5) | copy-start | bytes 7060
  238.9 48.0 %all-to-all-start = ((bf16[3,196,768]{1,0,2:T(4,128)(2,1)}), bf16[3,196,768]{1,0,2:T(4,128)(2,1)S(1)}, u32[]{:S(2)}, u32[]{:S(2)}) async-start(bf16[3,196,768]{1,0,2:T(4,128)(2,1)} %copy.341), calls=%async_computation | async-start | bytes 3145728 | tf_op jit(solution)/shard_map/all_to_all | solution.py:104
  286.9 42.0 %all-to-all-start.1 = ((bf16[3,196,768]{1,0,2:T(4,128)(2,1)}), bf16[3,196,768]{1,0,2:T(4,128)(2,1)}, u32[]{:S(2)}, u32[]{:S(2)}) async-start(bf16[3,196,768]{1,0,2:T(4,128)(2,1)} %copy.347), calls=%async_computation.1 | async-start | bytes 3145728 | tf_op jit(solution)/shard_map/all_to_all | solution.py:102
  328.9 41.4 %all-to-all-start.2 = ((bf16[3,196,768]{1,0,2:T(4,128)(2,1)}), bf16[3,196,768]{1,0,2:T(4,128)(2,1)}, u32[]{:S(2)}, u32[]{:S(2)}) async-start(bf16[3,196,768]{1,0,2:T(4,128)(2,1)} %copy.353), calls=%async_computation.2 | async-start | bytes 3145728 | tf_op jit(solution)/shard_map/all_to_all | solution.py:103
  378.8 36.6 %all-to-all-start.3 = ((bf16[12,196,192]{1,2,0:T(8,128)(2,1)}), bf16[12,196,192]{1,2,0:T(8,128)(2,1)S(1)}, u32[]{:S(2)}, u32[]{:S(2)}) async-start(bf16[12,196,192]{1,2,0:T(8,128)(2,1)} %bitcast.470), calls=%async_computation.3 | async-start | bytes 2359296 | tf_op jit(solution)/shard_map/all_to_all | solution.py:120
  416.4 46.6 %all-to-all-start.8 = ((bf16[3,196,768]{1,0,2:T(4,128)(2,1)}), bf16[3,196,768]{1,0,2:T(4,128)(2,1)}, u32[]{:S(2)}, u32[]{:S(2)}) async-start(bf16[3,196,768]{1,0,2:T(4,128)(2,1)} %copy.377), calls=%async_computation.8 | async-start | bytes 3145728 | tf_op jit(solution)/shard_map/all_to_all | solution.py:180
  463.0 40.7 %all-to-all-start.4 = ((bf16[3,196,768]{1,0,2:T(4,128)(2,1)}), bf16[3,196,768]{1,0,2:T(4,128)(2,1)S(1)}, u32[]{:S(2)}, u32[]{:S(2)}) async-start(bf16[3,196,768]{1,0,2:T(4,128)(2,1)} %copy.359), calls=%async_computation.4 | async-start | bytes 3145728 | tf_op jit(solution)/shard_map/all_to_all | solution.py:104
  503.7 40.9 %all-to-all-start.5 = ((bf16[3,196,768]{1,0,2:T(4,128)(2,1)}), bf16[3,196,768]{1,0,2:T(4,128)(2,1)}, u32[]{:S(2)}, u32[]{:S(2)}) async-start(bf16[3,196,768]{1,0,2:T(4,128)(2,1)} %copy.365), calls=%async_computation.5 | async-start | bytes 3145728 | tf_op jit(solution)/shard_map/all_to_all | solution.py:102
  544.5 40.9 %all-to-all-start.6 = ((bf16[3,196,768]{1,0,2:T(4,128)(2,1)}), bf16[3,196,768]{1,0,2:T(4,128)(2,1)}, u32[]{:S(2)}, u32[]{:S(2)}) async-start(bf16[3,196,768]{1,0,2:T(4,128)(2,1)} %copy.371), calls=%async_computation.6 | async-start | bytes 3145728 | tf_op jit(solution)/shard_map/all_to_all | solution.py:103
  596.9 32.4 %all-to-all-start.9 = ((bf16[12,196,192]{1,2,0:T(8,128)(2,1)}), bf16[12,196,192]{1,2,0:T(8,128)(2,1)}, u32[]{:S(2)}, u32[]{:S(2)}) async-start(bf16[12,196,192]{1,2,0:T(8,128)(2,1)} %bitcast.475), calls=%async_computation.9 | async-start | bytes 2359296 | tf_op jit(solution)/shard_map/all_to_all | solution.py:206
  629.2 32.6 %all-to-all-start.10 = ((bf16[12,196,192]{1,2,0:T(8,128)(2,1)}), bf16[12,196,192]{1,2,0:T(8,128)(2,1)}, u32[]{:S(2)}, u32[]{:S(2)}) async-start(bf16[12,196,192]{1,2,0:T(8,128)(2,1)} %bitcast.473), calls=%async_computation.10 | async-start | bytes 2359296 | tf_op jit(solution)/shard_map/all_to_all | solution.py:209
  661.9 61.4 %all-to-all-start.11 = ((bf16[12,196,192]{1,2,0:T(8,128)(2,1)}), bf16[12,196,192]{1,2,0:T(8,128)(2,1)}, u32[]{:S(2)}, u32[]{:S(2)}) async-start(bf16[12,196,192]{1,2,0:T(8,128)(2,1)} %bitcast.468), calls=%async_computation.11 | async-start | bytes 2359296 | tf_op jit(solution)/shard_map/all_to_all | solution.py:212
  723.2 78.3 %all-to-all-start.7 = ((bf16[12,196,192]{1,2,0:T(8,128)(2,1)}), bf16[12,196,192]{1,2,0:T(8,128)(2,1)}, u32[]{:S(2)}, u32[]{:S(2)}) async-start(bf16[12,196,192]{1,2,0:T(8,128)(2,1)} %bitcast.61), calls=%async_computation.7 | async-start | bytes 2359296 | tf_op jit(solution)/shard_map/all_to_all | solution.py:120
  801.6 40.7 %all-to-all-start.12 = ((bf16[3,196,768]{1,0,2:T(4,128)(2,1)}), bf16[3,196,768]{1,0,2:T(4,128)(2,1)}, u32[]{:S(2)}, u32[]{:S(2)}) async-start(bf16[3,196,768]{1,0,2:T(4,128)(2,1)} %copy.401), calls=%async_computation.12 | async-start | bytes 3145728 | tf_op jit(solution)/shard_map/all_to_all | solution.py:180
  853.9 31.9 %all-to-all-start.14 = ((bf16[12,196,192]{1,2,0:T(8,128)(2,1)}), bf16[12,196,192]{1,2,0:T(8,128)(2,1)S(1)}, u32[]{:S(2)}, u32[]{:S(2)}) async-start(bf16[12,196,192]{1,2,0:T(8,128)(2,1)} %bitcast.474), calls=%async_computation.14 | async-start | bytes 2359296 | tf_op jit(solution)/shard_map/all_to_all | solution.py:209
  885.9 32.4 %all-to-all-start.13 = ((bf16[12,196,192]{1,2,0:T(8,128)(2,1)}), bf16[12,196,192]{1,2,0:T(8,128)(2,1)}, u32[]{:S(2)}, u32[]{:S(2)}) async-start(bf16[12,196,192]{1,2,0:T(8,128)(2,1)} %bitcast.472), calls=%async_computation.13 | async-start | bytes 2359296 | tf_op jit(solution)/shard_map/all_to_all | solution.py:206
  918.3 41.0 %all-to-all-start.15 = ((bf16[12,196,192]{1,2,0:T(8,128)(2,1)}), bf16[12,196,192]{1,2,0:T(8,128)(2,1)}, u32[]{:S(2)}, u32[]{:S(2)}) async-start(bf16[12,196,192]{1,2,0:T(8,128)(2,1)} %bitcast.469), calls=%async_computation.15 | async-start | bytes 2359296 | tf_op jit(solution)/shard_map/all_to_all | solution.py:212
  922.6 503.8 %reduce-scatter.3.cloned.1.call-start = ((), (), s32[]{:S(2)}) async-start(), calls=%async_computation.20 | async-start | bytes 63700992 | tf_op jit(solution)/shard_map/reduce_scatter | solution.py:255
  1107.3 391.4 %reduce-scatter.5.cloned.1.call-start = ((), (), s32[]{:S(2)}) async-start(), calls=%async_computation.21 | async-start | bytes 4423680 | tf_op jit(solution)/shard_map/reduce_scatter | solution.py:256
  1432.2 186.3 %all-gather.9.cloned.1.call-start = ((), (), s32[]{:S(2)}) async-start(), calls=%async_computation.22 | async-start | bytes 7962624 | tf_op jit(solution)/shard_map/all_gather | solution.py:263
  1498.7 134.8 %all-gather.11.cloned.1.call-start = ((), (), s32[]{:S(2)}) async-start(), calls=%async_computation.23 | async-start | bytes 7962624 | tf_op jit(solution)/shard_map/all_gather | solution.py:277
  (97 other events, 990.3 us)
Sparse Core Ops, SparseCore 0:
  10.2 72.6 all-gather.4
  84.8 137.2 all-gather.6
  1107.4 318.8 reduce-scatter.2
  1432.3 66.3 reduce-scatter.4
  1500.6 49.1 all-gather.8
  1551.7 49.2 all-gather.10
where the time goes:
time: 1660 us; the launch traced here: 1650 us
  waiting for transfers between devices  802 us (48%)
  local copies, waits for them, and re-layouts  340 us (20%)
  other arithmetic  197 us (12%)
  matrix products  179 us (11%)
  starting transfers between devices  74.6 us (4%)
  blocking collectives  41.8 us (3%)
    reduce_scatter x1, waiting for transfers between devices, on_device(): lax.psum_scatter(partial_grad, 'dp', scatter_dimension=1, tiled=True)  319 us
    all_gather x1, waiting for transfers between devices, on_device(): full_blocks = lax.all_gather(block_rows, 'dp', axis=1, tiled=True)  138 us
    all_gather x1, waiting for transfers between devices, on_device(): lax.all_gather(weights.astype(jnp.bfloat16), 'head', axis=0, tiled=True)  73 us
    reduce_scatter x1, waiting for transfers between devices, on_device(): lax.psum_scatter(rows_part.astype(jnp.bfloat16), 'head', scatter_dimensio...  66.4 us
    all_to_all x2, waiting for transfers between devices, on_device(): lax.all_to_all(queries, 'head', split_axis=2, concat_axis=0, tiled=True)  66.3 us
    all_to_all x2, waiting for transfers between devices, on_device(): lax.all_to_all(key_vecs, 'head', split_axis=2, concat_axis=0, tiled=True)  62 us
    concatenate x1, local copies, waits for them, and re-layouts, on_device(): partial_grad = jnp.concatenate(weight_parts, axis=0)  56.4 us
    psum x1, blocking collectives, on_device(): vector_grad = lax.psum(jnp.stack(vector_parts), ('dp', 'head'))  41.8 us
  transfers between devices with their start and end apart: 22, of which 14 were waited for; matrix products, arithmetic and copies ran while one was open for 29% of the time, Pallas kernels for 0%

commit v1 on v0

v1 whole, which is shorter than its diff:
```python
import functools
import math

import jax
import jax.numpy as jnp
from jax import lax
from jax.experimental import pallas as pl
from jax.experimental.pallas import tpu as pltpu
from jax.sharding import PartitionSpec as P

D = 768
HEADS = 12
HEAD_DIM = 64
FF = 3072
SEQ = 196
PAD = 208
LAYERS = 2
STEP = 10
RATIO = FF // D
IN_COUNT = 3 + RATIO
OUT_COUNT = 1 + RATIO
PER_LAYER = IN_COUNT + OUT_COUNT
PAIR = 2 * HEAD_DIM
TILE = 256

EPS_NORM = 1e-06
BETA_ONE = 0.9
BETA_TWO = 0.95
ADAM_EPS = 1e-08
RATE_VEC = 0.3
RATE_MAT = 0.003
DECAY_MAT = 0.1
STAT_DECAY = 0.5
EMA_DECAY = 0.8
SCALE = HEAD_DIM ** (-0.5)
EXP2_SCALE = SCALE * math.log2(math.e)

BF = jnp.bfloat16
F32 = jnp.float32
NN = (((1,), (0,)), ((), ()))
NT = (((1,), (1,)), ((), ()))
TN = (((0,), (0,)), ((), ()))


def dot(a, b, dims=NN):
    return lax.dot_general(a, b, dims, preferred_element_type=F32)


def call(kernel, grid, operands, in_specs, outs, out_specs, scratch, flops, name):
    moved = sum(o.size * o.dtype.itemsize for o in operands) + sum(
        math.prod(o.shape) * o.dtype.itemsize for o in outs
    )
    return pl.pallas_call(
        kernel,
        grid=grid,
        in_specs=in_specs,
        out_specs=out_specs,
        out_shape=outs,
        scratch_shapes=scratch,
        compiler_params=pltpu.CompilerParams(vmem_limit_bytes=56 * 1024 * 1024),
        cost_estimate=pl.CostEstimate(flops=flops, bytes_accessed=moved, transcendentals=0),
        name=name,
    )(*operands)


def whole(shape):
    return pl.BlockSpec(shape, lambda *ids: (0,) * len(shape))


def sds(shape, dtype):
    return jax.ShapeDtypeStruct(shape, dtype)


def block_total(units):
    return sum(count for _, _, count in units)


def piece_operands(units):
    arrays, specs, start = [], [], 0
    for pieces, first, count in units:
        for piece in pieces:
            arrays.append(piece)
            specs.append(
                pl.BlockSpec(
                    (1,) + piece.shape[1:],
                    functools.partial(
                        lambda at, first, count, j: (first + jnp.clip(j - at, 0, count - 1), 0, 0),
                        start,
                        first,
                        count,
                    ),
                )
            )
        start += count
    return arrays, specs


def read_block(j, units, refs, held, offsets):
    if len(units) == 1 and len(units[0][0]) == 1:
        return refs[0][0]
    start, at = 0, 0
    for pieces, _, count in units:
        mine = refs[at : at + len(pieces)]

        @pl.when((j >= start) & (j < start + count))
        def _(mine=mine):
            rows_at = offsets(len(mine))
            for ref, row in zip(mine, rows_at):
                rows = ref.shape[1]
                held[pl.ds(pl.multiple_of(row, 16), rows), :] = ref[0]

        start += count
        at += len(pieces)
    return held[...]


def piece_rows(count):
    if count == 1:
        return [0]
    me = lax.axis_index("dp")
    rows = D // count
    core, x, y = lax.rem(me, 2), lax.rem(me // 2, 2), me // 4
    return [
        ((y + dy - 2 * y * dy) * 4 + (x + dx - 2 * x * dx) * 2 + (core + dc - 2 * core * dc)) * rows
        for dy in (0, 1)
        for dx in (0, 1)
        for dc in (0, 1)
    ]


def row_parts(values):
    average = jnp.mean(values, axis=-1, keepdims=True)
    centred = values - average
    inverse = lax.rsqrt(jnp.mean(centred * centred, axis=-1, keepdims=True) + EPS_NORM)
    return centred * inverse, inverse


def head_mixer():
    row = lax.broadcasted_iota(jnp.int32, (TILE, TILE), 0) // HEAD_DIM
    column = lax.broadcasted_iota(jnp.int32, (TILE, TILE), 1) // HEAD_DIM
    return jnp.where(row == column, 1.0 / HEAD_DIM, 0.0).astype(BF)


def head_mean(values, mixer):
    high = values.astype(BF)
    low = (values - high.astype(F32)).astype(BF)
    return jnp.concatenate(
        [
            dot(high[:, at : at + TILE], mixer) + dot(low[:, at : at + TILE], mixer)
            for at in range(0, D, TILE)
        ],
        axis=1,
    )


def gelu_parts(z):
    decay = jnp.exp(-0.5 * z * z)
    t = 1.0 / (1.0 + 0.3275911 * math.sqrt(0.5) * jnp.abs(z))
    poly = t * (
        0.254829592
        + t * (-0.284496736 + t * (1.421413741 + t * (-1.453152027 + t * 1.061405429)))
    )
    tail = 0.5 * poly * decay
    share = jnp.where(z >= 0, 1.0 - tail, tail)
    return z * share, share + z * decay * (1.0 / math.sqrt(2.0 * math.pi))


def row_steps(total, size, body):
    def step(i, carry):
        body(pl.ds(pl.multiple_of(i * size, size), size))
        return carry

    lax.fori_loop(0, total // size, step, 0)


def mlp_in(stream, gain, bias, units):
    tokens = stream.shape[0]
    weights, w_specs = piece_operands(units)

    def kernel(x_ref, g_ref, b_ref, *refs):
        w_refs, (h_ref, a_ref, s_ref, held, wide) = refs[: len(weights)], refs[len(weights) :]
        j = pl.program_id(0)

        @pl.when(j == 0)
        def _():
            def body(rows):
                unit, _ = row_parts(x_ref[rows, :].astype(F32))
                h_ref[rows, :] = (unit * g_ref[...]).astype(BF)

            row_steps(tokens, 48, body)

        wide[...] = dot(h_ref[...], read_block(j, units, w_refs, held, piece_rows))

        def body(rows):
            act, slope = gelu_parts(wide[rows, :] + b_ref[...])
            a_ref[rows, :] = act.astype(BF)
            s_ref[rows, :] = slope.astype(BF)

        row_steps(tokens, 16, body)

    return call(
        kernel,
        (RATIO,),
        [stream, gain, bias] + weights,
        [whole((tokens, D)), whole((1, D)), pl.BlockSpec((1, D), lambda j: (0, j))] + w_specs,
        [sds((tokens, D), BF), sds((tokens, FF), BF), sds((tokens, FF), BF)],
        [whole((tokens, D))] + [pl.BlockSpec((tokens, D), lambda j: (0, j))] * 2,
        [pltpu.VMEM((D, D), BF), pltpu.VMEM((tokens, D), F32)],
        2 * tokens * D * FF,
        "mlp_in",
    )


def half_masks(rows):
    low = lax.broadcasted_iota(jnp.int32, (rows, PAIR), 1) < HEAD_DIM
    return low


def split_pair(values, low):
    zero = jnp.zeros_like(values)
    return jnp.where(low, values, zero), jnp.where(low, zero, values)


def attend(normed, q_gain, k_gain, units):
    tokens = normed.shape[0]
    images = tokens // PAD
    weights, w_specs = piece_operands(units)

    def kernel(h_ref, gq_ref, gk_ref, *refs):
        w_refs = refs[: len(weights)]
        q_ref, k_ref, v_ref, qu_ref, qi_ref, ku_ref, ki_ref, o_ref, held, wide = refs[len(weights) :]
        j = pl.program_id(0)
        wide[...] = dot(h_ref[...], read_block(j, units, w_refs, held, piece_rows))

        def normalise(g_ref, n_ref, u_ref, i_ref):
            mixer = head_mixer()

            def body(rows):
                raw = wide[rows, :]
                centred = raw - head_mean(raw, mixer)
                inverse = lax.rsqrt(head_mean(centred * centred, mixer) + EPS_NORM)
                unit = centred * inverse
                n_ref[rows, :] = (unit * g_ref[...]).astype(BF)
                u_ref[rows, :] = unit.astype(BF)
                i_ref[rows, :] = inverse

            row_steps(tokens, 208, body)

        @pl.when(j == 0)
        def _():
            normalise(gq_ref, q_ref, qu_ref, qi_ref)

        @pl.when(j == 1)
        def _():
            normalise(gk_ref, k_ref, ku_ref, ki_ref)

        @pl.when(j == 2)
        def _():
            v_ref[...] = wide[...].astype(BF)
            low = half_masks(PAD)
            valid = lax.broadcasted_iota(jnp.int32, (PAD, PAD), 1) < SEQ

            def body(pair, carry):
                lanes = pl.ds(pl.multiple_of(pair * PAIR, PAIR), PAIR)
                for image in range(images):
                    rows = pl.ds(image * PAD, PAD)
                    keys, values = k_ref[rows, lanes], v_ref[rows, lanes]
                    sides = []
                    for query in split_pair(q_ref[rows, lanes], low):
                        raised = jnp.exp2(dot(query, keys, NT) * EXP2_SCALE)
                        raised = jnp.where(valid, raised, 0.0)
                        total = jnp.sum(raised, axis=1, keepdims=True)
                        sides.append(dot(raised.astype(BF), values) * (1.0 / total))
                    o_ref[rows, lanes] = jnp.where(low, sides[0], sides[1]).astype(BF)
                return carry

            lax.fori_loop(0, HEADS // 2, body, 0)

    flat = sds((tokens, D), BF)
    flat32 = sds((tokens, D), F32)
    return call(
        kernel,
        (3,),
        [normed, q_gain, k_gain] + weights,
        [whole((tokens, D)), whole((1, D)), whole((1, D))] + w_specs,
        [flat, flat, flat, flat, flat32, flat, flat32, flat],
        [whole((tokens, D))] * 8,
        [pltpu.VMEM((D, D), BF), pltpu.VMEM((tokens, D), F32)],
        2 * tokens * D * 3 * D + 4 * tokens * PAD * D,
        "attend",
    )


def project(stream, attended, hidden, bias, units, last):
    tokens = stream.shape[0]
    weights, w_specs = piece_operands(units)

    def kernel(x_ref, o_ref, a_ref, b_ref, *refs):
        w_refs, (y_ref, total, held) = refs[: len(weights)], refs[len(weights) :]
        j = pl.program_id(0)
        block = read_block(j, units, w_refs, held, piece_rows)

        @pl.when(j == 0)
        def _():
            total[...] = x_ref[...].astype(F32) + b_ref[...] + dot(o_ref[...], block)

        @pl.when(j > 0)
        def _():
            total[...] += dot(a_ref[...], block)

        @pl.when(j == OUT_COUNT - 1)
        def _():
            y_ref[...] = total[...].astype(y_ref.dtype)

    return call(
        kernel,
        (OUT_COUNT,),
        [stream, attended, hidden, bias] + weights,
        [
            whole((tokens, D)),
            whole((tokens, D)),
            pl.BlockSpec((tokens, D), lambda j: (0, jnp.maximum(j - 1, 0))),
            whole((1, D)),
        ]
        + w_specs,
        [sds((tokens, D), BF if last else F32)],
        [whole((tokens, D))],
        [pltpu.VMEM((tokens, D), F32), pltpu.VMEM((D, D), BF)],
        2 * tokens * D * OUT_COUNT * D,
        "project",
    )[0]


def mlp_back(grad, slope, units):
    tokens = grad.shape[0]
    weights, w_specs = piece_operands(units)

    def kernel(g_ref, s_ref, *refs):
        w_refs = refs[: len(weights)]
        dy_ref, do_ref, du_ref, dbo_ref, dbu_ref, held = refs[len(weights) :]
        j = pl.program_id(0)

        @pl.when(j == 0)
        def _():
            dy = g_ref[...].astype(BF)
            dy_ref[...] = dy
            dbo_ref[...] = jnp.sum(dy.astype(F32), axis=0, keepdims=True)

        wide = dot(dy_ref[...], read_block(j, units, w_refs, held, piece_rows), NT)

        @pl.when(j == 0)
        def _():
            do_ref[...] = wide.astype(BF)

        @pl.when(j > 0)
        def _():
            du = (wide * s_ref[...].astype(F32)).astype(BF)
            du_ref[...] = du
            dbu_ref[...] = jnp.sum(du.astype(F32), axis=0, keepdims=True)

    shifted = pl.BlockSpec((tokens, D), lambda j: (0, jnp.maximum(j - 1, 0)))
    return call(
        kernel,
        (OUT_COUNT,),
        [grad, slope] + weights,
        [whole((tokens, D)), shifted] + w_specs,
        [
            sds((tokens, D), BF),
            sds((tokens, D), BF),
            sds((tokens, FF), BF),
            sds((1, D), F32),
            sds((1, FF), F32),
        ],
        [
            whole((tokens, D)),
            whole((tokens, D)),
            shifted,
            whole((1, D)),
            pl.BlockSpec((1, D), lambda j: (0, jnp.maximum(j - 1, 0))),
        ],
        [pltpu.VMEM((D, D), BF)],
        2 * tokens * D * OUT_COUNT * D,
        "mlp_back",
    )


def attend_back(grad_o, queries, keys, values, q_unit, q_inverse, k_unit, k_inverse, q_gain, k_gain):
    tokens = grad_o.shape[0]
    images = tokens // PAD

    def kernel(
        do_ref, q_ref, k_ref, v_ref, qu_ref, qi_ref, ku_ref, ki_ref, gq_ref, gk_ref,
        dz_ref, dgq_ref, dgk_ref, dq_held, dk_held,
    ):
        low = half_masks(PAD)
        valid = lax.broadcasted_iota(jnp.int32, (PAD, PAD), 0) < SEQ

        def body(pair, carry):
            lanes = pl.ds(pl.multiple_of(pair * PAIR, PAIR), PAIR)
            for image in range(images):
                rows = pl.ds(image * PAD, PAD)
                key, value = k_ref[rows, lanes], v_ref[rows, lanes]
                sides = []
                for query, grad in zip(
                    split_pair(q_ref[rows, lanes], low), split_pair(do_ref[rows, lanes], low)
                ):
                    raised = jnp.exp2(dot(key, query, NT) * EXP2_SCALE)
                    raised = jnp.where(valid, raised, 0.0)
                    probs = raised * (1.0 / jnp.sum(raised, axis=0, keepdims=True))
                    grad_probs = dot(value, grad, NT)
                    mixed = probs * grad_probs
                    row_dot = jnp.sum(mixed, axis=0, keepdims=True)
                    scores = (mixed - probs * row_dot).astype(BF)
                    sides.append(
                        (
                            dot(scores, key, TN),
                            dot(scores, query),
                            dot(probs.astype(BF), grad),
                        )
                    )
                dq_held[rows, lanes] = (jnp.where(low, sides[0][0], sides[1][0]) * SCALE).astype(BF)
                dk_held[rows, lanes] = ((sides[0][1] + sides[1][1]) * SCALE).astype(BF)
                dz_ref[rows, pl.ds(pl.multiple_of(2 * D + pair * PAIR, PAIR), PAIR)] = (
                    sides[0][2] + sides[1][2]
                ).astype(BF)
            return carry

        lax.fori_loop(0, HEADS // 2, body, 0)
        mixer = head_mixer()
        for held, u_ref, i_ref, g_ref, dg_ref, at in (
            (dq_held, qu_ref, qi_ref, gq_ref, dgq_ref, 0),
            (dk_held, ku_ref, ki_ref, gk_ref, dgk_ref, D),
        ):
            dg_ref[...] = jnp.zeros_like(dg_ref)

            def body(rows):
                grad, unit = held[rows, :].astype(F32), u_ref[rows, :].astype(F32)
                dg_ref[...] += jnp.sum(grad * unit, axis=0, keepdims=True)
                hat = grad * g_ref[...]
                out = i_ref[rows, :] * (
                    hat - head_mean(hat, mixer) - unit * head_mean(hat * unit, mixer)
                )
                dz_ref[rows, pl.ds(at, D)] = out.astype(BF)

            row_steps(tokens, 208, body)

    return call(
        kernel,
        (1,),
        [grad_o, queries, keys, values, q_unit, q_inverse, k_unit, k_inverse, q_gain, k_gain],
        [whole((tokens, D))] * 8 + [whole((1, D))] * 2,
        [sds((tokens, 3 * D), BF), sds((1, D), F32), sds((1, D), F32)],
        [whole((tokens, 3 * D)), whole((1, D)), whole((1, D))],
        [pltpu.VMEM((tokens, D), BF), pltpu.VMEM((tokens, D), BF)],
        10 * tokens * PAD * D,
        "attend_back",
    )


def weight_grads(left, right, count, name):
    tokens = left.shape[0]

    def kernel(l_ref, r_ref, out_ref):
        out_ref[0] = dot(l_ref[...], r_ref[...], TN).astype(BF)

    def spec(array):
        wide = array.shape[1] > D
        return pl.BlockSpec((tokens, D), (lambda j: (0, j)) if wide else (lambda j: (0, 0)))

    return call(
        kernel,
        (count,),
        [left, right],
        [spec(left), spec(right)],
        [sds((count, D, D), BF)],
        [pl.BlockSpec((1, D, D), lambda j: (j, 0, 0))],
        [],
        2 * tokens * D * count * D,
        name,
    )[0]


def stream_back(grad, stream, gain, grad_u, grad_qkv, units):
    tokens = grad.shape[0]
    weights, w_specs = piece_operands(units)

    def kernel(g_ref, x_ref, c_ref, du_ref, dz_ref, *refs):
        w_refs, (out_ref, dg_ref, total, held) = refs[: len(weights)], refs[len(weights) :]
        j = pl.program_id(0)
        block = read_block(j, units, w_refs, held, piece_rows)

        @pl.when(j == 0)
        def _():
            total[...] = dot(du_ref[...], block, NT)

        @pl.when((j > 0) & (j < RATIO))
        def _():
            total[...] += dot(du_ref[...], block, NT)

        @pl.when(j >= RATIO)
        def _():
            total[...] += dot(dz_ref[...], block, NT)

        @pl.when(j == IN_COUNT - 1)
        def _():
            dg_ref[...] = jnp.zeros_like(dg_ref)

            def body(rows):
                unit, inverse = row_parts(x_ref[rows, :].astype(F32))
                grad_h = total[rows, :]
                dg_ref[...] += jnp.sum(grad_h * unit, axis=0, keepdims=True)
                hat = grad_h * c_ref[...]
                out_ref[rows, :] = g_ref[rows, :].astype(F32) + inverse * (
                    hat
                    - jnp.mean(hat, axis=-1, keepdims=True)
                    - unit * jnp.mean(hat * unit, axis=-1, keepdims=True)
                )

            row_steps(tokens, 48, body)

    return call(
        kernel,
        (IN_COUNT,),
        [grad, stream, gain, grad_u, grad_qkv] + weights,
        [
            whole((tokens, D)),
            whole((tokens, D)),
            whole((1, D)),
            pl.BlockSpec((tokens, D), lambda j: (0, jnp.minimum(j, RATIO - 1))),
            pl.BlockSpec((tokens, D), lambda j: (0, jnp.maximum(j - RATIO, 0))),
        ]
        + w_specs,
        [sds((tokens, D), F32), sds((1, D), F32)],
        [whole((tokens, D)), whole((1, D))],
        [pltpu.VMEM((tokens, D), F32), pltpu.VMEM((D, D), BF)],
        2 * tokens * D * IN_COUNT * D,
        "stream_back",
    )


def shampoo(grad, full, right_full, left_root, left_stats, right_stats, weights, ema):
    count, rows, _ = grad.shape

    def kernel(g_ref, f_ref, r_ref, lr_ref, ls_ref, rs_ref, w_ref, e_ref, lo_ref, ro_ref, wo_ref, eo_ref):
        at = lax.axis_index("dp") * rows
        block = f_ref[0]
        gram = dot(g_ref[0].astype(BF), block, NT)
        lo_ref[0] = STAT_DECAY * ls_ref[0] + (1.0 - STAT_DECAY) * gram
        pick = (
            lax.broadcasted_iota(jnp.int32, (rows, D), 1)
            == lax.broadcasted_iota(jnp.int32, (rows, D), 0) + at
        )
        columns = dot(jnp.where(pick, 1.0, 0.0).astype(BF), block, NT).astype(BF)
        ro_ref[0] = STAT_DECAY * rs_ref[0] + (1.0 - STAT_DECAY) * dot(columns, block)
        lifted = dot(lr_ref[0].astype(BF), block).astype(BF)
        precond = dot(lifted, r_ref[0])
        renewed = w_ref[0] * (1.0 - RATE_MAT * DECAY_MAT) - RATE_MAT * precond
        wo_ref[0] = renewed
        eo_ref[0] = EMA_DECAY * e_ref[0] + (1.0 - EMA_DECAY) * renewed

    own = pl.BlockSpec((1, rows, D), lambda j: (j, 0, 0))
    square = pl.BlockSpec((1, D, D), lambda j: (j, 0, 0))
    return call(
        kernel,
        (count,),
        [grad, full, right_full, left_root, left_stats, right_stats, weights, ema],
        [own, square, square] + [own] * 5,
        [sds((count, rows, D), F32)] * 4,
        [own] * 4,
        [],
        10 * rows * D * count * D,
        "shampoo",
    )


def split_vector(row_vec):
    ends = (D, D + HEAD_DIM, D + 2 * HEAD_DIM, D + 2 * HEAD_DIM + FF)
    ln_gain, q_gain, k_gain, mlp_bias, out_bias = jnp.split(row_vec, ends)
    return (
        ln_gain[None],
        jnp.tile(q_gain, HEADS)[None],
        jnp.tile(k_gain, HEADS)[None],
        mlp_bias[None],
        out_bias[None],
    )


def pad_tokens(array):
    return jnp.pad(array, ((0, 0), (0, PAD - SEQ), (0, 0))).reshape(-1, D)


def cut_tokens(array):
    return array.reshape(-1, PAD, D)[:, :SEQ]


def on_device(
    image_tokens,
    cotangent,
    weights,
    weights_ema,
    left_stats,
    right_stats,
    left_root,
    right_root,
    vectors,
    vec_first,
    vec_second,
):
    rounded = weights.astype(BF)
    block_rows = lax.all_gather(rounded, "head", axis=0, tiled=True)
    full_blocks = lax.all_gather(block_rows, "dp", axis=1, tiled=True)
    right_full = lax.all_gather(right_root.astype(BF), "dp", axis=1, tiled=True)

    def group(depth, first, count):
        return [([full_blocks], depth * PER_LAYER + first, count)]

    stream = pad_tokens(image_tokens)
    saved = []
    for depth in range(LAYERS):
        ln_gain, q_gain, k_gain, mlp_bias, out_bias = split_vector(vectors[depth])
        normed, hidden, slope = mlp_in(stream, ln_gain, mlp_bias, group(depth, 3, RATIO))
        queries, keys, values, q_unit, q_inv, k_unit, k_inv, attended = attend(
            normed, q_gain, k_gain, group(depth, 0, 3)
        )
        saved.append(
            (stream, normed, hidden, slope, queries, keys, values, q_unit, q_inv, k_unit, k_inv, attended)
        )
        stream = project(
            stream, attended, hidden, out_bias, group(depth, IN_COUNT, OUT_COUNT), depth == LAYERS - 1
        )
    block_out = cut_tokens(stream)
    grad = pad_tokens(cotangent)
    weight_parts = [None] * LAYERS
    vector_parts = [None] * LAYERS
    for depth in reversed(range(LAYERS)):
        ln_gain, q_gain, k_gain, _, _ = split_vector(vectors[depth])
        stream, normed, hidden, slope, queries, keys, values, q_unit, q_inv, k_unit, k_inv, attended = saved[depth]
        dy, do, du, dbo, dbu = mlp_back(grad, slope, group(depth, IN_COUNT, OUT_COUNT))
        dqkv, dgq, dgk = attend_back(
            do, queries, keys, values, q_unit, q_inv, k_unit, k_inv, q_gain, k_gain
        )
        weight_parts[depth] = [
            weight_grads(normed, dqkv, 3, "grad_qkv"),
            weight_grads(normed, du, RATIO, "grad_u"),
            weight_grads(attended, dy, 1, "grad_o"),
            weight_grads(hidden, dy, RATIO, "grad_a"),
        ]
        grad, dg = stream_back(
            grad, stream, ln_gain, du, dqkv, group(depth, 3, RATIO) + group(depth, 0, 3)
        )
        vector_parts[depth] = jnp.concatenate(
            [
                dg[0],
                dgq.reshape(HEADS, HEAD_DIM).sum(0),
                dgk.reshape(HEADS, HEAD_DIM).sum(0),
                dbu[0],
                dbo[0],
            ]
        )
    grad_stream = cut_tokens(grad)
    partial_grad = jnp.concatenate([part for parts in weight_parts for part in parts], axis=0)
    rows_part = lax.psum_scatter(partial_grad, "dp", scatter_dimension=1, tiled=True)
    own_grad = lax.psum_scatter(rows_part, "head", scatter_dimension=0, tiled=True)
    weight_grad = own_grad.astype(F32)
    grad_full = lax.all_gather(own_grad, "dp", axis=1, tiled=True)
    vector_grad = lax.psum(jnp.stack(vector_parts), ("dp", "head"))
    left_new, right_new, weight_new, ema_new = shampoo(
        weight_grad, grad_full, right_full, left_root, left_stats, right_stats, weights, weights_ema
    )
    first_new = BETA_ONE * vec_first + (1.0 - BETA_ONE) * vector_grad
    second_new = BETA_TWO * vec_second + (1.0 - BETA_TWO) * vector_grad * vector_grad
    first_hat = first_new / (1.0 - BETA_ONE**STEP)
    second_hat = second_new / (1.0 - BETA_TWO**STEP)
    vec_new = vectors - RATE_VEC * first_hat / (jnp.sqrt(second_hat) + ADAM_EPS)
    return (
        block_out,
        grad_stream,
        weight_grad,
        left_new,
        right_new,
        weight_new,
        ema_new,
        first_new,
        second_new,
        vec_new,
    )


def solution(mesh):
    tokens, blocks = P(("dp", "head"), None, None), P("head", "dp", None)
    return jax.shard_map(
        on_device,
        mesh=mesh,
        in_specs=(tokens, tokens) + (blocks,) * 6 + (P(),) * 3,
        out_specs=(tokens, tokens) + (blocks,) * 5 + (P(),) * 3,
        check_vma=False,
    )
```

time: 1660 us -> 827 us (0.50)
  waiting for transfers between devices: 802 us -> 473 us
  local copies, waits for them, and re-layouts: 340 us -> 34 us
  Pallas kernels: 0 us -> 251 us
  other arithmetic: 197 us -> 11 us
  matrix products: 179 us -> 0 us
  starting transfers between devices: 74.6 us -> 0.24 us
    pallas_call x0 -> x19, Pallas kernels: none -> 251 us  [call(): pl.pallas_call(kernel, grid=grid, in_specs=in_specs, out_specs=out_specs,...]
    all_to_all x16 -> x0, waiting for transfers between devices: 206 us -> none  [the longest x2 66.3 us: on_device(): lax.all_to_all(queries, 'head', split_axis=2, concat_axis=0, tiled=True)]
    dot_general x28 -> x0, matrix products: 179 us -> none  [the longest x2 24.3 us: on_device(): jnp.einsum('isbn,bkn->isk', grad_mixed, in_blocks, preferred_element_type...]
    reduce_scatter x1, waiting for transfers between devices: 319 us -> 173 us  [on_device(): lax.psum_scatter(partial_grad, 'dp', scatter_dimension=1, tiled=True)]
    reduce_sum x27 -> x4, other arithmetic: 82.4 us -> 0.09 us  [the longest x2 0.04 us: on_device(): dgq.reshape(HEADS, HEAD_DIM).sum(0)]
    all_to_all x16 -> x0, starting transfers between devices: 73.9 us -> none  [the longest x2 10.5 us: on_device(): lax.all_to_all(grad_att, 'head', split_axis=2, concat_axis=0, tiled=True)]
    convert_element_type x16 -> x3, other arithmetic: 75 us -> 4.97 us  [the longest x1 2.6 us: on_device(): rounded = weights.astype(BF)]
    convert_element_type x25 -> x0, local copies, waits for them, and re-layouts: 67.3 us -> none  [the longest x6 20 us: on_device(): grad_k_tok.astype(jnp.float32).reshape(image_count, SEQ, HEADS, HEAD_DIM)]
  transfers between devices with their start and end apart: 22 -> 6, of which waited for: 14 -> 5; matrix products, arithmetic and copies ran while one was open for 29% -> 2% of each run, Pallas kernels for 0% -> 3%
where the time goes in v1:
time: 827 us; the launch traced here: 825 us
  waiting for transfers between devices  473 us (57%)
  Pallas kernels  251 us (30%)
  blocking collectives  41.4 us (5%)
  local copies, waits for them, and re-layouts  34 us (4%)
  between operations  14.4 us (2%)
  other arithmetic  11 us (1%)
    pallas_call x19, Pallas kernels, call(): pl.pallas_call(kernel, grid=grid, in_specs=in_specs, out_specs=out_specs,...  251 us
    reduce_scatter x1, waiting for transfers between devices, on_device(): lax.psum_scatter(partial_grad, 'dp', scatter_dimension=1, tiled=True)  173 us
    all_gather x1, waiting for transfers between devices, on_device(): full_blocks = lax.all_gather(block_rows, 'dp', axis=1, tiled=True)  133 us
    all_gather x1, waiting for transfers between devices, on_device(): block_rows = lax.all_gather(rounded, 'head', axis=0, tiled=True)  73 us
    reduce_scatter x1, waiting for transfers between devices, on_device(): lax.psum_scatter(rows_part, 'head', scatter_dimension=0, tiled=True)  67.4 us
    psum x1, blocking collectives, on_device(): vector_grad = lax.psum(jnp.stack(vector_parts), ('dp', 'head'))  41.4 us
    all_gather x1, waiting for transfers between devices, on_device(): grad_full = lax.all_gather(own_grad, 'dp', axis=1, tiled=True)  26 us
    unnamed x55, local copies, waits for them, and re-layouts  17.3 us
  transfers between devices with their start and end apart: 6, of which 5 were waited for; matrix products, arithmetic and copies ran while one was open for 2% of the time, Pallas kernels for 3%

profile of v1, /device:TPU:0, one launch (start us, length us, event | category | flops | bytes accessed | tf_op | source)
XLA Modules:
  0.0 825.2 jit_solution(12405683134388956586)
XLA Ops:
  7.3 2.6 convert_element_type.12
  9.9 73.0 %all-gather.5.cloned.1.call-done = bf16[24,96,768]{2,1,0:T(8,128)(2,1)} async-done(((bf16[6,96,768]{2,1,0:T(8,128)(2,1)}), bf16[24,96,768]{2,1,0:T(8,128)(2,1)}) %all-gather.5.cloned.1.call-update) | async-done | bytes 3538960 | tf_op jit(solution)/shard_map/all_gather | solution.py:610
  89.0 133.0 %all-gather.7.cloned.1.call-done.refs_0_.refs_1_ = bf16[24,768,768]{2,1,0:T(8,128)(2,1)} async-done(((bf16[24,96,768]{2,1,0:T(8,128)(2,1)}), bf16[24,768,768]{2,1,0:T(8,128)(2,1)}) %all-gather.7.cloned.1.call-update) | async-done | bytes 28311568 | tf_op jit(solution)/shard_map/all_gather | solution.py:611
  222.1 18.7 %mlp_in.2 = (bf16[624,768]{1,0:T(8,128)(2,1)}, bf16[624,3072]{1,0:T(8,128)(2,1)}, bf16[624,3072]{1,0:T(8,128)(2,1)}) custom-call(bf16[624,768]{1,0:T(8,128)(2,1)} %bitcast.14, f32[1,768]{1,0:T(1,128)} %get-tuple-element.108.g_ref.c_ref, f32[1,3072]{1,0:T(1,128)} %get-tuple-element.114.b_ref, bf16[24,768,768]{2,1,0:T(8,128)(2,1)} %all-gather.7.cloned.1.call-done.refs_0_.refs_1_), custom_call_target="tpu_custom_call" | custom-call | flops 2944401408 | bytes 37911552 | tf_op jit(solution)/shard_map/mlp_in/pallas_call | solution.py:53
  240.8 16.5 %attend.2 = (bf16[624,768]{1,0:T(8,128)(2,1)}, bf16[624,768]{1,0:T(8,128)(2,1)}, bf16[624,768]{1,0:T(8,128)(2,1)}, bf16[624,768]{1,0:T(8,128)(2,1)}, f32[624,768...) custom-call(bf16[624,768]{1,0:T(8,128)(2,1)} %get-tuple-element.56.h_ref.l_ref, ...), custom_call_target="tpu_custom_call" | custom-call | flops 2607022080 | bytes 38860800 | tf_op jit(solution)/shard_map/attend/pallas_call | solution.py:53
  257.3 9.8 %project.2.x_ref = f32[624,768]{1,0:T(8,128)} custom-call(bf16[624,768]{1,0:T(8,128)(2,1)} %bitcast.15, bf16[624,768]{1,0:T(8,128)(2,1)} %get-tuple-element.57.o_ref, bf16[624,3072]{1,0:T(8,128)(2,1)} %get-tuple-element.58.a_ref.l_ref, f32[1,768]{1,0:T(1,128)} %get-tuple-element.107.b_ref, bf16[24,768,768]{2,1,0:T(8,128)(2,1)} %all-gather.7.cloned.1.call-done.refs_0_.refs_1_), custom_call_target="tpu_custom_call" | custom-call | flops 3680501760 | bytes 35982336 | tf_op jit(solution)/shard_map/project/pallas_call | solution.py:53
  267.0 19.0 %mlp_in.3 = (bf16[624,768]{1,0:T(8,128)(2,1)}, bf16[624,3072]{1,0:T(8,128)(2,1)}, bf16[624,3072]{1,0:T(8,128)(2,1)}) custom-call(f32[624,768]{1,0:T(8,128)} %project.2.x_ref, f32[1,768]{1,0:T(1,128)} %get-tuple-element.106.g_ref.c_ref, f32[1,3072]{1,0:T(1,128)} %get-tuple-element.113.b_ref, bf16[24,768,768]{2,1,0:T(8,128)(2,1)} %all-gather.7.cloned.1.call-done.refs_0_.refs_1_), custom_call_target="tpu_custom_call" | custom-call | flops 2944401408 | bytes 38870016 | tf_op jit(solution)/shard_map/mlp_in/pallas_call | solution.py:53
  286.0 10.8 %mlp_back.2 = (bf16[624,768]{1,0:T(8,128)(2,1)}, bf16[624,768]{1,0:T(8,128)(2,1)}, bf16[624,3072]{1,0:T(8,128)(2,1)}, f32[1,768]{1,0:T(1,128)}, f32[1,3072]{1,0:T(1,128)}) custom-call(bf16[624,768]{1,0:T(8,128)(2,1)} %bitcast.17, bf16[624,3072]{1,0:T(8,128)(2,1)} %get-tuple-element.62.s_ref, bf16[24,768,768]{2,1,0:T(8,128)(2,1)} %all-gather.7.cloned.1.call-done.refs_0_.refs_1_), custom_call_target="tpu_custom_call" | custom-call | flops 3680501760 | bytes 38870016 | tf_op jit(solution)/shard_map/mlp_back/pallas_call | solution.py:53
  296.8 16.6 %attend.3 = (bf16[624,768]{1,0:T(8,128)(2,1)}, bf16[624,768]{1,0:T(8,128)(2,1)}, bf16[624,768]{1,0:T(8,128)(2,1)}, bf16[624,768]{1,0:T(8,128)(2,1)}, f32[624,768...) custom-call(bf16[624,768]{1,0:T(8,128)(2,1)} %get-tuple-element.59.h_ref.l_ref, ...), custom_call_target="tpu_custom_call" | custom-call | flops 2607022080 | bytes 38860800 | tf_op jit(solution)/shard_map/attend/pallas_call | solution.py:53
  313.4 23.3 %attend_back.2 = (bf16[624,2304]{1,0:T(8,128)(2,1)}, f32[1,768]{1,0:T(1,128)}, f32[1,768]{1,0:T(1,128)}) custom-call(bf16[624,768]{1,0:T(8,128)(2,1)} %get-tuple-element.64.do_ref, bf16[624,768]{1,0:T(8,128)(2,1)} %get-tuple-element.65.q_ref, bf16[624,768]{1,0:T(8,128)(2,1)} %get-tuple-element.66.k_ref, bf16[624,768]{1,0:T(8,128)(2,1)} %get-tuple-element.67.v_ref, ...), custom_call_target="tpu_custom_call" | custom-call | flops 996802560 | bytes 12472320 | tf_op jit(solution)/shard_map/attend_back/pallas_call | solution.py:53
  336.8 6.4 grad_qkv.3
  343.2 7.6 grad_u.3
  350.8 17.0 %stream_back.2 = (f32[624,768]{1,0:T(8,128)}, f32[1,768]{1,0:T(1,128)}) custom-call(bf16[624,768]{1,0:T(8,128)(2,1)} %bitcast.18, f32[624,768]{1,0:T(8,128)} %project.2.x_ref, f32[1,768]{1,0:T(1,128)} %get-tuple-element.106.g_ref.c_ref, bf16[624,3072]{1,0:T(8,128)(2,1)} %get-tuple-element.63.du_ref.r_ref, bf16[624,2304]{1,0:T(8,128)(2,1)} %get-tuple-element.72.dz_ref.r_ref, ...), custom_call_target="tpu_custom_call" | custom-call | flops 5152702464 | bytes 68130816 | tf_op jit(solution)/shard_map/stream_back/pallas_call | solution.py:53
  367.8 11.4 %mlp_back.3 = (bf16[624,768]{1,0:T(8,128)(2,1)}, bf16[624,768]{1,0:T(8,128)(2,1)}, bf16[624,3072]{1,0:T(8,128)(2,1)}, f32[1,768]{1,0:T(1,128)}, f32[1,3072]{1,0:T(1,128)}) custom-call(f32[624,768]{1,0:T(8,128)} %get-tuple-element.73.g_ref, bf16[624,3072]{1,0:T(8,128)(2,1)} %get-tuple-element.74.s_ref, ...), custom_call_target="tpu_custom_call" | custom-call | flops 3680501760 | bytes 39828480 | tf_op jit(solution)/shard_map/mlp_back/pallas_call | solution.py:53
  379.3 23.0 %attend_back.3 = (bf16[624,2304]{1,0:T(8,128)(2,1)}, f32[1,768]{1,0:T(1,128)}, f32[1,768]{1,0:T(1,128)}) custom-call(bf16[624,768]{1,0:T(8,128)(2,1)} %get-tuple-element.76.do_ref, bf16[624,768]{1,0:T(8,128)(2,1)} %get-tuple-element.77.q_ref, bf16[624,768]{1,0:T(8,128)(2,1)} %get-tuple-element.78.k_ref, bf16[624,768]{1,0:T(8,128)(2,1)} %get-tuple-element.79.v_ref, ...), custom_call_target="tpu_custom_call" | custom-call | flops 996802560 | bytes 12472320 | tf_op jit(solution)/shard_map/attend_back/pallas_call | solution.py:53
  402.3 6.4 grad_qkv.2
  408.7 4.1 constant_dynamic-update-slice_fusion.5
  412.8 7.6 grad_u.2
  420.4 7.6 grad_a.2
  428.1 5.0 constant_dynamic-update-slice_fusion.4
  435.3 2.7 constant_dynamic-update-slice_fusion.3
  441.0 2.4 constant_dynamic-update-slice_fusion.1
  443.4 7.8 grad_a.3
  453.4 4.7 constant_dynamic-update-slice_fusion
  458.2 173.4 %reduce-scatter.3.cloned.1.call-done = bf16[24,96,768]{2,1,0:T(8,128)(2,1)} async-done(((bf16[24,768,768]{2,1,0:T(8,128)(2,1)}), bf16[24,96,768]{2,1,0:T(8,128)(2,1)}) %reduce-scatter.3.cloned.1.call-update) | async-done | bytes 3538960 | tf_op jit(solution)/shard_map/reduce_scatter | solution.py:662
  632.7 67.4 %reduce-scatter.5.cloned.1.call-done = bf16[6,96,768]{2,1,0:T(8,128)(2,1)} async-done(((bf16[24,96,768]{2,1,0:T(8,128)(2,1)}), bf16[6,96,768]{2,1,0:T(8,128)(2,1)}) %reduce-scatter.5.cloned.1.call-update) | async-done | bytes 884752 | tf_op jit(solution)/shard_map/reduce_scatter | solution.py:663
  700.2 9.7 %project.3 = bf16[624,768]{1,0:T(8,128)(2,1)} custom-call(f32[624,768]{1,0:T(8,128)} %project.2.x_ref, bf16[624,768]{1,0:T(8,128)(2,1)} %get-tuple-element.60.o_ref, bf16[624,3072]{1,0:T(8,128)(2,1)} %get-tuple-element.61.a_ref.l_ref, f32[1,768]{1,0:T(1,128)} %get-tuple-element.105.b_ref, bf16[24,768,768]{2,1,0:T(8,128)(2,1)} %all-gather.7.cloned.1.call-done.refs_0_.refs_1_), custom_call_target="tpu_custom_call" | custom-call | flops 3680501760 | bytes 35982336 | tf_op jit(solution)/shard_map/project/pallas_call | solution.py:53
  712.3 17.1 %stream_back.3 = (f32[624,768]{1,0:T(8,128)}, f32[1,768]{1,0:T(1,128)}) custom-call(f32[624,768]{1,0:T(8,128)} %get-tuple-element.73.g_ref, bf16[624,768]{1,0:T(8,128)(2,1)} %bitcast.16, f32[1,768]{1,0:T(1,128)} %get-tuple-element.108.g_ref.c_ref, bf16[624,3072]{1,0:T(8,128)(2,1)} %get-tuple-element.75.du_ref.r_ref, ...), custom_call_target="tpu_custom_call" | custom-call | flops 5152702464 | bytes 68130816 | tf_op jit(solution)/shard_map/stream_back/pallas_call | solution.py:53
  729.4 3.2 slice.33
  734.1 41.4 %psum.7 = f32[2,4736]{1,0:T(2,128)S(1)} all-reduce(f32[2,4736]{1,0:T(2,128)S(1)} %pad_maximum_fusion), channel_id=1, replica_groups=mesh['dp'=8,'head'=4] {'dp','head'}, use_global_device_ids=true, to_apply=%region_6.7 | all-reduce | flops 9472 | bytes 75776 | tf_op jit(solution)/shard_map/psum | solution.py:666
  777.6 26.0 %all-gather.9.cloned.1.call-done.f_ref = bf16[6,768,768]{2,1,0:T(8,128)(2,1)} async-done(((bf16[6,96,768]{2,1,0:T(8,128)(2,1)}), bf16[6,768,768]{2,1,0:T(8,128)(2,1)}) %all-gather.9.cloned.1.call-update) | async-done | bytes 7077904 | tf_op jit(solution)/shard_map/all_gather | solution.py:665
  803.6 14.7 %shampoo.1 = (f32[6,96,768]{2,1,0:T(8,128)}, f32[6,96,768]{2,1,0:T(8,128)}, f32[6,96,768]{2,1,0:T(8,128)}, f32[6,96,768]{2,1,0:T(8,128)}) custom-call(f32[6,96,768]{2,1,0:T(8,128)} %convert_element_type.13.g_ref, bf16[6,768,768]{2,1,0:T(8,128)(2,1)} %all-gather.9.cloned.1.call-done.f_ref, bf16[6,768,768]{2,1,0:T(8,128)(2,1)} %all-gather.11.cloned.1.call-done.r_ref, ...), custom_call_target="tpu_custom_call" | custom-call | flops 3397386240 | bytes 31850496 | tf_op jit(solution)/shard_map/shampoo/pallas_call | solution.py:53
  (105 shorter events, 20.6 us)
Async XLA Ops:
  7.2 75.8 %copy-start.10 = (f32[2,4736]{1,0:T(2,128)S(1)}, f32[2,4736]{1,0:T(2,128)}, u32[]{:S(2)}) copy-start(f32[2,4736]{1,0:T(2,128)} %param.19) | copy-start | bytes 113668
  7.2 78.6 %copy-start.8 = (bf16[3,196,768]{2,1,0:T(8,128)(2,1)S(1)}, bf16[3,196,768]{2,1,0:T(8,128)(2,1)}, u32[]{:S(2)}) copy-start(bf16[3,196,768]{2,1,0:T(8,128)(2,1)} %param.11) | copy-start | bytes 2709508
  7.2 79.6 %copy-start.9 = (bf16[3,196,768]{2,1,0:T(8,128)(2,1)S(1)}, bf16[3,196,768]{2,1,0:T(8,128)(2,1)}, u32[]{:S(2)}) copy-start(bf16[3,196,768]{2,1,0:T(8,128)(2,1)} %param.12) | copy-start | bytes 2709508
  7.2 75.7 %all-gather.5.cloned.1.call-start = ((), (), s32[]{:S(2)}) async-start(), calls=%async_computation.2 | async-start | bytes 4423680 | tf_op jit(solution)/shard_map/all_gather | solution.py:610
  9.9 212.2 %all-gather.7.cloned.1.call-start = ((), (), s32[]{:S(2)}) async-start(), calls=%async_computation.3 | async-start | bytes 31850496 | tf_op jit(solution)/shard_map/all_gather | solution.py:611
  82.9 548.6 %reduce-scatter.3.cloned.1.call-start = ((), (), s32[]{:S(2)}) async-start(), calls=%async_computation.4 | async-start | bytes 31850496 | tf_op jit(solution)/shard_map/reduce_scatter | solution.py:662
  428.1 5.0 copy-start.2
  428.1 5.0 copy-start.7
  428.1 7.2 copy-start
  433.1 7.9 slice-start
  435.3 3.7 copy-start.3
  435.3 5.7 slice-start.1
  443.4 7.8 copy-start.1
  443.4 7.8 copy-start.6
  458.1 173.5 %copy-start.5 = (f32[6,96,768]{2,1,0:T(8,128)S(1)}, f32[6,96,768]{2,1,0:T(8,128)}, u32[]{:S(2)}) copy-start(f32[6,96,768]{2,1,0:T(8,128)} %param.18) | copy-start | bytes 5308420
  458.2 242.0 %reduce-scatter.5.cloned.1.call-start = ((), (), s32[]{:S(2)}) async-start(), calls=%async_computation.5 | async-start | bytes 4423680 | tf_op jit(solution)/shard_map/reduce_scatter | solution.py:663
  631.6 146.0 %all-gather.11.cloned.1.call-start = ((), (), s32[]{:S(2)}) async-start(), calls=%async_computation.7 | async-start | bytes 7962624 | tf_op jit(solution)/shard_map/all_gather | solution.py:612
  632.7 170.9 %all-gather.9.cloned.1.call-start = ((), (), s32[]{:S(2)}) async-start(), calls=%async_computation.6 | async-start | bytes 7962624 | tf_op jit(solution)/shard_map/all_gather | solution.py:665
  712.1 20.4 %copy-start.22 = (f32[1,768]{1,0:T(1,128)S(1)}, f32[1,768]{1,0:T(1,128)}, u32[]{:S(2)}) copy-start(f32[1,768]{1,0:T(1,128)} %get-tuple-element.97) | copy-start | bytes 9220
  712.2 20.4 %copy-start.19 = (f32[1,768]{1,0:T(1,128)S(1)}, f32[1,768]{1,0:T(1,128)}, u32[]{:S(2)}) copy-start(f32[1,768]{1,0:T(1,128)} %get-tuple-element.98) | copy-start | bytes 9220
  712.2 20.5 %copy-start.18 = (f32[1,768]{1,0:T(1,128)S(1)}, f32[1,768]{1,0:T(1,128)}, u32[]{:S(2)}) copy-start(f32[1,768]{1,0:T(1,128)} %get-tuple-element.99) | copy-start | bytes 9220
  712.2 20.7 %copy-start.16 = (f32[1,768]{1,0:T(1,128)S(1)}, f32[1,768]{1,0:T(1,128)}, u32[]{:S(2)}) copy-start(f32[1,768]{1,0:T(1,128)} %get-tuple-element.101) | copy-start | bytes 9220
  712.2 20.7 %copy-start.14 = (f32[1,3072]{1,0:T(1,128)S(1)}, f32[1,3072]{1,0:T(1,128)}, u32[]{:S(2)}) copy-start(f32[1,3072]{1,0:T(1,128)} %get-tuple-element.100) | copy-start | bytes 36868
  712.2 21.5 %copy-start.21 = (f32[1,768]{1,0:T(1,128)S(1)}, f32[1,768]{1,0:T(1,128)}, u32[]{:S(2)}) copy-start(f32[1,768]{1,0:T(1,128)} %get-tuple-element.93) | copy-start | bytes 9220
  712.2 21.6 %copy-start.20 = (f32[1,768]{1,0:T(1,128)S(1)}, f32[1,768]{1,0:T(1,128)}, u32[]{:S(2)}) copy-start(f32[1,768]{1,0:T(1,128)} %get-tuple-element.94) | copy-start | bytes 9220
  712.2 21.7 %copy-start.17 = (f32[1,768]{1,0:T(1,128)S(1)}, f32[1,768]{1,0:T(1,128)}, u32[]{:S(2)}) copy-start(f32[1,768]{1,0:T(1,128)} %get-tuple-element.96) | copy-start | bytes 9220
  712.2 21.7 %copy-start.15 = (f32[1,3072]{1,0:T(1,128)S(1)}, f32[1,3072]{1,0:T(1,128)}, u32[]{:S(2)}) copy-start(f32[1,3072]{1,0:T(1,128)} %get-tuple-element.95) | copy-start | bytes 36868
  712.2 63.3 %copy-start.11 = (f32[2,4736]{1,0:T(2,128)S(1)}, f32[2,4736]{1,0:T(2,128)}, u32[]{:S(2)}) copy-start(f32[2,4736]{1,0:T(2,128)} %param.19) | copy-start | bytes 113668
  712.2 63.2 %copy-start.12 = (f32[2,4736]{1,0:T(2,128)S(1)}, f32[2,4736]{1,0:T(2,128)}, u32[]{:S(2)}) copy-start(f32[2,4736]{1,0:T(2,128)} %param.21) | copy-start | bytes 113668
  712.2 63.2 %copy-start.13 = (f32[2,4736]{1,0:T(2,128)S(1)}, f32[2,4736]{1,0:T(2,128)}, u32[]{:S(2)}) copy-start(f32[2,4736]{1,0:T(2,128)} %param.20) | copy-start | bytes 113668
  729.4 46.9 %copy-start.4 = (bf16[6,96,768]{2,1,0:T(8,128)(2,1)S(1)}, bf16[6,96,768]{2,1,0:T(8,128)(2,1)}, u32[]{:S(2)}) copy-start(bf16[6,96,768]{2,1,0:T(8,128)(2,1)} %reduce-scatter.5.cloned.1.call-done) | copy-start | bytes 2654212
Sparse Core Ops, SparseCore 0:
  10.2 72.6 all-gather.4
  84.8 137.2 all-gather.6
  458.3 173.2 reduce-scatter.2
  633.7 66.3 reduce-scatter.4
  702.5 49.7 all-gather.10
  754.0 49.5 all-gather.8

commit v2 on v1

--- a/solution.py
+++ b/solution.py
@@ -46,7 +46,7 @@
     return lax.dot_general(a, b, dims, preferred_element_type=F32)
 
 
-def call(kernel, grid, operands, in_specs, outs, out_specs, scratch, flops, name):
+def call(kernel, grid, operands, in_specs, outs, out_specs, scratch, flops, name, aliases=None):
     moved = sum(o.size * o.dtype.itemsize for o in operands) + sum(
         math.prod(o.shape) * o.dtype.itemsize for o in outs
     )
@@ -59,6 +59,7 @@
         scratch_shapes=scratch,
         compiler_params=pltpu.CompilerParams(vmem_limit_bytes=56 * 1024 * 1024),
         cost_estimate=pl.CostEstimate(flops=flops, bytes_accessed=moved, transcendentals=0),
+        input_output_aliases=aliases or {},
         name=name,
     )(*operands)
 
@@ -71,61 +72,70 @@
     return jax.ShapeDtypeStruct(shape, dtype)
 
 
-def block_total(units):
-    return sum(count for _, _, count in units)
-
-
-def piece_operands(units):
-    arrays, specs, start = [], [], 0
-    for pieces, first, count in units:
-        for piece in pieces:
-            arrays.append(piece)
-            specs.append(
-                pl.BlockSpec(
-                    (1,) + piece.shape[1:],
-                    functools.partial(
-                        lambda at, first, count, j: (first + jnp.clip(j - at, 0, count - 1), 0, 0),
-                        start,
-                        first,
-                        count,
-                    ),
-                )
-            )
-        start += count
-    return arrays, specs
-
-
-def read_block(j, units, refs, held, offsets):
-    if len(units) == 1 and len(units[0][0]) == 1:
-        return refs[0][0]
-    start, at = 0, 0
-    for pieces, _, count in units:
-        mine = refs[at : at + len(pieces)]
-
-        @pl.when((j >= start) & (j < start + count))
-        def _(mine=mine):
-            rows_at = offsets(len(mine))
-            for ref, row in zip(mine, rows_at):
-                rows = ref.shape[1]
-                held[pl.ds(pl.multiple_of(row, 16), rows), :] = ref[0]
-
-        start += count
-        at += len(pieces)
-    return held[...]
-
-
-def piece_rows(count):
-    if count == 1:
-        return [0]
+CHIPS = ((0, 0), (0, 1), (1, 0), (1, 1))
+
+
+class Blocks:
+    def __init__(self, steps):
+        self.steps = steps
+        self.arrays = []
+        for places in steps:
+            for _, pieces in places:
+                for array, _ in pieces:
+                    if not any(array is other for other in self.arrays):
+                        self.arrays.append(array)
+        self.count = len(steps[0][0][1])
+        self.specs = [pl.BlockSpec(memory_space=pl.ANY)] * len(self.arrays)
+        self.scratch = [pltpu.VMEM((2, D, D), BF), pltpu.SemaphoreType.DMA((2, self.count))]
+
+    def bind(self, refs, held, sems):
+        self.refs, self.held, self.sems = refs, held, sems
+
+    def copies(self, pieces, slot):
+        made = []
+        for at, (array, block) in enumerate(pieces):
+            ref = next(ref for ref, other in zip(self.refs, self.arrays) if other is array)
+            target = self.held.at[slot]
+            if self.count > 1:
+                rows = array.shape[-2]
+                row = piece_row(*CHIPS[at % 4], at // 4, rows)
+                target = self.held.at[slot, pl.ds(pl.multiple_of(row, 16), rows)]
+            made.append(pltpu.make_async_copy(ref.at[block], target, self.sems.at[slot, at]))
+        return made
+
+    def start(self, j, wanted):
+        head = lax.axis_index("head")
+        for step, places in enumerate(self.steps):
+            for owners, pieces in places:
+                here = wanted == step
+                if owners is not None:
+                    here = here & functools.reduce(lambda a, b: a | b, [head == owner for owner in owners])
+
+                @pl.when(here)
+                def _(step=step, pieces=pieces):
+                    for copy in self.copies(pieces, step % 2):
+                        copy.start()
+
+    def step(self, j):
+        @pl.when(j == 0)
+        def _():
+            self.start(j, j)
+
+        @pl.when(j + 1 < len(self.steps))
+        def _():
+            self.start(j, j + 1)
+
+        slot = lax.rem(j, 2)
+        for copy in self.copies(self.steps[0][0][1], slot):
+            copy.wait()
+        return self.held[slot]
+
+
+def piece_row(dy, dx, dc, rows):
     me = lax.axis_index("dp")
-    rows = D // count
     core, x, y = lax.rem(me, 2), lax.rem(me // 2, 2), me // 4
-    return [
-        ((y + dy - 2 * y * dy) * 4 + (x + dx - 2 * x * dx) * 2 + (core + dc - 2 * core * dc)) * rows
-        for dy in (0, 1)
-        for dx in (0, 1)
-        for dc in (0, 1)
-    ]
+    y, x, core = (1 - v if d else v for v, d in ((y, dy), (x, dx), (core, dc)))
+    return (y * 4 + x * 2 + core) * rows
 
 
 def row_parts(values):
@@ -173,23 +183,14 @@
     lax.fori_loop(0, total // size, step, 0)
 
 
-def mlp_in(stream, gain, bias, units):
-    tokens = stream.shape[0]
-    weights, w_specs = piece_operands(units)
-
-    def kernel(x_ref, g_ref, b_ref, *refs):
-        w_refs, (h_ref, a_ref, s_ref, held, wide) = refs[: len(weights)], refs[len(weights) :]
+def mlp_in(normed, bias, blocks):
+    tokens = normed.shape[0]
+
+    def kernel(h_ref, b_ref, *refs):
+        w_refs, (a_ref, s_ref, wide, *fetch) = refs[: len(blocks.arrays)], refs[len(blocks.arrays) :]
+        blocks.bind(w_refs, *fetch)
         j = pl.program_id(0)
-
-        @pl.when(j == 0)
-        def _():
-            def body(rows):
-                unit, _ = row_parts(x_ref[rows, :].astype(F32))
-                h_ref[rows, :] = (unit * g_ref[...]).astype(BF)
-
-            row_steps(tokens, 48, body)
-
-        wide[...] = dot(h_ref[...], read_block(j, units, w_refs, held, piece_rows))
+        wide[...] = dot(h_ref[...], blocks.step(j))
 
         def body(rows):
             act, slope = gelu_parts(wide[rows, :] + b_ref[...])
@@ -201,11 +202,11 @@
     return call(
         kernel,
         (RATIO,),
-        [stream, gain, bias] + weights,
-        [whole((tokens, D)), whole((1, D)), pl.BlockSpec((1, D), lambda j: (0, j))] + w_specs,
-        [sds((tokens, D), BF), sds((tokens, FF), BF), sds((tokens, FF), BF)],
-        [whole((tokens, D))] + [pl.BlockSpec((tokens, D), lambda j: (0, j))] * 2,
-        [pltpu.VMEM((D, D), BF), pltpu.VMEM((tokens, D), F32)],
+        [normed, bias] + blocks.arrays,
+        [whole((tokens, D)), pl.BlockSpec((1, D), lambda j: (0, j))] + blocks.specs,
+        [sds((tokens, FF), BF), sds((tokens, FF), BF)],
+        [pl.BlockSpec((tokens, D), lambda j: (0, j))] * 2,
+        [pltpu.VMEM((tokens, D), F32)] + blocks.scratch,
         2 * tokens * D * FF,
         "mlp_in",
     )
@@ -221,16 +222,25 @@
     return jnp.where(low, values, zero), jnp.where(low, zero, values)
 
 
-def attend(normed, q_gain, k_gain, units):
-    tokens = normed.shape[0]
+def attend(stream, ln_gain, q_gain, k_gain, blocks):
+    tokens = stream.shape[0]
     images = tokens // PAD
-    weights, w_specs = piece_operands(units)
-
-    def kernel(h_ref, gq_ref, gk_ref, *refs):
-        w_refs = refs[: len(weights)]
-        q_ref, k_ref, v_ref, qu_ref, qi_ref, ku_ref, ki_ref, o_ref, held, wide = refs[len(weights) :]
+
+    def kernel(x_ref, g_ref, gq_ref, gk_ref, *refs):
+        w_refs, refs = refs[: len(blocks.arrays)], refs[len(blocks.arrays) :]
+        h_ref, q_ref, k_ref, v_ref, qu_ref, qi_ref, ku_ref, ki_ref, o_ref, wide, *fetch = refs
+        blocks.bind(w_refs, *fetch)
         j = pl.program_id(0)
-        wide[...] = dot(h_ref[...], read_block(j, units, w_refs, held, piece_rows))
+
+        @pl.when(j == 0)
+        def _():
+            def body(rows):
+                unit, _ = row_parts(x_ref[rows, :].astype(F32))
+                h_ref[rows, :] = (unit * g_ref[...]).astype(BF)
+
+            row_steps(tokens, 48, body)
+
+        wide[...] = dot(h_ref[...], blocks.step(j))
 
         def normalise(g_ref, n_ref, u_ref, i_ref):
             mixer = head_mixer()
@@ -281,24 +291,24 @@
     return call(
         kernel,
         (3,),
-        [normed, q_gain, k_gain] + weights,
-        [whole((tokens, D)), whole((1, D)), whole((1, D))] + w_specs,
-        [flat, flat, flat, flat, flat32, flat, flat32, flat],
-        [whole((tokens, D))] * 8,
-        [pltpu.VMEM((D, D), BF), pltpu.VMEM((tokens, D), F32)],
+        [stream, ln_gain, q_gain, k_gain] + blocks.arrays,
+        [whole((tokens, D))] + [whole((1, D))] * 3 + blocks.specs,
+        [flat, flat, flat, flat, flat, flat32, flat, flat32, flat],
+        [whole((tokens, D))] * 9,
+        [pltpu.VMEM((tokens, D), F32)] + blocks.scratch,
         2 * tokens * D * 3 * D + 4 * tokens * PAD * D,
         "attend",
     )
 
 
-def project(stream, attended, hidden, bias, units, last):
+def project(stream, attended, hidden, bias, blocks, last):
     tokens = stream.shape[0]
-    weights, w_specs = piece_operands(units)
 
     def kernel(x_ref, o_ref, a_ref, b_ref, *refs):
-        w_refs, (y_ref, total, held) = refs[: len(weights)], refs[len(weights) :]
+        w_refs, (y_ref, total, *fetch) = refs[: len(blocks.arrays)], refs[len(blocks.arrays) :]
+        blocks.bind(w_refs, *fetch)
         j = pl.program_id(0)
-        block = read_block(j, units, w_refs, held, piece_rows)
+        block = blocks.step(j)
 
         @pl.when(j == 0)
         def _():
@@ -315,29 +325,29 @@
     return call(
         kernel,
         (OUT_COUNT,),
-        [stream, attended, hidden, bias] + weights,
+        [stream, attended, hidden, bias] + blocks.arrays,
         [
             whole((tokens, D)),
             whole((tokens, D)),
             pl.BlockSpec((tokens, D), lambda j: (0, jnp.maximum(j - 1, 0))),
             whole((1, D)),
         ]
-        + w_specs,
+        + blocks.specs,
         [sds((tokens, D), BF if last else F32)],
         [whole((tokens, D))],
-        [pltpu.VMEM((tokens, D), F32), pltpu.VMEM((D, D), BF)],
+        [pltpu.VMEM((tokens, D), F32)] + blocks.scratch,
         2 * tokens * D * OUT_COUNT * D,
         "project",
     )[0]
 
 
-def mlp_back(grad, slope, units):
+def mlp_back(grad, slope, blocks):
     tokens = grad.shape[0]
-    weights, w_specs = piece_operands(units)
 
     def kernel(g_ref, s_ref, *refs):
-        w_refs = refs[: len(weights)]
-        dy_ref, do_ref, du_ref, dbo_ref, dbu_ref, held = refs[len(weights) :]
+        w_refs, refs = refs[: len(blocks.arrays)], refs[len(blocks.arrays) :]
+        dy_ref, do_ref, du_ref, dbo_ref, dbu_ref, *fetch = refs
+        blocks.bind(w_refs, *fetch)
         j = pl.program_id(0)
 
         @pl.when(j == 0)
@@ -346,7 +356,7 @@
             dy_ref[...] = dy
             dbo_ref[...] = jnp.sum(dy.astype(F32), axis=0, keepdims=True)
 
-        wide = dot(dy_ref[...], read_block(j, units, w_refs, held, piece_rows), NT)
+        wide = dot(dy_ref[...], blocks.step(j), NT)
 
         @pl.when(j == 0)
         def _():
@@ -362,8 +372,8 @@
     return call(
         kernel,
         (OUT_COUNT,),
-        [grad, slope] + weights,
-        [whole((tokens, D)), shifted] + w_specs,
+        [grad, slope] + blocks.arrays,
+        [whole((tokens, D)), shifted] + blocks.specs,
         [
             sds((tokens, D), BF),
             sds((tokens, D), BF),
@@ -378,7 +388,7 @@
             whole((1, D)),
             pl.BlockSpec((1, D), lambda j: (0, jnp.maximum(j - 1, 0))),
         ],
-        [pltpu.VMEM((D, D), BF)],
+        blocks.scratch,
         2 * tokens * D * OUT_COUNT * D,
         "mlp_back",
     )
@@ -457,37 +467,76 @@
     )
 
 
-def weight_grads(left, right, count, name):
-    tokens = left.shape[0]
-
-    def kernel(l_ref, r_ref, out_ref):
-        out_ref[0] = dot(l_ref[...], r_ref[...], TN).astype(BF)
-
-    def spec(array):
-        wide = array.shape[1] > D
-        return pl.BlockSpec((tokens, D), (lambda j: (0, j)) if wide else (lambda j: (0, 0)))
-
+def weight_grads(segments, cut, name):
+    tokens = segments[0][0].shape[0]
+    total = sum(count for _, _, count in segments)
+    operands, specs, start = [], [], 0
+    for left, right, count in segments:
+        for side in (left, right):
+            index = functools.partial(
+                lambda at, last, j: (0, jnp.clip(j - at, 0, last)), start, side.shape[1] // D - 1
+            )
+            operands.append(side)
+            specs.append(pl.BlockSpec((tokens, D), index))
+        start += count
+
+    def kernel(*refs):
+        ins, outs = refs[: len(operands)], refs[len(operands) :]
+        j = pl.program_id(0)
+        start = 0
+        for at, (_, _, count) in enumerate(segments):
+
+            def body(at=at):
+                value = dot(ins[2 * at][...], ins[2 * at + 1][...], TN)
+                if cut:
+                    outs[-1][...] = value
+                else:
+                    outs[0][0] = value.astype(BF)
+
+            if count == total:
+                body()
+            else:
+                pl.when((j >= start) & (j < start + count))(body)
+            start += count
+        if cut:
+            held, rows = outs[-1], D // 8
+            for chip, (dy, dx) in enumerate(CHIPS):
+                for core in (0, 1):
+                    row = pl.multiple_of(piece_row(dy, dx, core, rows), 16)
+                    part = held[pl.ds(row, rows), :].astype(BF)
+                    if core == 0:
+                        outs[chip][0] = part
+                    else:
+                        outs[4][chip, 0] = part
+
+    if cut:
+        shapes = [sds((total, D // 8, D), BF)] * 4 + [sds((4, total, D // 8, D), BF)]
+        out_specs = [pl.BlockSpec((1, D // 8, D), lambda j: (j, 0, 0))] * 4
+        out_specs += [pl.BlockSpec((4, 1, D // 8, D), lambda j: (0, j, 0, 0))]
+    else:
+        shapes = [sds((total, D, D), BF)]
+        out_specs = [pl.BlockSpec((1, D, D), lambda j: (j, 0, 0))]
     return call(
         kernel,
-        (count,),
-        [left, right],
-        [spec(left), spec(right)],
-        [sds((count, D, D), BF)],
-        [pl.BlockSpec((1, D, D), lambda j: (j, 0, 0))],
-        [],
-        2 * tokens * D * count * D,
+        (total,),
+        operands,
+        specs,
+        shapes,
+        out_specs,
+        [pltpu.VMEM((D, D), F32)] if cut else [],
+        2 * tokens * D * total * D,
         name,
-    )[0]
-
-
-def stream_back(grad, stream, gain, grad_u, grad_qkv, units):
+    )
+
+
+def stream_back(grad, stream, gain, grad_u, grad_qkv, blocks):
     tokens = grad.shape[0]
-    weights, w_specs = piece_operands(units)
 
     def kernel(g_ref, x_ref, c_ref, du_ref, dz_ref, *refs):
-        w_refs, (out_ref, dg_ref, total, held) = refs[: len(weights)], refs[len(weights) :]
+        w_refs, (out_ref, dg_ref, total, *fetch) = refs[: len(blocks.arrays)], refs[len(blocks.arrays) :]
+        blocks.bind(w_refs, *fetch)
         j = pl.program_id(0)
-        block = read_block(j, units, w_refs, held, piece_rows)
+        block = blocks.step(j)
 
         @pl.when(j == 0)
         def _():
@@ -521,7 +570,7 @@
     return call(
         kernel,
         (IN_COUNT,),
-        [grad, stream, gain, grad_u, grad_qkv] + weights,
+        [grad, stream, gain, grad_u, grad_qkv] + blocks.arrays,
         [
             whole((tokens, D)),
             whole((tokens, D)),
@@ -529,21 +578,29 @@
             pl.BlockSpec((tokens, D), lambda j: (0, jnp.minimum(j, RATIO - 1))),
             pl.BlockSpec((tokens, D), lambda j: (0, jnp.maximum(j - RATIO, 0))),
         ]
-        + w_specs,
+        + blocks.specs,
         [sds((tokens, D), F32), sds((1, D), F32)],
         [whole((tokens, D)), whole((1, D))],
-        [pltpu.VMEM((tokens, D), F32), pltpu.VMEM((D, D), BF)],
+        [pltpu.VMEM((tokens, D), F32)] + blocks.scratch,
         2 * tokens * D * IN_COUNT * D,
         "stream_back",
     )
 
 
-def shampoo(grad, full, right_full, left_root, left_stats, right_stats, weights, ema):
+def shampoo(grad, full, right, left_root, left_stats, right_stats, weights, ema, first, earlier):
     count, rows, _ = grad.shape
 
-    def kernel(g_ref, f_ref, r_ref, lr_ref, ls_ref, rs_ref, w_ref, e_ref, lo_ref, ro_ref, wo_ref, eo_ref):
+    def kernel(g_ref, lr_ref, ls_ref, rs_ref, w_ref, e_ref, *refs):
+        f_refs, refs = refs[: len(full.arrays)], refs[len(full.arrays) :]
+        r_refs, refs = refs[: len(right.arrays)], refs[len(right.arrays) + len(earlier) :]
+        go_ref, lo_ref, ro_ref, wo_ref, eo_ref, f_held, f_sems, r_held, r_sems = refs
+        full.bind(f_refs, f_held, f_sems)
+        right.bind(r_refs, r_held, r_sems)
+        j = pl.program_id(0)
         at = lax.axis_index("dp") * rows
-        block = f_ref[0]
+        block = full.step(j)
+        right_block = right.step(j)
+        go_ref[0] = g_ref[0]
         gram = dot(g_ref[0].astype(BF), block, NT)
         lo_ref[0] = STAT_DECAY * ls_ref[0] + (1.0 - STAT_DECAY) * gram
         pick = (
@@ -553,23 +610,25 @@
         columns = dot(jnp.where(pick, 1.0, 0.0).astype(BF), block, NT).astype(BF)
         ro_ref[0] = STAT_DECAY * rs_ref[0] + (1.0 - STAT_DECAY) * dot(columns, block)
         lifted = dot(lr_ref[0].astype(BF), block).astype(BF)
-        precond = dot(lifted, r_ref[0])
+        precond = dot(lifted, right_block)
         renewed = w_ref[0] * (1.0 - RATE_MAT * DECAY_MAT) - RATE_MAT * precond
         wo_ref[0] = renewed
         eo_ref[0] = EMA_DECAY * e_ref[0] + (1.0 - EMA_DECAY) * renewed
 
-    own = pl.BlockSpec((1, rows, D), lambda j: (j, 0, 0))
-    square = pl.BlockSpec((1, D, D), lambda j: (j, 0, 0))
+    part = pl.BlockSpec((1, rows, D), lambda j: (j, 0, 0))
+    own = pl.BlockSpec((1, rows, D), lambda j: (first + j, 0, 0))
+    inputs = [grad, left_root, left_stats, right_stats, weights, ema] + full.arrays + right.arrays
     return call(
         kernel,
         (count,),
-        [grad, full, right_full, left_root, left_stats, right_stats, weights, ema],
-        [own, square, square] + [own] * 5,
-        [sds((count, rows, D), F32)] * 4,
-        [own] * 4,
-        [],
+        inputs + list(earlier),
+        [part] + [own] * 5 + full.specs + right.specs + [pl.BlockSpec(memory_space=pl.ANY)] * len(earlier),
+        [sds(weights.shape, F32)] * 5,
+        [own] * 5,
+        full.scratch + right.scratch,
         10 * rows * D * count * D,
         "shampoo",
+        {len(inputs) + at: at for at in range(len(earlier))},
     )
 
 
@@ -591,6 +650,272 @@
 
 def cut_tokens(array):
     return array.reshape(-1, PAD, D)[:, :SEQ]
+
+
+QKV, MLP, OUT = 0, 3, IN_COUNT
+SIZES = {QKV: 3, MLP: RATIO, OUT: OUT_COUNT}
+
+
+class Collectives:
+    cut = False
+
+    def __init__(self, weights, right_root):
+        rows = lax.all_gather(weights.astype(BF), "head", axis=0, tiled=True)
+        self.blocks = lax.all_gather(rows, "dp", axis=1, tiled=True)
+        self.right = lax.all_gather(right_root.astype(BF), "dp", axis=1, tiled=True)
+        self.count = weights.shape[0]
+        self.parts = {}
+
+    def group(self, *runs):
+        return Blocks(
+            [
+                [(None, [(self.blocks, depth * PER_LAYER + first + at)])]
+                for depth, first, count in runs
+                for at in range(count)
+            ]
+        )
+
+    def next(self, array):
+        return array
+
+    def done(self, name, array):
+        pass
+
+    def add_grads(self, depth, first, pieces):
+        self.parts[depth, first] = pieces[0]
+
+    def finish(self, renew):
+        partial = jnp.concatenate([self.parts[key] for key in sorted(self.parts)], axis=0)
+        rows = lax.psum_scatter(partial, "dp", scatter_dimension=1, tiled=True)
+        own = lax.psum_scatter(rows, "head", scatter_dimension=0, tiled=True)
+        full = lax.all_gather(own, "dp", axis=1, tiled=True)
+        full, right = (
+            Blocks([[(None, [(array, at)])] for at in range(self.count)]) for array in (full, self.right)
+        )
+        return renew(own.astype(F32), full, right, 0, ())
+
+    def vector_sum(self, vectors):
+        return lax.psum(vectors, ("dp", "head"))
+
+
+DP, LINE = 8, 4
+HALF = 3
+STEPS = {"core": 1, "x": 2, "y": 4}
+ROUNDS = ((2, 0, 0, 0), (1, 2, 1, 1), (3, 3, 3, 2))
+
+
+def swap(array, axis):
+    return lax.ppermute(array, "dp", [(i, i ^ STEPS[axis]) for i in range(DP)])
+
+
+def hop(array, *pairs):
+    return lax.ppermute(array, "head", pairs)
+
+
+def after(array, *earlier):
+    return lax.optimization_barrier((array,) + earlier)[0] if earlier else array
+
+
+class PlaneGather:
+    def __init__(self, own, half):
+        self.own, self.half = own, half
+
+    def first(self, *earlier):
+        own = self.own = after(self.own, *earlier)
+        self.x, self.y = swap(own, "x"), swap(own, "y")
+        return [own]
+
+    def second(self, *earlier):
+        x, y = after(self.x[: self.half], *earlier), after(self.y[self.half :], *earlier)
+        self.far = [swap(x, "y"), swap(y, "x")]
+        return [x, y]
+
+    def cores(self, *earlier):
+        self.chips = [after(chip, *earlier) for chip in [self.own, self.x, self.y] + self.far]
+        self.others = [swap(chip, "core") for chip in self.chips]
+        return self.chips
+
+    def pieces(self, at):
+        made = []
+        for chips in (self.chips, self.others):
+            made += [(chip, at) for chip in chips[:3]]
+            made.append((chips[3], at) if at < self.half else (chips[4], at - self.half))
+        return made
+
+
+class Permutes:
+    cut = True
+
+    def __init__(self, weights, right_root):
+        self.parts = {}
+        self.last, self.pins, self.chains = (), [], []
+        self.right_root = right_root.astype(BF)
+        own = weights.astype(BF)
+        head = lax.axis_index("head")
+        plan = self.plan = [PlaneGather(own[:HALF], 1), PlaneGather(own[HALF:], 2)]
+        halves = [lax.all_gather(part.own, "head") for part in plan]
+        for at in (0, 1, 2):
+            owner = functools.reduce(
+                lambda value, z: jnp.where(head == z, ROUNDS[at][z], value), range(1, LINE), ROUNDS[at][0]
+            )
+            for side in (0, 1):
+                plan.append(
+                    PlaneGather(lax.dynamic_index_in_dim(halves[side], owner, 0, keepdims=False), 1 + side)
+                )
+        plan[0].first()
+        plan[1].first()
+        plan[0].second()
+        plan[1].second()
+        plan[2].first(*plan[1].far)
+        plan[0].cores(*plan[1].far)
+        plan[1].cores(*plan[1].far)
+        plan[4].first(plan[2].x)
+        plan[2].second()
+        plan[2].cores()
+        self.pins += plan[4].second(*plan[2].far)
+
+    def done(self, name, array):
+        plan = self.plan
+        self.last, self.pins = (array,), []
+        if name == "attend0":
+            plan[4].cores(array)
+            plan[3].first(array)
+            plan[5].first(array)
+            plan[3].second(array)
+            plan[3].cores(array)
+            self.pins += plan[5].second(*plan[3].far)
+            self.pins += plan[6].first(*plan[3].far)
+        if name == "mlp0":
+            plan[5].cores(array)
+            self.pins += plan[6].second(array)
+            self.pins += plan[7].first(array)
+        if name == "project0":
+            plan[6].cores(array)
+            self.pins += plan[7].second(array)
+        if name == "attend1":
+            plan[7].cores(array)
+        if name == "project1":
+            self.right = lax.all_gather(after(self.right_root, array), "dp", axis=1, tiled=True)
+        self.chains = [chain for chain in self.chains if next(chain, None)]
+
+    def next(self, array):
+        return after(array, *self.last, *self.pins)
+
+    def tied(self, array):
+        return after(array, *self.last)
+
+    def send(self, array, axis):
+        self.pins.append(array)
+        return swap(array, axis)
+
+    def place(self, owner, side, head):
+        if head == owner:
+            return side
+        return next(2 + 2 * at + side for at in (0, 1, 2) if ROUNDS[at][head] == owner)
+
+    def group(self, *runs):
+        steps = []
+        for depth, first, count in runs:
+            for block in range(first, first + count):
+                owner, at = 2 * depth + block // (2 * HALF), block % (2 * HALF)
+                side, at = at // HALF, at % HALF
+                places = [self.place(owner, side, head) for head in range(LINE)]
+                steps.append(
+                    [
+                        (
+                            [head for head in range(LINE) if places[head] == place],
+                            self.plan[place].pieces(at),
+                        )
+                        for place in sorted(set(places))
+                    ]
+                )
+        return Blocks(steps)
+
+    def add_grads(self, depth, first, pieces):
+        chain = self.reduce(depth, first, pieces[:4], pieces[4])
+        next(chain)
+        self.chains.append(chain)
+
+    def reduce(self, depth, first, mine, theirs):
+        count = mine[0].shape[0]
+        half = count // 2
+        core = self.send(theirs, "core")
+        yield True
+        far = (self.tied(mine[3]).astype(F32) + core[3].astype(F32)).astype(BF)
+        far_x, far_y = self.send(far[:half], "x"), self.send(far[half:], "y")
+        yield True
+        low = jnp.pad(far_x.astype(F32), ((0, count - half), (0, 0), (0, 0)))
+        high = jnp.pad(far_y.astype(F32), ((half, 0), (0, 0), (0, 0)))
+        to_x = (self.tied(mine[1]).astype(F32) + core[1].astype(F32) + high).astype(BF)
+        to_y = (self.tied(mine[2]).astype(F32) + core[2].astype(F32) + low).astype(BF)
+        x, y = self.send(to_x, "x"), self.send(to_y, "y")
+        yield True
+        total = self.tied(mine[0]).astype(F32) + core[0].astype(F32) + x.astype(F32) + y.astype(F32)
+        total = total.astype(BF)
+        split = min(max(2 * HALF - first, 0), count)
+        runs = [(side, low, high) for side, low, high in ((0, 0, split), (1, split, count)) if low < high]
+        totals = [total[low:high] for _, low, high in runs]
+        self.pins += totals
+        outer, inner, far_in, far_out = (0, 1, 2, 3) if depth == 0 else (3, 2, 1, 0)
+        ones = []
+        for (side, _, _), part in zip(runs, totals):
+            owner = 2 * depth + side
+            ones.append(hop(part, (far_out, far_in), (outer if owner == inner else inner, owner)))
+        yield True
+        for (side, low, high), part, one in zip(runs, totals, ones):
+            joined = (self.tied(part).astype(F32) + one.astype(F32)).astype(BF)
+            self.pins.append(joined)
+            owner = 2 * depth + side
+            last = hop(joined, (far_in, owner))
+            for at in range(low, high):
+                self.parts[depth, first + at] = (joined, last, at - low)
+        yield True
+
+    def own_blocks(self, low, high):
+        head = lax.axis_index("head")
+        own = None
+        for owner in range(LINE):
+            runs = []
+            for at in range(low, high):
+                joined, last, block = self.parts[owner // 2, 2 * HALF * (owner % 2) + at]
+                if runs and runs[-1][0] is joined:
+                    runs[-1][3] = block + 1
+                else:
+                    runs.append([joined, last, block, block + 1])
+            sums = [a[start:stop].astype(F32) + b[start:stop].astype(F32) for a, b, start, stop in runs]
+            value = sums[0] if len(sums) == 1 else jnp.concatenate(sums, axis=0)
+            own = value if own is None else jnp.where(head == owner, value, own)
+        return own
+
+    def finish(self, renew):
+        self.last = ()
+        while len(self.chains) > 1:
+            self.chains = [chain for chain in self.chains if next(chain, None)]
+        results = ()
+        for low, high in ((HALF, 2 * HALF), (0, HALF)):
+            if low == 0:
+                while self.chains:
+                    self.chains = [chain for chain in self.chains if next(chain, None)]
+            own = self.own_blocks(low, high)
+            full = PlaneGather(own.astype(BF), 1 + (low == 0))
+            full.first()
+            full.second()
+            full.cores()
+            results = renew(
+                own,
+                Blocks([[(None, full.pieces(at))] for at in range(HALF)]),
+                Blocks([[(None, [(self.right, low + at)])] for at in range(HALF)]),
+                low,
+                results,
+            )
+        return results
+
+    def vector_sum(self, vectors):
+        for axis in ("core", "x", "y"):
+            vectors = vectors + swap(vectors, axis)
+        for step in (1, 2):
+            vectors = vectors + hop(vectors, *((i, i ^ step) for i in range(LINE)))
+        return vectors
 
 
 def on_device(
@@ -606,48 +931,57 @@
     vec_first,
     vec_second,
 ):
-    rounded = weights.astype(BF)
-    block_rows = lax.all_gather(rounded, "head", axis=0, tiled=True)
-    full_blocks = lax.all_gather(block_rows, "dp", axis=1, tiled=True)
-    right_full = lax.all_gather(right_root.astype(BF), "dp", axis=1, tiled=True)
-
-    def group(depth, first, count):
-        return [([full_blocks], depth * PER_LAYER + first, count)]
-
+    fits = lax.axis_size("dp") == DP and lax.axis_size("head") == LINE
+    links = (Permutes if fits else Collectives)(weights, right_root)
     stream = pad_tokens(image_tokens)
+    grad = pad_tokens(cotangent)
     saved = []
+    top = LAYERS - 1
     for depth in range(LAYERS):
         ln_gain, q_gain, k_gain, mlp_bias, out_bias = split_vector(vectors[depth])
-        normed, hidden, slope = mlp_in(stream, ln_gain, mlp_bias, group(depth, 3, RATIO))
-        queries, keys, values, q_unit, q_inv, k_unit, k_inv, attended = attend(
-            normed, q_gain, k_gain, group(depth, 0, 3)
+        normed, queries, keys, values, q_unit, q_inv, k_unit, k_inv, attended = attend(
+            links.next(stream), ln_gain, q_gain, k_gain, links.group((depth, QKV, 3))
         )
+        links.done(f"attend{depth}", attended)
+        hidden, slope = mlp_in(links.next(normed), mlp_bias, links.group((depth, MLP, RATIO)))
+        links.done(f"mlp{depth}", hidden)
         saved.append(
             (stream, normed, hidden, slope, queries, keys, values, q_unit, q_inv, k_unit, k_inv, attended)
         )
+        if depth == top:
+            pieces = weight_grads(
+                [(links.next(attended), grad, 1), (hidden, grad, RATIO)], links.cut, "grad_out"
+            )
+            links.done("grad_out", pieces[0])
+            links.add_grads(depth, OUT, pieces)
         stream = project(
-            stream, attended, hidden, out_bias, group(depth, IN_COUNT, OUT_COUNT), depth == LAYERS - 1
+            links.next(stream), attended, hidden, out_bias, links.group((depth, OUT, OUT_COUNT)), depth == top
         )
+        links.done(f"project{depth}", stream)
     block_out = cut_tokens(stream)
-    grad = pad_tokens(cotangent)
-    weight_parts = [None] * LAYERS
     vector_parts = [None] * LAYERS
     for depth in reversed(range(LAYERS)):
         ln_gain, q_gain, k_gain, _, _ = split_vector(vectors[depth])
         stream, normed, hidden, slope, queries, keys, values, q_unit, q_inv, k_unit, k_inv, attended = saved[depth]
-        dy, do, du, dbo, dbu = mlp_back(grad, slope, group(depth, IN_COUNT, OUT_COUNT))
+        dy, do, du, dbo, dbu = mlp_back(links.next(grad), slope, links.group((depth, OUT, OUT_COUNT)))
+        links.done("mlp_back", dy)
+        segments = [(links.next(normed), du, RATIO)]
+        if depth < top:
+            segments += [(attended, dy, 1), (hidden, dy, RATIO)]
+        pieces = weight_grads(segments, links.cut, "grad_mlp")
+        links.done("grad_mlp", pieces[0])
+        links.add_grads(depth, MLP, pieces)
         dqkv, dgq, dgk = attend_back(
-            do, queries, keys, values, q_unit, q_inv, k_unit, k_inv, q_gain, k_gain
+            links.next(do), queries, keys, values, q_unit, q_inv, k_unit, k_inv, q_gain, k_gain
         )
-        weight_parts[depth] = [
-            weight_grads(normed, dqkv, 3, "grad_qkv"),
-            weight_grads(normed, du, RATIO, "grad_u"),
-            weight_grads(attended, dy, 1, "grad_o"),
-            weight_grads(hidden, dy, RATIO, "grad_a"),
-        ]
+        links.done("attend_back", dqkv)
+        pieces = weight_grads([(links.next(normed), dqkv, 3)], links.cut, "grad_qkv")
+        links.done("grad_qkv", pieces[0])
+        links.add_grads(depth, QKV, pieces)
         grad, dg = stream_back(
-            grad, stream, ln_gain, du, dqkv, group(depth, 3, RATIO) + group(depth, 0, 3)
+            links.next(grad), stream, ln_gain, du, dqkv, links.group((depth, MLP, RATIO), (depth, QKV, 3))
         )
+        links.done("stream_back", grad)
         vector_parts[depth] = jnp.concatenate(
             [
                 dg[0],
@@ -658,15 +992,14 @@
             ]
         )
     grad_stream = cut_tokens(grad)
-    partial_grad = jnp.concatenate([part for parts in weight_parts for part in parts], axis=0)
-    rows_part = lax.psum_scatter(partial_grad, "dp", scatter_dimension=1, tiled=True)
-    own_grad = lax.psum_scatter(rows_part, "head", scatter_dimension=0, tiled=True)
-    weight_grad = own_grad.astype(F32)
-    grad_full = lax.all_gather(own_grad, "dp", axis=1, tiled=True)
-    vector_grad = lax.psum(jnp.stack(vector_parts), ("dp", "head"))
-    left_new, right_new, weight_new, ema_new = shampoo(
-        weight_grad, grad_full, right_full, left_root, left_stats, right_stats, weights, weights_ema
-    )
+    vector_grad = links.vector_sum(jnp.stack(vector_parts))
+
+    def renew(own, full, right, first, earlier):
+        return shampoo(
+            own, full, right, left_root, left_stats, right_stats, weights, weights_ema, first, earlier
+        )
+
+    weight_grad, left_new, right_new, weight_new, ema_new = links.finish(renew)
     first_new = BETA_ONE * vec_first + (1.0 - BETA_ONE) * vector_grad
     second_new = BETA_TWO * vec_second + (1.0 - BETA_TWO) * vector_grad * vector_grad
     first_hat = first_new / (1.0 - BETA_ONE**STEP)

time: 827 us -> 706 us (0.85)
  waiting for transfers between devices: 473 us -> 231 us
  starting transfers between devices: 0.24 us -> 109 us
  blocking collectives: 41.4 us -> 0 us
  Pallas kernels: 251 us -> 278 us
  other arithmetic: 11 us -> 30.5 us
    reduce_scatter x2 -> x0, waiting for transfers between devices: 241 us -> none  [the longest x1 173 us: on_device(): lax.psum_scatter(partial_grad, 'dp', scatter_dimension=1, tiled=True)]
    all_gather x4 -> x3, waiting for transfers between devices: 232 us -> 15.8 us  [the longest x2 15.8 us: __init__(): halves = [lax.all_gather(part.own, 'head') for part in plan]]
    ppermute x0 -> x134, waiting for transfers between devices: none -> 214 us  [the longest x118 158 us: swap(): return lax.ppermute(array, 'dp', [(i, i ^ STEPS[axis]) for i in range(DP)])]
    ppermute x0 -> x134, starting transfers between devices: none -> 108 us  [the longest x118 82.8 us: swap(): return lax.ppermute(array, 'dp', [(i, i ^ STEPS[axis]) for i in range(DP)])]
    psum x1 -> x0, blocking collectives: 41.4 us -> none  [on_device(): vector_grad = lax.psum(jnp.stack(vector_parts), ('dp', 'head'))]
    pallas_call x19, Pallas kernels: 251 us -> 278 us  [call(): pl.pallas_call(kernel, grid=grid, in_specs=in_specs, out_specs=out_specs,...]
    convert_element_type x3 -> x25, other arithmetic: 4.97 us -> 22.8 us  [the longest x4 6.21 us: reduce(): (self.tied(mine[2]).astype(F32) + core[2].astype(F32) + low).astype(BF)]
    unnamed x55 -> x236, local copies, waits for them, and re-layouts: 17.3 us -> 7.58 us
  transfers between devices with their start and end apart: 6 -> 137, of which waited for: 5 -> 38; matrix products, arithmetic and copies ran while one was open for 2% -> 8% of each run, Pallas kernels for 3% -> 30%
where the time goes in v2:
time: 706 us; the launch traced here: 700 us
  Pallas kernels  278 us (39%)
  waiting for transfers between devices  231 us (33%)
  starting transfers between devices  109 us (15%)
  local copies, waits for them, and re-layouts  37 us (5%)
  other arithmetic  30.5 us (4%)
  between operations  15.9 us (2%)
    pallas_call x19, Pallas kernels, call(): pl.pallas_call(kernel, grid=grid, in_specs=in_specs, out_specs=out_specs,...  278 us
    ppermute x118, waiting for transfers between devices, swap(): return lax.ppermute(array, 'dp', [(i, i ^ STEPS[axis]) for i in range(DP)])  158 us
    ppermute x118, starting transfers between devices, swap(): return lax.ppermute(array, 'dp', [(i, i ^ STEPS[axis]) for i in range(DP)])  82.8 us
    ppermute x16, waiting for transfers between devices, hop(): return lax.ppermute(array, 'head', pairs)  56.7 us
    ppermute x16, starting transfers between devices, hop(): return lax.ppermute(array, 'head', pairs)  25.7 us
    all_gather x2, waiting for transfers between devices, __init__(): halves = [lax.all_gather(part.own, 'head') for part in plan]  15.8 us
  transfers between devices with their start and end apart: 137, of which 38 were waited for; matrix products, arithmetic and copies ran while one was open for 8% of the time, Pallas kernels for 30%

profile of v2, /device:TPU:0, one launch (start us, length us, event | category | flops | bytes accessed | tf_op | source)
XLA Modules:
  0.0 700.3 jit_solution(15407837002647254054)
XLA Ops:
  15.7 9.1 %collective-permute-done.refs_1_.refs_17_ = bf16[3,96,768]{2,1,0:T(8,128)(2,1)S(1)} collective-permute-done((bf16[3,96,768]{2,1,0:T(8,128)(2,1)}, bf16[3,96,768]{2,1,0:T(8,128)(2,1)S(1)}, u32[]{:S(2)}, u32[]{:S(2)}) %collective-permute-start) | collective-permute-done | bytes 442400 | tf_op jit(solution)/shard_map/ppermute | solution.py:708
  39.2 13.7 %all-gather.8.cloned.1.call-done = bf16[12,96,768]{2,1,0:T(8,128)(2,1)} async-done(((bf16[3,96,768]{2,1,0:T(8,128)(2,1)}), bf16[12,96,768]{2,1,0:T(8,128)(2,1)}) %all-gather.8.cloned.1.call-update) | async-done | bytes 1769488 | tf_op jit(solution)/shard_map/all_gather | solution.py:756
  78.0 8.7 %collective-permute-done.8.refs_18_.refs_34_.refs_74_.refs_46_ = bf16[2,96,768]{2,1,0:T(8,128)(2,1)} collective-permute-done((bf16[2,96,768]{2,1,0:T(8,128)(2,1)S(1)}, bf16[2,96,768]{2,1,0:T(8,128)(2,1)}, u32[]{:S(2)}, u32[]{:S(2)}) %collective-permute-start.8) | collective-permute-done | bytes 294944 | tf_op jit(solution)/shard_map/ppermute | solution.py:708
  98.6 20.9 %attend.2 = (bf16[624,768]{1,0:T(8,128)(2,1)}, bf16[624,768]{1,0:T(8,128)(2,1)}, bf16[624,768]{1,0:T(8,128)(2,1)}, bf16[624,768]{1,0:T(8,128)(2,1)}, bf16[624,76...) custom-call(bf16[624,768]{1,0:T(8,128)(2,1)} %bitcast.128, ...), custom_call_target="tpu_custom_call" | custom-call | flops 2607022080 | bytes 18588672 | tf_op jit(solution)/shard_map/attend/pallas_call | solution.py:53
  123.7 8.8 %collective-permute-done.27.refs_10_ = bf16[3,96,768]{2,1,0:T(8,128)(2,1)S(1)} collective-permute-done((bf16[3,96,768]{2,1,0:T(8,128)(2,1)S(1)}, bf16[3,96,768]{2,1,0:T(8,128)(2,1)S(1)}, u32[]{:S(2)}, u32[]{:S(2)}) %collective-permute-start.27) | collective-permute-done | bytes 442400 | tf_op jit(solution)/shard_map/ppermute | solution.py:708
  134.7 14.4 %collective-permute-done.47.refs_11_.refs_36_.refs_76_ = bf16[2,96,768]{2,1,0:T(8,128)(2,1)} collective-permute-done((bf16[2,96,768]{2,1,0:T(8,128)(2,1)S(1)}, bf16[2,96,768]{2,1,0:T(8,128)(2,1)}, u32[]{:S(2)}, u32[]{:S(2)}) %collective-permute-start.47) | collective-permute-done | bytes 294944 | tf_op jit(solution)/shard_map/ppermute | solution.py:708
  166.4 17.8 %mlp_in.2 = (bf16[624,3072]{1,0:T(8,128)(2,1)}, bf16[624,3072]{1,0:T(8,128)(2,1)}) custom-call(bf16[624,768]{1,0:T(8,128)(2,1)} %get-tuple-element.309.h_ref.refs_0_, f32[1,3072]{1,0:T(1,128)} %get-tuple-element.378.b_ref, bf16[3,96,768]{2,1,0:T(8,128)(2,1)} %get-tuple-element.197.refs_0_.refs_16_, bf16[3,96,768]{2,1,0:T(8,128)(2,1)} %copy-done.7, ...), custom_call_target="tpu_custom_call" | custom-call | flops 2944401408 | bytes 21614592 | tf_op jit(solution)/shard_map/mlp_in/pallas_call | solution.py:53
  192.7 10.8 %project.2.x_ref = f32[624,768]{1,0:T(8,128)} custom-call(bf16[624,768]{1,0:T(8,128)(2,1)} %bitcast.129, bf16[624,768]{1,0:T(8,128)(2,1)} %get-tuple-element.188.o_ref.refs_2_, bf16[624,3072]{1,0:T(8,128)(2,1)} %get-tuple-element.211.a_ref.refs_4_, f32[1,768]{1,0:T(1,128)} %get-tuple-element.375.b_ref, ...), custom_call_target="tpu_custom_call" | custom-call | flops 3680501760 | bytes 21236736 | tf_op jit(solution)/shard_map/project/pallas_call | solution.py:53
  212.0 21.5 %attend.3 = (bf16[624,768]{1,0:T(8,128)(2,1)}, bf16[624,768]{1,0:T(8,128)(2,1)}, bf16[624,768]{1,0:T(8,128)(2,1)}, bf16[624,768]{1,0:T(8,128)(2,1)}, bf16[624,76...) custom-call(f32[624,768]{1,0:T(8,128)} %project.2.x_ref, ...), custom_call_target="tpu_custom_call" | custom-call | flops 2607022080 | bytes 26625024 | tf_op jit(solution)/shard_map/attend/pallas_call | solution.py:53
  243.0 17.7 %mlp_in.3 = (bf16[624,3072]{1,0:T(8,128)(2,1)}, bf16[624,3072]{1,0:T(8,128)(2,1)}) custom-call(bf16[624,768]{1,0:T(8,128)(2,1)} %get-tuple-element.270.h_ref.refs_0_, f32[1,3072]{1,0:T(1,128)} %get-tuple-element.377.b_ref, bf16[3,96,768]{2,1,0:T(8,128)(2,1)} %get-tuple-element.197.refs_0_.refs_16_, bf16[3,96,768]{2,1,0:T(8,128)(2,1)} %copy-done.7, ...), custom_call_target="tpu_custom_call" | custom-call | flops 2944401408 | bytes 28692480 | tf_op jit(solution)/shard_map/mlp_in/pallas_call | solution.py:53
  260.7 10.1 %grad_out.1 = (bf16[5,96,768]{2,1,0:T(8,128)(2,1)}, bf16[5,96,768]{2,1,0:T(8,128)(2,1)}, bf16[5,96,768]{2,1,0:T(8,128)(2,1)}, bf16[5,96,768]{2,1,0:T(8,128)(2,1)}, bf16[4,5,96,768]{3,2,1,0:T(8,128)(2,1)}) custom-call(bf16[624,768]{1,0:T(8,128)(2,1)} %get-tuple-element.239.refs_0_.o_ref, bf16[624,768]{1,0:T(8,128)(2,1)} %bitcast.131, ...), custom_call_target="tpu_custom_call" | custom-call | flops 3680501760 | bytes 12607488 | tf_op jit(solution)/shard_map/grad_out/pallas_call | solution.py:53
  270.9 10.8 %project.3 = bf16[624,768]{1,0:T(8,128)(2,1)} custom-call(f32[624,768]{1,0:T(8,128)} %project.2.x_ref, bf16[624,768]{1,0:T(8,128)(2,1)} %get-tuple-element.239.refs_0_.o_ref, bf16[624,3072]{1,0:T(8,128)(2,1)} %get-tuple-element.238.refs_2_.a_ref, f32[1,768]{1,0:T(1,128)} %get-tuple-element.373.b_ref, ...), custom_call_target="tpu_custom_call" | custom-call | flops 3680501760 | bytes 21236736 | tf_op jit(solution)/shard_map/project/pallas_call | solution.py:53
  284.2 12.3 %mlp_back.2 = (bf16[624,768]{1,0:T(8,128)(2,1)}, bf16[624,768]{1,0:T(8,128)(2,1)}, bf16[624,3072]{1,0:T(8,128)(2,1)}, f32[1,768]{1,0:T(1,128)}, f32[1,3072]{1,0:T(1,128)}) custom-call(bf16[624,768]{1,0:T(8,128)(2,1)} %bitcast.133, bf16[624,3072]{1,0:T(8,128)(2,1)} %get-tuple-element.246.s_ref, ...), custom_call_target="tpu_custom_call" | custom-call | flops 3680501760 | bytes 24124416 | tf_op jit(solution)/shard_map/mlp_back/pallas_call | solution.py:53
  297.9 8.3 %grad_mlp.2 = (bf16[4,96,768]{2,1,0:T(8,128)(2,1)}, bf16[4,96,768]{2,1,0:T(8,128)(2,1)}, bf16[4,96,768]{2,1,0:T(8,128)(2,1)}, bf16[4,96,768]{2,1,0:T(8,128)(2,1)}, bf16[4,4,96,768]{3,2,1,0:T(8,128)(2,1)}) custom-call(bf16[624,768]{1,0:T(8,128)(2,1)} %get-tuple-element.270.h_ref.refs_0_, bf16[624,3072]{1,0:T(8,128)(2,1)} %get-tuple-element.254.refs_1_.du_ref), custom_call_target="tpu_custom_call" | custom-call | flops 2944401408 | bytes 9510912 | tf_op jit(solution)/shard_map/grad_mlp/pallas_call | solution.py:53
  308.4 16.8 %collective-permute-done.76 = bf16[5,96,768]{2,1,0:T(8,128)(2,1)S(1)} collective-permute-done((bf16[5,96,768]{2,1,0:T(8,128)(2,1)S(1)}, bf16[5,96,768]{2,1,0:T(8,128)(2,1)S(1)}, u32[]{:S(2)}, u32[]{:S(2)}) %collective-permute-start.76) | collective-permute-done | bytes 737312 | tf_op jit(solution)/shard_map/ppermute | solution.py:708
  329.1 23.0 %attend_back.2 = (bf16[624,2304]{1,0:T(8,128)(2,1)}, f32[1,768]{1,0:T(1,128)}, f32[1,768]{1,0:T(1,128)}) custom-call(bf16[624,768]{1,0:T(8,128)(2,1)} %get-tuple-element.258.do_ref, bf16[624,768]{1,0:T(8,128)(2,1)} %get-tuple-element.259.q_ref, bf16[624,768]{1,0:T(8,128)(2,1)} %get-tuple-element.260.k_ref, bf16[624,768]{1,0:T(8,128)(2,1)} %get-tuple-element.261.v_ref, ...), custom_call_target="tpu_custom_call" | custom-call | flops 996802560 | bytes 12472320 | tf_op jit(solution)/shard_map/attend_back/pallas_call | solution.py:53
  361.2 8.2 %collective-permute-done.80 = bf16[2,96,768]{2,1,0:T(8,128)(2,1)S(1)} collective-permute-done((bf16[2,96,768]{2,1,0:T(8,128)(2,1)S(1)}, bf16[2,96,768]{2,1,0:T(8,128)(2,1)S(1)}, u32[]{:S(2)}, u32[]{:S(2)}) %collective-permute-start.80) | collective-permute-done | bytes 294944 | tf_op jit(solution)/shard_map/ppermute | solution.py:708
  372.2 18.1 %stream_back.2 = (f32[624,768]{1,0:T(8,128)}, f32[1,768]{1,0:T(1,128)}) custom-call(bf16[624,768]{1,0:T(8,128)(2,1)} %bitcast.134, f32[624,768]{1,0:T(8,128)} %project.2.x_ref, f32[1,768]{1,0:T(1,128)} %get-tuple-element.374.g_ref.c_ref, bf16[624,3072]{1,0:T(8,128)(2,1)} %get-tuple-element.254.refs_1_.du_ref, ...), custom_call_target="tpu_custom_call" | custom-call | flops 5152702464 | bytes 39819264 | tf_op jit(solution)/shard_map/stream_back/pallas_call | solution.py:53
  395.6 12.8 %mlp_back.3 = (bf16[624,768]{1,0:T(8,128)(2,1)}, bf16[624,768]{1,0:T(8,128)(2,1)}, bf16[624,3072]{1,0:T(8,128)(2,1)}, f32[1,768]{1,0:T(1,128)}, f32[1,3072]{1,0:T(1,128)}) custom-call(f32[624,768]{1,0:T(8,128)} %get-tuple-element.316.g_ref, bf16[624,3072]{1,0:T(8,128)(2,1)} %get-tuple-element.283.s_ref, ...), custom_call_target="tpu_custom_call" | custom-call | flops 3680501760 | bytes 25082880 | tf_op jit(solution)/shard_map/mlp_back/pallas_call | solution.py:53
  409.9 16.5 %grad_mlp.3 = (bf16[9,96,768]{2,1,0:T(8,128)(2,1)}, bf16[9,96,768]{2,1,0:T(8,128)(2,1)}, bf16[9,96,768]{2,1,0:T(8,128)(2,1)}, bf16[9,96,768]{2,1,0:T(8,128)(2,1)}, bf16[4,9,96,768]{3,2,1,0:T(8,128)(2,1)}) custom-call(bf16[624,768]{1,0:T(8,128)(2,1)} %get-tuple-element.309.h_ref.refs_0_, bf16[624,3072]{1,0:T(8,128)(2,1)} %get-tuple-element.293.refs_1_.du_ref, ...), custom_call_target="tpu_custom_call" | custom-call | flops 6624903168 | bytes 22118400 | tf_op jit(solution)/shard_map/grad_mlp/pallas_call | solution.py:53
  429.6 10.6 %collective-permute-done.89 = bf16[3,96,768]{2,1,0:T(8,128)(2,1)S(1)} collective-permute-done((bf16[3,96,768]{2,1,0:T(8,128)(2,1)S(1)}, bf16[3,96,768]{2,1,0:T(8,128)(2,1)S(1)}, u32[]{:S(2)}, u32[]{:S(2)}) %collective-permute-start.89) | collective-permute-done | bytes 442400 | tf_op jit(solution)/shard_map/ppermute | solution.py:708
  444.6 23.1 %attend_back.3 = (bf16[624,2304]{1,0:T(8,128)(2,1)}, f32[1,768]{1,0:T(1,128)}, f32[1,768]{1,0:T(1,128)}) custom-call(bf16[624,768]{1,0:T(8,128)(2,1)} %get-tuple-element.297.do_ref, bf16[624,768]{1,0:T(8,128)(2,1)} %get-tuple-element.298.q_ref, bf16[624,768]{1,0:T(8,128)(2,1)} %get-tuple-element.299.k_ref, bf16[624,768]{1,0:T(8,128)(2,1)} %get-tuple-element.300.v_ref, ...), custom_call_target="tpu_custom_call" | custom-call | flops 996802560 | bytes 12472320 | tf_op jit(solution)/shard_map/attend_back/pallas_call | solution.py:53
  483.3 8.2 %collective-permute-done.93 = bf16[4,96,768]{2,1,0:T(8,128)(2,1)S(1)} collective-permute-done((bf16[4,96,768]{2,1,0:T(8,128)(2,1)}, bf16[4,96,768]{2,1,0:T(8,128)(2,1)S(1)}, u32[]{:S(2)}, u32[]{:S(2)}) %collective-permute-start.93) | collective-permute-done | bytes 589856 | tf_op jit(solution)/shard_map/ppermute | solution.py:708
  512.7 18.3 %stream_back.3 = (f32[624,768]{1,0:T(8,128)}, f32[1,768]{1,0:T(1,128)}) custom-call(f32[624,768]{1,0:T(8,128)} %get-tuple-element.316.g_ref, bf16[624,768]{1,0:T(8,128)(2,1)} %bitcast.130, f32[1,768]{1,0:T(1,128)} %get-tuple-element.376.g_ref.c_ref, bf16[624,3072]{1,0:T(8,128)(2,1)} %get-tuple-element.293.refs_1_.du_ref, ...), custom_call_target="tpu_custom_call" | custom-call | flops 5152702464 | bytes 28612608 | tf_op jit(solution)/shard_map/stream_back/pallas_call | solution.py:53
  541.7 8.4 %collective-permute-start.99 = (bf16[6,96,768]{2,1,0:T(8,128)(2,1)S(1)}, bf16[6,96,768]{2,1,0:T(8,128)(2,1)S(1)}, u32[]{:S(2)}, u32[]{:S(2)}) collective-permute-start(bf16[6,96,768]{2,1,0:T(8,128)(2,1)S(1)} %slice.336), channel_id=1, source_target_pairs={{3,2},{0,1},{7,6},{4,5},{11,10},{8,9},{15,14},{12,13},{19,18},{16,... | collective-permute-start | bytes 2654216 | tf_op jit(solution)/shard_map/ppermute | solution.py:712
  569.5 7.5 %collective-permute-done.106 = bf16[3,96,768]{2,1,0:T(8,128)(2,1)S(1)} collective-permute-done((bf16[3,96,768]{2,1,0:T(8,128)(2,1)S(1)}, bf16[3,96,768]{2,1,0:T(8,128)(2,1)S(1)}, u32[]{:S(2)}, u32[]{:S(2)}) %collective-permute-start.106) | collective-permute-done | bytes 442400 | tf_op jit(solution)/shard_map/ppermute | solution.py:712
  581.1 7.9 %collective-permute-done.119 = bf16[3,96,768]{2,1,0:T(8,128)(2,1)S(1)} collective-permute-done((bf16[3,96,768]{2,1,0:T(8,128)(2,1)S(1)}, bf16[3,96,768]{2,1,0:T(8,128)(2,1)S(1)}, u32[]{:S(2)}, u32[]{:S(2)}) %collective-permute-start.119) | collective-permute-done | bytes 442400 | tf_op jit(solution)/shard_map/ppermute | solution.py:712
  589.0 28.4 %collective-permute-done.107 = bf16[3,96,768]{2,1,0:T(8,128)(2,1)S(1)} collective-permute-done((bf16[3,96,768]{2,1,0:T(8,128)(2,1)S(1)}, bf16[3,96,768]{2,1,0:T(8,128)(2,1)S(1)}, u32[]{:S(2)}, u32[]{:S(2)}) %collective-permute-start.107) | collective-permute-done | bytes 442400 | tf_op jit(solution)/shard_map/ppermute | solution.py:712
  626.5 15.5 %collective-permute-done.131 = f32[2,4736]{1,0:T(2,128)S(1)} collective-permute-done((f32[2,4736]{1,0:T(2,128)S(1)}, f32[2,4736]{1,0:T(2,128)S(1)}, u32[]{:S(2)}, u32[]{:S(2)}) %collective-permute-start.131) | collective-permute-done | bytes 37920 | tf_op jit(solution)/shard_map/ppermute | solution.py:708
  655.7 7.5 %collective-permute-done.122.refs_3_ = bf16[1,96,768]{2,1,0:T(8,128)(2,1)S(1)} collective-permute-done((bf16[1,96,768]{2,1,0:T(8,128)(2,1)S(1)}, bf16[1,96,768]{2,1,0:T(8,128)(2,1)S(1)}, u32[]{:S(2)}, u32[]{:S(2)}) %collective-permute-start.122) | collective-permute-done | bytes 147488 | tf_op jit(solution)/shard_map/ppermute | solution.py:708
  670.4 11.1 %shampoo.2 = (f32[6,96,768]{2,1,0:T(8,128)}, f32[6,96,768]{2,1,0:T(8,128)}, f32[6,96,768]{2,1,0:T(8,128)}, f32[6,96,768]{2,1,0:T(8,128)}, f32[6,96,768]{2,1,0:T(8,128)}) custom-call(f32[3,96,768]{2,1,0:T(8,128)} %get-tuple-element.348.g_ref, f32[6,96,768]{2,1,0:T(8,128)} %lr_ref.3, f32[6,96,768]{2,1,0:T(8,128)} %ls_ref.3, f32[6,96,768]{2,1,0:T(8,128)} %rs_ref.3, ...), custom_call_target="tpu_custom_call" | custom-call | flops 1698693120 | bytes 29196288 | tf_op jit(solution)/shard_map/shampoo/pallas_call | solution.py:53
  682.6 10.9 %shampoo.3 = (f32[6,96,768]{2,1,0:T(8,128)}, f32[6,96,768]{2,1,0:T(8,128)}, f32[6,96,768]{2,1,0:T(8,128)}, f32[6,96,768]{2,1,0:T(8,128)}, f32[6,96,768]{2,1,0:T(8,128)}) custom-call(f32[3,96,768]{2,1,0:T(8,128)} %get-tuple-element.358.g_ref, f32[6,96,768]{2,1,0:T(8,128)} %lr_ref.3, ...), custom_call_target="tpu_custom_call", output_to_operand_aliasing={{0}: (17, {}), {1}: (18, {}), {2}: (19, {}), {3}: (20, {}),... | custom-call | flops 1698693120 | bytes 38043648 | tf_op jit(solution)/shard_map/shampoo/pallas_call | solution.py:53
  (604 shorter events, 246.5 us)
Async XLA Ops:
  7.2 45.8 %all-gather.8.cloned.1.call-start = ((), (), s32[]{:S(2)}) async-start(), calls=%async_computation.1 | async-start | bytes 2211840 | tf_op jit(solution)/shard_map/all_gather | solution.py:756
  9.8 84.0 %all-gather.10.cloned.1.call-start = ((), (), s32[]{:S(2)}) async-start(), calls=%async_computation.2 | async-start | bytes 2211840 | tf_op jit(solution)/shard_map/all_gather | solution.py:756
  10.5 659.5 %all-gather.6.cloned.1.call-start = ((), (), s32[]{:S(2)}) async-start(), calls=%async_computation | async-start | bytes 7962624 | tf_op jit(solution)/shard_map/all_gather | solution.py:798
  24.8 30.5 %collective-permute-start.1 = (bf16[2,96,768]{2,1,0:T(8,128)(2,1)S(1)}, bf16[2,96,768]{2,1,0:T(8,128)(2,1)S(1)}, u32[]{:S(2)}, u32[]{:S(2)}) collective-permute-start(bf16[2,96,768]{2,1,0:T(8,128)(2,1)S(1)} %slice.290), channel_id=1, source_target_pairs={{0,16},{4,20},{8,24},{12,28},{16,0},{20,4},{24,8},{28,12},{1,17},{... | collective-permute-start | bytes 884744 | tf_op jit(solution)/shard_map/ppermute | solution.py:708
  27.8 29.1 %collective-permute-start.21 = (bf16[2,96,768]{2,1,0:T(8,128)(2,1)}, bf16[2,96,768]{2,1,0:T(8,128)(2,1)S(1)}, u32[]{:S(2)}, u32[]{:S(2)}) collective-permute-start(bf16[2,96,768]{2,1,0:T(8,128)(2,1)} %slice.297), channel_id=1, source_target_pairs={{0,8},{4,12},{8,0},{12,4},{16,24},{20,28},{24,16},{28,20},{1,9},{5... | collective-permute-start | bytes 884744 | tf_op jit(solution)/shard_map/ppermute | solution.py:708
  91.6 28.5 %collective-permute-start.30 = (bf16[3,96,768]{2,1,0:T(8,128)(2,1)S(1)}, bf16[3,96,768]{2,1,0:T(8,128)(2,1)S(1)}, u32[]{:S(2)}, u32[]{:S(2)}) collective-permute-start(bf16[3,96,768]{2,1,0:T(8,128)(2,1)S(1)} %copy-done.1), channel_id=1, source_target_pairs={{0,4},{4,0},{8,12},{12,8},{16,20},{20,16},{24,28},{28,24},{1,5},{5... | collective-permute-start | bytes 1327112 | tf_op jit(solution)/shard_map/ppermute | solution.py:708
  96.4 25.3 %collective-permute-start.31 = (bf16[3,96,768]{2,1,0:T(8,128)(2,1)S(1)}, bf16[3,96,768]{2,1,0:T(8,128)(2,1)S(1)}, u32[]{:S(2)}, u32[]{:S(2)}) collective-permute-start(bf16[3,96,768]{2,1,0:T(8,128)(2,1)S(1)} %collective-permute-done.refs_1_.refs_17_), channel_id=1, source_target_pairs={{0,4},{4,0},{8,12},{12,8},{16,20},{20,16},{24,28},{28,24},{1,5},{5... | collective-permute-start | bytes 1327112 | tf_op jit(solution)/shard_map/ppermute | solution.py:708
  96.5 25.7 %collective-permute-start.32 = (bf16[3,96,768]{2,1,0:T(8,128)(2,1)S(1)}, bf16[3,96,768]{2,1,0:T(8,128)(2,1)S(1)}, u32[]{:S(2)}, u32[]{:S(2)}) collective-permute-start(bf16[3,96,768]{2,1,0:T(8,128)(2,1)S(1)} %copy-done.9), channel_id=1, source_target_pairs={{0,4},{4,0},{8,12},{12,8},{16,20},{20,16},{24,28},{28,24},{1,5},{5... | collective-permute-start | bytes 1327112 | tf_op jit(solution)/shard_map/ppermute | solution.py:708
  97.0 23.1 %collective-permute-start.33 = (bf16[2,96,768]{2,1,0:T(8,128)(2,1)S(1)}, bf16[2,96,768]{2,1,0:T(8,128)(2,1)S(1)}, u32[]{:S(2)}, u32[]{:S(2)}) collective-permute-start(bf16[2,96,768]{2,1,0:T(8,128)(2,1)S(1)} %copy-done.16), channel_id=1, source_target_pairs={{0,4},{4,0},{8,12},{12,8},{16,20},{20,16},{24,28},{28,24},{1,5},{5... | collective-permute-start | bytes 884744 | tf_op jit(solution)/shard_map/ppermute | solution.py:708
  97.1 22.4 %collective-permute-start.40 = (bf16[1,96,768]{2,1,0:T(8,128)(2,1)S(1)}, bf16[1,96,768]{2,1,0:T(8,128)(2,1)S(1)}, u32[]{:S(2)}, u32[]{:S(2)}) collective-permute-start(bf16[1,96,768]{2,1,0:T(8,128)(2,1)S(1)} %slice.292), channel_id=1, source_target_pairs={{0,16},{4,20},{8,24},{12,28},{16,0},{20,4},{24,8},{28,12},{1,17},{... | collective-permute-start | bytes 442376 | tf_op jit(solution)/shard_map/ppermute | solution.py:708
  121.7 27.4 %collective-permute-start.24 = (bf16[3,96,768]{2,1,0:T(8,128)(2,1)S(1)}, bf16[3,96,768]{2,1,0:T(8,128)(2,1)S(1)}, u32[]{:S(2)}, u32[]{:S(2)}) collective-permute-start(bf16[3,96,768]{2,1,0:T(8,128)(2,1)S(1)} %get-tuple-element.217.refs_24_.refs_16_), channel_id=1, source_target_pairs={{0,8},{4,12},{8,0},{12,4},{16,24},{20,28},{24,16},{28,20},{1,9},{5... | collective-permute-start | bytes 1327112 | tf_op jit(solution)/shard_map/ppermute | solution.py:708
  122.2 27.4 %collective-permute-start.29 = (bf16[3,96,768]{2,1,0:T(8,128)(2,1)S(1)}, bf16[3,96,768]{2,1,0:T(8,128)(2,1)S(1)}, u32[]{:S(2)}, u32[]{:S(2)}) collective-permute-start(bf16[3,96,768]{2,1,0:T(8,128)(2,1)S(1)} %get-tuple-element.217.refs_24_.refs_16_), channel_id=1, source_target_pairs={{0,16},{4,20},{8,24},{12,28},{16,0},{20,4},{24,8},{28,12},{1,17},{... | collective-permute-start | bytes 1327112 | tf_op jit(solution)/shard_map/ppermute | solution.py:708
  123.7 26.0 %collective-permute-start.34 = (bf16[3,96,768]{2,1,0:T(8,128)(2,1)S(1)}, bf16[3,96,768]{2,1,0:T(8,128)(2,1)S(1)}, u32[]{:S(2)}, u32[]{:S(2)}) collective-permute-start(bf16[3,96,768]{2,1,0:T(8,128)(2,1)S(1)} %get-tuple-element.201.refs_8_), channel_id=1, source_target_pairs={{0,4},{4,0},{8,12},{12,8},{16,20},{20,16},{24,28},{28,24},{1,5},{5... | collective-permute-start | bytes 1327112 | tf_op jit(solution)/shard_map/ppermute | solution.py:708
  159.9 24.3 %collective-permute-start.48 = (bf16[2,96,768]{2,1,0:T(8,128)(2,1)}, bf16[2,96,768]{2,1,0:T(8,128)(2,1)}, u32[]{:S(2)}, u32[]{:S(2)}) collective-permute-start(bf16[2,96,768]{2,1,0:T(8,128)(2,1)} %collective-permute-done.47.refs_11_.refs_36_.refs_76_), channel_id=1, source_target_pairs={{0,4},{4,0},{8,12},{12,8},{16,20},{20,16},{24,28},{28,24},{1,5},{5... | collective-permute-start | bytes 884744 | tf_op jit(solution)/shard_map/ppermute | solution.py:708
  160.9 24.0 %collective-permute-start.45 = (bf16[3,96,768]{2,1,0:T(8,128)(2,1)}, bf16[3,96,768]{2,1,0:T(8,128)(2,1)}, u32[]{:S(2)}, u32[]{:S(2)}) collective-permute-start(bf16[3,96,768]{2,1,0:T(8,128)(2,1)} %get-tuple-element.225.refs_24_.refs_48_.refs_8_), channel_id=1, source_target_pairs={{0,8},{4,12},{8,0},{12,4},{16,24},{20,28},{24,16},{28,20},{1,9},{5... | collective-permute-start | bytes 1327112 | tf_op jit(solution)/shard_map/ppermute | solution.py:708
  162.4 22.4 %collective-permute-start.49 = (bf16[2,96,768]{2,1,0:T(8,128)(2,1)}, bf16[2,96,768]{2,1,0:T(8,128)(2,1)}, u32[]{:S(2)}, u32[]{:S(2)}) collective-permute-start(bf16[2,96,768]{2,1,0:T(8,128)(2,1)} %slice.298), channel_id=1, source_target_pairs={{0,16},{4,20},{8,24},{12,28},{16,0},{20,4},{24,8},{28,12},{1,17},{... | collective-permute-start | bytes 884744 | tf_op jit(solution)/shard_map/ppermute | solution.py:708
  209.3 26.3 %collective-permute-start.65 = (bf16[2,96,768]{2,1,0:T(8,128)(2,1)S(1)}, bf16[2,96,768]{2,1,0:T(8,128)(2,1)S(1)}, u32[]{:S(2)}, u32[]{:S(2)}) collective-permute-start(bf16[2,96,768]{2,1,0:T(8,128)(2,1)S(1)} %slice.304), channel_id=1, source_target_pairs={{0,16},{4,20},{8,24},{12,28},{16,0},{20,4},{24,8},{28,12},{1,17},{... | collective-permute-start | bytes 884744 | tf_op jit(solution)/shard_map/ppermute | solution.py:708
  306.2 46.0 %collective-permute-start.78 = (bf16[4,4,96,768]{3,2,1,0:T(8,128)(2,1)}, bf16[4,4,96,768]{3,2,1,0:T(8,128)(2,1)S(1)}, u32[]{:S(2)}, u32[]{:S(2)}) collective-permute-start(bf16[4,4,96,768]{3,2,1,0:T(8,128)(2,1)} %get-tuple-element.257), channel_id=1, source_target_pairs={{0,4},{4,0},{8,12},{12,8},{16,20},{20,16},{24,28},{28,24},{1,5},{5... | collective-permute-start | bytes 7077896 | tf_op jit(solution)/shard_map/ppermute | solution.py:708
  326.8 25.3 %collective-permute-start.77 = (bf16[5,96,768]{2,1,0:T(8,128)(2,1)S(1)}, bf16[5,96,768]{2,1,0:T(8,128)(2,1)S(1)}, u32[]{:S(2)}, u32[]{:S(2)}) collective-permute-start(bf16[5,96,768]{2,1,0:T(8,128)(2,1)S(1)} %fusion.10), channel_id=1, source_target_pairs={{0,1},{2,3},{4,5},{6,7},{8,9},{10,11},{12,13},{14,15},{16,17},{18,... | collective-permute-start | bytes 2211848 | tf_op jit(solution)/shard_map/ppermute | solution.py:712
  360.0 33.3 %collective-permute-start.83 = (bf16[4,3,96,768]{3,2,1,0:T(8,128)(2,1)}, bf16[4,3,96,768]{3,2,1,0:T(8,128)(2,1)S(1)}, u32[]{:S(2)}, u32[]{:S(2)}) collective-permute-start(bf16[4,3,96,768]{3,2,1,0:T(8,128)(2,1)} %get-tuple-element.276), channel_id=1, source_target_pairs={{0,4},{4,0},{8,12},{12,8},{16,20},{20,16},{24,28},{28,24},{1,5},{5... | collective-permute-start | bytes 5308424 | tf_op jit(solution)/shard_map/ppermute | solution.py:708
  426.4 41.3 %collective-permute-start.91 = (bf16[4,9,96,768]{3,2,1,0:T(8,128)(2,1)}, bf16[4,9,96,768]{3,2,1,0:T(8,128)(2,1)}, u32[]{:S(2)}, u32[]{:S(2)}) collective-permute-start(bf16[4,9,96,768]{3,2,1,0:T(8,128)(2,1)} %get-tuple-element.296), channel_id=1, source_target_pairs={{0,4},{4,0},{8,12},{12,8},{16,20},{20,16},{24,28},{28,24},{1,5},{5... | collective-permute-start | bytes 15925256 | tf_op jit(solution)/shard_map/ppermute | solution.py:708
  443.3 30.8 %collective-permute-start.90 = (bf16[3,96,768]{2,1,0:T(8,128)(2,1)S(1)}, bf16[3,96,768]{2,1,0:T(8,128)(2,1)S(1)}, u32[]{:S(2)}, u32[]{:S(2)}) collective-permute-start(bf16[3,96,768]{2,1,0:T(8,128)(2,1)S(1)} %fusion.34), channel_id=1, source_target_pairs={{0,1},{3,2},{4,5},{7,6},{8,9},{11,10},{12,13},{15,14},{16,17},{19,... | collective-permute-start | bytes 1327112 | tf_op jit(solution)/shard_map/ppermute | solution.py:712
  481.7 52.3 %collective-permute-start.101 = (bf16[4,3,96,768]{3,2,1,0:T(8,128)(2,1)}, bf16[4,3,96,768]{3,2,1,0:T(8,128)(2,1)S(1)}, u32[]{:S(2)}, u32[]{:S(2)}) collective-permute-start(bf16[4,3,96,768]{3,2,1,0:T(8,128)(2,1)} %get-tuple-element.315), channel_id=1, source_target_pairs={{0,4},{4,0},{8,12},{12,8},{16,20},{20,16},{24,28},{28,24},{1,5},{5... | collective-permute-start | bytes 5308424 | tf_op jit(solution)/shard_map/ppermute | solution.py:708
  498.8 38.5 %collective-permute-start.98 = (bf16[9,96,768]{2,1,0:T(8,128)(2,1)}, bf16[9,96,768]{2,1,0:T(8,128)(2,1)}, u32[]{:S(2)}, u32[]{:S(2)}) collective-permute-start(bf16[9,96,768]{2,1,0:T(8,128)(2,1)} %get-tuple-element.351), channel_id=1, source_target_pairs={{0,16},{4,20},{8,24},{12,28},{16,0},{20,4},{24,8},{28,12},{1,17},{... | collective-permute-start | bytes 3981320 | tf_op jit(solution)/shard_map/ppermute | solution.py:708
  499.2 38.1 %collective-permute-start.97 = (bf16[9,96,768]{2,1,0:T(8,128)(2,1)}, bf16[9,96,768]{2,1,0:T(8,128)(2,1)}, u32[]{:S(2)}, u32[]{:S(2)}) collective-permute-start(bf16[9,96,768]{2,1,0:T(8,128)(2,1)} %get-tuple-element.352), channel_id=1, source_target_pairs={{0,8},{4,12},{8,0},{12,4},{16,24},{20,28},{24,16},{28,20},{1,9},{5... | collective-permute-start | bytes 3981320 | tf_op jit(solution)/shard_map/ppermute | solution.py:708
  506.8 72.5 %collective-permute-start.117 = (bf16[3,96,768]{2,1,0:T(8,128)(2,1)S(1)}, bf16[3,96,768]{2,1,0:T(8,128)(2,1)}, u32[]{:S(2)}, u32[]{:S(2)}) collective-permute-start(bf16[3,96,768]{2,1,0:T(8,128)(2,1)S(1)} %add_convert_fusion.5), channel_id=1, source_target_pairs={{1,2},{5,6},{9,10},{13,14},{17,18},{21,22},{25,26},{29,30}} | collective-permute-start | bytes 1327112 | tf_op jit(solution)/shard_map/ppermute | solution.py:712
  541.7 26.3 %collective-permute-start.99 = (bf16[6,96,768]{2,1,0:T(8,128)(2,1)S(1)}, bf16[6,96,768]{2,1,0:T(8,128)(2,1)S(1)}, u32[]{:S(2)}, u32[]{:S(2)}) collective-permute-start(bf16[6,96,768]{2,1,0:T(8,128)(2,1)S(1)} %slice.336), channel_id=1, source_target_pairs={{3,2},{0,1},{7,6},{4,5},{11,10},{8,9},{15,14},{12,13},{19,18},{16,... | collective-permute-start | bytes 2654216 | tf_op jit(solution)/shard_map/ppermute | solution.py:712
  577.1 40.4 %collective-permute-start.100 = (bf16[6,96,768]{2,1,0:T(8,128)(2,1)S(1)}, bf16[6,96,768]{2,1,0:T(8,128)(2,1)S(1)}, u32[]{:S(2)}, u32[]{:S(2)}) collective-permute-start(bf16[6,96,768]{2,1,0:T(8,128)(2,1)S(1)} %add_convert_fusion), channel_id=1, source_target_pairs={{2,1},{6,5},{10,9},{14,13},{18,17},{22,21},{26,25},{30,29}} | collective-permute-start | bytes 2654216 | tf_op jit(solution)/shard_map/ppermute | solution.py:712
  577.9 39.5 %collective-permute-start.107 = (bf16[3,96,768]{2,1,0:T(8,128)(2,1)S(1)}, bf16[3,96,768]{2,1,0:T(8,128)(2,1)S(1)}, u32[]{:S(2)}, u32[]{:S(2)}) collective-permute-start(bf16[3,96,768]{2,1,0:T(8,128)(2,1)S(1)} %add_convert_fusion.3), channel_id=1, source_target_pairs={{2,0},{6,4},{10,8},{14,12},{18,16},{22,20},{26,24},{30,28}} | collective-permute-start | bytes 1327112 | tf_op jit(solution)/shard_map/ppermute | solution.py:712
  579.3 45.5 %collective-permute-start.130 = (f32[2,4736]{1,0:T(2,128)S(1)}, f32[2,4736]{1,0:T(2,128)S(1)}, u32[]{:S(2)}, u32[]{:S(2)}) collective-permute-start(f32[2,4736]{1,0:T(2,128)S(1)} %fusion.41), channel_id=1, source_target_pairs={{0,8},{4,12},{8,0},{12,4},{16,24},{20,28},{24,16},{28,20},{1,9},{5... | collective-permute-start | bytes 113672 | tf_op jit(solution)/shard_map/ppermute | solution.py:708
  620.7 26.4 %collective-permute-start.108 = (bf16[3,96,768]{2,1,0:T(8,128)(2,1)S(1)}, bf16[3,96,768]{2,1,0:T(8,128)(2,1)S(1)}, u32[]{:S(2)}, u32[]{:S(2)}) collective-permute-start(bf16[3,96,768]{2,1,0:T(8,128)(2,1)S(1)} %get-tuple-element.357.refs_0_), channel_id=1, source_target_pairs={{0,8},{4,12},{8,0},{12,4},{16,24},{20,28},{24,16},{28,20},{1,9},{5... | collective-permute-start | bytes 1327112 | tf_op jit(solution)/shard_map/ppermute | solution.py:708
  623.8 22.8 %collective-permute-start.120 = (bf16[3,96,768]{2,1,0:T(8,128)(2,1)S(1)}, bf16[3,96,768]{2,1,0:T(8,128)(2,1)S(1)}, u32[]{:S(2)}, u32[]{:S(2)}) collective-permute-start(bf16[3,96,768]{2,1,0:T(8,128)(2,1)S(1)} %get-tuple-element.347.refs_0_), channel_id=1, source_target_pairs={{0,8},{4,12},{8,0},{12,4},{16,24},{20,28},{24,16},{28,20},{1,9},{5... | collective-permute-start | bytes 1327112 | tf_op jit(solution)/shard_map/ppermute | solution.py:708
  (223 other events, 3293.8 us)
Sparse Core Ops, SparseCore 0:
  9.9 43.0 all-gather.7
  54.5 39.1 all-gather.9
  427.6 59.0 all-gather.5

commit v3 on v2

v3 whole, which is shorter than its diff:
```python
import functools
import math

import jax
import jax.numpy as jnp
from jax import lax
from jax.experimental import pallas as pl
from jax.experimental.pallas import tpu as pltpu
from jax.sharding import PartitionSpec as P

D = 768
HEADS = 12
HEAD_DIM = 64
FF = 3072
SEQ = 196
PAD = 208
LAYERS = 2
STEP = 10
RATIO = FF // D
IN_COUNT = 3 + RATIO
OUT_COUNT = 1 + RATIO
PER_LAYER = IN_COUNT + OUT_COUNT
PAIR = 2 * HEAD_DIM
TILE = 256

EPS_NORM = 1e-06
BETA_ONE = 0.9
BETA_TWO = 0.95
ADAM_EPS = 1e-08
RATE_VEC = 0.3
RATE_MAT = 0.003
DECAY_MAT = 0.1
STAT_DECAY = 0.5
EMA_DECAY = 0.8
SCALE = HEAD_DIM ** (-0.5)
EXP2_SCALE = SCALE * math.log2(math.e)

BF = jnp.bfloat16
F32 = jnp.float32
NN = (((1,), (0,)), ((), ()))
NT = (((1,), (1,)), ((), ()))
TN = (((0,), (0,)), ((), ()))


def dot(a, b, dims=NN):
    return lax.dot_general(a, b, dims, preferred_element_type=F32)


def call(kernel, grid, operands, in_specs, outs, out_specs, scratch, about_us, name, aliases=None):
    moved = sum(o.size * o.dtype.itemsize for o in operands) + sum(
        math.prod(o.shape) * o.dtype.itemsize for o in outs
    )
    return pl.pallas_call(
        kernel,
        grid=grid,
        in_specs=in_specs,
        out_specs=out_specs,
        out_shape=outs,
        scratch_shapes=scratch,
        compiler_params=pltpu.CompilerParams(vmem_limit_bytes=24 * 1024 * 1024),
        cost_estimate=pl.CostEstimate(flops=int(about_us * 1.1e9), bytes_accessed=moved, transcendentals=0),
        input_output_aliases=aliases or {},
        name=name,
    )(*operands)


def whole(shape):
    return pl.BlockSpec(shape, lambda *ids: (0,) * len(shape))


def sds(shape, dtype):
    return jax.ShapeDtypeStruct(shape, dtype)


WAYS = (0, 1, 2, 3)


class Blocks:
    def __init__(self, steps):
        self.steps = steps
        self.arrays = []
        for places in steps:
            for _, pieces in places:
                for array, _ in pieces:
                    if not any(array is other for other in self.arrays):
                        self.arrays.append(array)
        self.count = len(steps[0][0][1])
        self.specs = [pl.BlockSpec(memory_space=pltpu.HBM)] * len(self.arrays)
        self.scratch = [pltpu.VMEM((2, D, D), BF), pltpu.SemaphoreType.DMA((2, self.count))]

    def bind(self, refs, held, sems):
        self.refs, self.held, self.sems = refs, held, sems

    def copies(self, pieces, slot):
        made = []
        for at, (array, block) in enumerate(pieces):
            ref = next(ref for ref, other in zip(self.refs, self.arrays) if other is array)
            target = self.held.at[slot]
            if self.count > 1:
                rows = array.shape[-2]
                row = piece_row(at % 4, at // 4, rows)
                target = self.held.at[slot, pl.ds(pl.multiple_of(row, 16), rows)]
            made.append(pltpu.make_async_copy(ref.at[block], target, self.sems.at[slot, at]))
        return made

    def start(self, j, wanted):
        head = lax.axis_index("head")
        for step, places in enumerate(self.steps):
            for owners, pieces in places:
                here = wanted == step
                if owners is not None:
                    here = here & functools.reduce(lambda a, b: a | b, [head == owner for owner in owners])

                @pl.when(here)
                def _(step=step, pieces=pieces):
                    for copy in self.copies(pieces, step % 2):
                        copy.start()

    def step(self, j):
        @pl.when(j == 0)
        def _():
            self.start(j, j)

        @pl.when(j + 1 < len(self.steps))
        def _():
            self.start(j, j + 1)

        slot = lax.rem(j, 2)
        for copy in self.copies(self.steps[0][0][1], slot):
            copy.wait()
        return self.held.at[slot]


def piece_row(way, dc, rows):
    me = lax.axis_index("dp")
    core, x, y = lax.rem(me, 2), lax.rem(me // 2, 2), me // 4
    core = 1 - core if dc else core
    dx, dy = ((0, 0), (1 - core, core), (core, 1 - core), (1, 1))[way]
    return ((y + dy - 2 * y * dy) * 4 + (x + dx - 2 * x * dx) * 2 + core) * rows


def row_parts(values):
    average = jnp.mean(values, axis=-1, keepdims=True)
    centred = values - average
    inverse = lax.rsqrt(jnp.mean(centred * centred, axis=-1, keepdims=True) + EPS_NORM)
    return centred * inverse, inverse


def head_mixer():
    row = lax.broadcasted_iota(jnp.int32, (TILE, TILE), 0) // HEAD_DIM
    column = lax.broadcasted_iota(jnp.int32, (TILE, TILE), 1) // HEAD_DIM
    return jnp.where(row == column, 1.0 / HEAD_DIM, 0.0).astype(BF)


def head_mean(values, mixer):
    high = values.astype(BF)
    low = (values - high.astype(F32)).astype(BF)
    return dot(high, mixer) + dot(low, mixer)


def gelu_parts(z):
    decay = jnp.exp2(z * z * (-0.5 * math.log2(math.e)))
    t = 1.0 / (1.0 + (0.3275911 * math.sqrt(0.5)) * jnp.abs(z))
    poly = 0.5 * 1.061405429
    for factor in (-1.453152027, 1.421413741, -0.284496736, 0.254829592):
        poly = poly * t + 0.5 * factor
    tail = poly * t * decay
    share = jnp.where(z >= 0, 1.0 - tail, tail)
    return z * share, share + z * decay * (1.0 / math.sqrt(2.0 * math.pi))


def tiles(rows, columns):
    return [(slice(r, r + PAD), slice(c, c + TILE)) for r in range(0, rows, PAD) for c in range(0, columns, TILE)]


def mlp_in(normed, bias, blocks):
    tokens = normed.shape[0]

    def kernel(h_ref, b_ref, *refs):
        w_refs, (a_ref, s_ref, *fetch) = refs[: len(blocks.arrays)], refs[len(blocks.arrays) :]
        blocks.bind(w_refs, *fetch)
        block = blocks.step(pl.program_id(0))
        spots = tiles(tokens, D)
        wide = [dot(h_ref[rows, :], block[:, columns]) for rows, columns in spots]
        for (rows, columns), z in zip(spots, wide):
            act, slope = gelu_parts(z + b_ref[:, columns])
            a_ref[rows, columns] = act.astype(BF)
            s_ref[rows, columns] = slope.astype(BF)

    return call(
        kernel,
        (RATIO,),
        [normed, bias] + blocks.arrays,
        [whole((tokens, D)), pl.BlockSpec((1, D), lambda j: (0, j))] + blocks.specs,
        [sds((tokens, FF), BF), sds((tokens, FF), BF)],
        [pl.BlockSpec((tokens, D), lambda j: (0, j))] * 2,
        blocks.scratch,
        11.0,
        "mlp_in",
    )


def half_masks(rows):
    low = lax.broadcasted_iota(jnp.int32, (rows, PAIR), 1) < HEAD_DIM
    return low


def split_pair(values, low):
    zero = jnp.zeros_like(values)
    return jnp.where(low, values, zero), jnp.where(low, zero, values)


def split_rows(values, top):
    zero = jnp.zeros_like(values)
    return jnp.where(top, values, zero), jnp.where(top, zero, values)


def qkv_in(stream, ln_gain, gains, blocks):
    tokens = stream.shape[0]

    def kernel(x_ref, g_ref, c_ref, *refs):
        w_refs, (h_ref, n_ref, u_ref, i_ref, *fetch) = refs[: len(blocks.arrays)], refs[len(blocks.arrays) :]
        blocks.bind(w_refs, *fetch)
        j = pl.program_id(0)

        @pl.when(j == 0)
        def _():
            for row in range(0, tokens, PAD):
                rows = slice(row, row + PAD)
                unit, _ = row_parts(x_ref[rows, :].astype(F32))
                h_ref[rows, :] = (unit * g_ref[...]).astype(BF)

        block = blocks.step(j)

        @pl.when(j < 2)
        def _():
            mixer = head_mixer()
            spots = tiles(tokens, D)
            raws = [dot(h_ref[rows, :], block[:, columns]) for rows, columns in spots]
            centred = [raw - head_mean(raw, mixer) for raw in raws]
            spreads = [head_mean(part * part, mixer) for part in centred]
            for (rows, columns), part, spread in zip(spots, centred, spreads):
                inverse = lax.rsqrt(spread + EPS_NORM)
                unit = part * inverse
                n_ref[rows, columns] = (unit * c_ref[0, :, columns]).astype(BF)
                u_ref[rows, columns] = unit.astype(BF)
                i_ref[rows, columns] = inverse

        @pl.when(j == 2)
        def _():
            n_ref[...] = dot(h_ref[...], block[...]).astype(BF)

    first_two = lambda j: (0, jnp.minimum(j, 1))
    return call(
        kernel,
        (3,),
        [stream, ln_gain, gains] + blocks.arrays,
        [
            whole((tokens, D)),
            whole((1, D)),
            pl.BlockSpec((1, 1, D), lambda j: (jnp.minimum(j, 1), 0, 0)),
        ]
        + blocks.specs,
        [
            sds((tokens, D), BF),
            sds((tokens, 3 * D), BF),
            sds((tokens, 2 * D), BF),
            sds((tokens, 2 * D), F32),
        ],
        [
            whole((tokens, D)),
            pl.BlockSpec((tokens, D), lambda j: (0, j)),
            pl.BlockSpec((tokens, D), first_two),
            pl.BlockSpec((tokens, D), first_two),
        ],
        blocks.scratch,
        9.0,
        "qkv_in",
    )


def attend(qkv):
    tokens = qkv.shape[0]

    def kernel(z_ref, o_ref):
        low = half_masks(PAD)
        valid = lax.broadcasted_iota(jnp.int32, (PAD, PAD), 1) < SEQ
        raw = []
        for at in range(0, D, PAIR):
            keys = z_ref[:, D + at : D + at + PAIR]
            raw += [dot(query, keys, NT) for query in split_pair(z_ref[:, at : at + PAIR], low)]
        raised = [jnp.where(valid, jnp.exp2(part * EXP2_SCALE), 0.0) for part in raw]
        shares = [1.0 / jnp.sum(part, axis=1, keepdims=True) for part in raised]
        for pair, at in enumerate(range(0, D, PAIR)):
            values = z_ref[:, 2 * D + at : 2 * D + at + PAIR]
            sides = [dot(raised[n].astype(BF), values) * shares[n] for n in (2 * pair, 2 * pair + 1)]
            o_ref[:, at : at + PAIR] = jnp.where(low, sides[0], sides[1]).astype(BF)

    return call(
        kernel,
        (tokens // PAD,),
        [qkv],
        [pl.BlockSpec((PAD, 3 * D), lambda i: (i, 0))],
        [sds((tokens, D), BF)],
        [pl.BlockSpec((PAD, D), lambda i: (i, 0))],
        [],
        8.0,
        "attend",
    )[0]


def project(stream, attended, hidden, bias, blocks, last):
    tokens = stream.shape[0]

    def kernel(x_ref, o_ref, a_ref, b_ref, *refs):
        w_refs, (y_ref, total, x_held, x_sem, *fetch) = refs[: len(blocks.arrays)], refs[len(blocks.arrays) :]
        blocks.bind(w_refs, *fetch)
        j = pl.program_id(0)
        x_copy = pltpu.make_async_copy(x_ref, x_held, x_sem)
        block = blocks.step(j)

        @pl.when(j == 0)
        def _():
            x_copy.start()
            total[...] = dot(o_ref[...], block[...])

        @pl.when((j > 0) & (j < OUT_COUNT - 1))
        def _():
            total[...] += dot(a_ref[...], block[...])

        @pl.when(j == OUT_COUNT - 1)
        def _():
            x_copy.wait()
            for rows, columns in tiles(tokens, D):
                y_ref[rows, columns] = (
                    total[rows, columns]
                    + (x_held[rows, columns].astype(F32) + b_ref[:, columns])
                    + dot(a_ref[rows, :], block[:, columns])
                ).astype(y_ref.dtype)

    return call(
        kernel,
        (OUT_COUNT,),
        [stream, attended, hidden, bias] + blocks.arrays,
        [
            pl.BlockSpec(memory_space=pl.ANY),
            whole((tokens, D)),
            pl.BlockSpec((tokens, D), lambda j: (0, jnp.maximum(j - 1, 0))),
            whole((1, D)),
        ]
        + blocks.specs,
        [sds((tokens, D), BF if last else F32)],
        [whole((tokens, D))],
        [pltpu.VMEM((tokens, D), F32), pltpu.VMEM((tokens, D), stream.dtype), pltpu.SemaphoreType.DMA]
        + blocks.scratch,
        8.0,
        "project",
    )[0]


def mlp_back(grad, slope, blocks):
    tokens = grad.shape[0]

    def kernel(g_ref, s_ref, *refs):
        w_refs, refs = refs[: len(blocks.arrays)], refs[len(blocks.arrays) :]
        dy_ref, do_ref, du_ref, dbo_ref, dbu_ref, *fetch = refs
        blocks.bind(w_refs, *fetch)
        j = pl.program_id(0)

        @pl.when(j == 0)
        def _():
            dy = g_ref[...].astype(BF)
            dy_ref[...] = dy
            dbo_ref[...] = jnp.sum(dy.astype(F32), axis=0, keepdims=True)

        block = blocks.step(j)

        @pl.when(j == 0)
        def _():
            do_ref[...] = dot(dy_ref[...], block[...], NT).astype(BF)

        @pl.when(j > 0)
        def _():
            du = (dot(dy_ref[...], block[...], NT) * s_ref[...].astype(F32)).astype(BF)
            du_ref[...] = du
            dbu_ref[...] = jnp.sum(du.astype(F32), axis=0, keepdims=True)

    shifted = pl.BlockSpec((tokens, D), lambda j: (0, jnp.maximum(j - 1, 0)))
    return call(
        kernel,
        (OUT_COUNT,),
        [grad, slope] + blocks.arrays,
        [whole((tokens, D)), shifted] + blocks.specs,
        [
            sds((tokens, D), BF),
            sds((tokens, D), BF),
            sds((tokens, FF), BF),
            sds((1, D), F32),
            sds((1, FF), F32),
        ],
        [
            whole((tokens, D)),
            whole((tokens, D)),
            shifted,
            whole((1, D)),
            pl.BlockSpec((1, D), lambda j: (0, jnp.maximum(j - 1, 0))),
        ],
        blocks.scratch,
        9.0,
        "mlp_back",
    )


def attend_back(grad_o, qkv, unit, inverse, gains):
    tokens = grad_o.shape[0]

    def kernel(do_ref, z_ref, u_ref, i_ref, c_ref, dz_ref, dc_ref):
        low = half_masks(PAD)
        valid = lax.broadcasted_iota(jnp.int32, (PAD, PAD), 0) < SEQ
        top = lax.broadcasted_iota(jnp.int32, (PAIR, PAD), 0) < HEAD_DIM
        mixer = head_mixer()

        @pl.when(pl.program_id(0) == 0)
        def _():
            dc_ref[...] = jnp.zeros_like(dc_ref)

        def norm_back(grad, which, columns):
            at = slice(which * D + columns.start, which * D + columns.stop)
            hats = u_ref[:, at].astype(F32)
            dc_ref[which, :, columns] += jnp.sum(grad * hats, axis=0, keepdims=True)
            pull = grad * c_ref[which, :, columns]
            dz_ref[:, at] = (
                i_ref[:, at] * (pull - head_mean(pull, mixer) - hats * head_mean(pull * hats, mixer))
            ).astype(BF)

        for tile in range(0, D, 768):
            grads_q, grads_k = [], []
            pairs = range(tile, tile + 768, PAIR)
            raw, pulled, keys_t = [], [], []
            for at in pairs:
                query, key, value = (z_ref[:, side + at : side + at + PAIR] for side in (0, D, 2 * D))
                grad = do_ref[:, at : at + PAIR]
                keys_t.append(key.T)
                for query_t, grad_t in zip(split_rows(query.T, top), split_rows(grad.T, top)):
                    raw.append(dot(key, query_t))
                    pulled.append(dot(value, grad_t))
            probs, scores = [], []
            for part, pull in zip(raw, pulled):
                raised = jnp.exp2(part * EXP2_SCALE)
                raised = jnp.where(valid, raised, 0.0)
                share = raised * (1.0 / jnp.sum(raised, axis=0, keepdims=True))
                mixed = share * pull
                row_dot = jnp.sum(mixed, axis=0, keepdims=True)
                probs.append(share.astype(BF))
                scores.append((mixed - share * row_dot).astype(BF))
            for n, at in enumerate(pairs):
                query, grad = z_ref[:, at : at + PAIR], do_ref[:, at : at + PAIR]
                both_v = dot(jnp.concatenate(probs[2 * n : 2 * n + 2], axis=0), grad)
                both_k = dot(jnp.concatenate(scores[2 * n : 2 * n + 2], axis=0), query)
                turned = [
                    dot(keys_t[n][h * HEAD_DIM : (h + 1) * HEAD_DIM], scores[2 * n + h]) for h in (0, 1)
                ]
                grads_q.append((jnp.concatenate(turned, axis=0) * SCALE).astype(BF).T.astype(F32))
                grads_k.append((jnp.where(low, both_k[:PAD], both_k[PAD:]) * SCALE).astype(BF).astype(F32))
                dz_ref[:, 2 * D + at : 2 * D + at + PAIR] = jnp.where(low, both_v[:PAD], both_v[PAD:]).astype(BF)
            for k in range(0, 768, TILE):
                n = k // PAIR
                norm_back(jnp.concatenate(grads_q[n : n + 2], axis=1), 0, slice(tile + k, tile + k + TILE))
                norm_back(jnp.concatenate(grads_k[n : n + 2], axis=1), 1, slice(tile + k, tile + k + TILE))

    def per_image(columns):
        return pl.BlockSpec((PAD, columns), lambda i: (i, 0))

    return call(
        kernel,
        (tokens // PAD,),
        [grad_o, qkv, unit, inverse, gains],
        [per_image(D), per_image(3 * D), per_image(2 * D), per_image(2 * D), whole((2, 1, D))],
        [sds((tokens, 3 * D), BF), sds((2, 1, D), F32)],
        [per_image(3 * D), whole((2, 1, D))],
        [],
        14.0,
        "attend_back",
    )


def weight_grads(segments, cut, name):
    total = sum(count for _, _, count in segments)
    operands, specs, start = [], [], 0
    for left, right, count in segments:
        for side in (left, right):
            side, first, last = (*side, count - 1) if isinstance(side, tuple) else (side, 0, 0)
            tokens = side.shape[0]
            index = functools.partial(
                lambda at, first, last, j: (0, first + jnp.clip(j - at, 0, last)), start, first, last
            )
            operands.append(side)
            specs.append(pl.BlockSpec((tokens, D), index))
        start += count

    def kernel(*refs):
        ins, outs = refs[: len(operands)], refs[len(operands) :]
        j = pl.program_id(0)
        slot = lax.rem(j, 2)

        def leave(block, slot):
            *mine, theirs, held, sems = outs
            rows = D // 8
            copies = []
            for way in WAYS:
                for core, target in enumerate((mine[way].at[block], theirs.at[way, block])):
                    row = pl.multiple_of(piece_row(way, core, rows), 16)
                    copies.append(
                        pltpu.make_async_copy(held.at[slot, pl.ds(row, rows)], target, sems.at[slot, core, way])
                    )
            return copies

        if cut:

            @pl.when(j >= 2)
            def _():
                for copy in leave(j - 2, slot):
                    copy.wait()

        start = 0
        for at, (_, _, count) in enumerate(segments):

            def body(at=at):
                value = dot(ins[2 * at][...], ins[2 * at + 1][...], TN).astype(BF)
                if cut:
                    outs[5][slot] = value
                else:
                    outs[0][0] = value

            if count == total:
                body()
            else:
                pl.when((j >= start) & (j < start + count))(body)
            start += count
        if cut:
            for copy in leave(j, slot):
                copy.start()

            @pl.when(j == total - 1)
            def _():
                if total > 1:
                    for copy in leave(j - 1, 1 - slot):
                        copy.wait()
                for copy in leave(j, slot):
                    copy.wait()

    if cut:
        shapes = [pltpu.HBM((total, D // 8, D), BF)] * 4 + [pltpu.HBM((4, total, D // 8, D), BF)]
        out_specs = [pl.BlockSpec(memory_space=pl.ANY)] * 5
    else:
        shapes = [sds((total, D, D), BF)]
        out_specs = [pl.BlockSpec((1, D, D), lambda j: (j, 0, 0))]
    return list(call(
        kernel,
        (total,),
        operands,
        specs,
        shapes,
        out_specs,
        [pltpu.VMEM((2, D, D), BF), pltpu.SemaphoreType.DMA((2, 2, 4))] if cut else [],
        1.0 + 1.4 * total,
        name,
    ))


def stream_back(grad, stream, gain, grad_u, grad_qkv, blocks):
    tokens = grad.shape[0]

    def kernel(g_ref, x_ref, c_ref, du_ref, dz_ref, *refs):
        w_refs, refs = refs[: len(blocks.arrays)], refs[len(blocks.arrays) :]
        out_ref, dg_ref, total, g_held, x_held, sems, *fetch = refs
        blocks.bind(w_refs, *fetch)
        j = pl.program_id(0)
        late = [
            pltpu.make_async_copy(g_ref, g_held, sems.at[0]),
            pltpu.make_async_copy(x_ref, x_held, sems.at[1]),
        ]
        block = blocks.step(j)

        @pl.when(j == 0)
        def _():
            for copy in late:
                copy.start()
            total[...] = dot(du_ref[...], block[...], NT)

        @pl.when((j > 0) & (j < RATIO))
        def _():
            total[...] += dot(du_ref[...], block[...], NT)

        @pl.when(j >= RATIO)
        def _():
            total[...] += dot(dz_ref[...], block[...], NT)

        @pl.when(j == IN_COUNT - 1)
        def _():
            for copy in late:
                copy.wait()
            sums = 0.0
            for row in range(0, tokens, PAD // 2):
                rows = slice(row, row + PAD // 2)
                unit, inverse = row_parts(x_held[rows, :].astype(F32))
                grad_h = total[rows, :]
                sums = sums + jnp.sum(grad_h * unit, axis=0, keepdims=True)
                hat = grad_h * c_ref[...]
                out_ref[rows, :] = g_held[rows, :].astype(F32) + inverse * (
                    hat
                    - jnp.mean(hat, axis=-1, keepdims=True)
                    - unit * jnp.mean(hat * unit, axis=-1, keepdims=True)
                )
            dg_ref[...] = sums

    return call(
        kernel,
        (IN_COUNT,),
        [grad, stream, gain, grad_u, grad_qkv] + blocks.arrays,
        [
            pl.BlockSpec(memory_space=pl.ANY),
            pl.BlockSpec(memory_space=pl.ANY),
            whole((1, D)),
            pl.BlockSpec((tokens, D), lambda j: (0, jnp.minimum(j, RATIO - 1))),
            pl.BlockSpec((tokens, D), lambda j: (0, jnp.maximum(j - RATIO, 0))),
        ]
        + blocks.specs,
        [sds((tokens, D), F32), sds((1, D), F32)],
        [whole((tokens, D)), whole((1, D))],
        [
            pltpu.VMEM((tokens, D), F32),
            pltpu.VMEM((tokens, D), grad.dtype),
            pltpu.VMEM((tokens, D), stream.dtype),
            pltpu.SemaphoreType.DMA((2,)),
        ]
        + blocks.scratch,
        12.0,
        "stream_back",
    )


def shampoo(grad, full, right, left_root, left_stats, right_stats, weights, ema, first, earlier):
    count, rows, _ = grad.shape

    def kernel(g_ref, lr_ref, ls_ref, rs_ref, w_ref, e_ref, *refs):
        f_refs, refs = refs[: len(full.arrays)], refs[len(full.arrays) :]
        r_refs, refs = refs[: len(right.arrays)], refs[len(right.arrays) + len(earlier) :]
        go_ref, lo_ref, ro_ref, wo_ref, eo_ref, f_held, f_sems, r_held, r_sems = refs
        full.bind(f_refs, f_held, f_sems)
        right.bind(r_refs, r_held, r_sems)
        j = pl.program_id(0)
        at = lax.axis_index("dp") * rows
        block = full.step(j)[...]
        right_block = right.step(j)[...]
        go_ref[0] = g_ref[0]
        gram = dot(g_ref[0].astype(BF), block, NT)
        lo_ref[0] = STAT_DECAY * ls_ref[0] + (1.0 - STAT_DECAY) * gram
        pick = (
            lax.broadcasted_iota(jnp.int32, (rows, D), 1)
            == lax.broadcasted_iota(jnp.int32, (rows, D), 0) + at
        )
        columns = dot(jnp.where(pick, 1.0, 0.0).astype(BF), block, NT).astype(BF)
        ro_ref[0] = STAT_DECAY * rs_ref[0] + (1.0 - STAT_DECAY) * dot(columns, block)
        lifted = dot(lr_ref[0].astype(BF), block).astype(BF)
        precond = dot(lifted, right_block)
        renewed = w_ref[0] * (1.0 - RATE_MAT * DECAY_MAT) - RATE_MAT * precond
        wo_ref[0] = renewed
        eo_ref[0] = EMA_DECAY * e_ref[0] + (1.0 - EMA_DECAY) * renewed

    part = pl.BlockSpec((1, rows, D), lambda j: (j, 0, 0))
    own = pl.BlockSpec((1, rows, D), lambda j: (first + j, 0, 0))
    inputs = [grad, left_root, left_stats, right_stats, weights, ema] + full.arrays + right.arrays
    return call(
        kernel,
        (count,),
        inputs + list(earlier),
        [part] + [own] * 5 + full.specs + right.specs + [pl.BlockSpec(memory_space=pl.ANY)] * len(earlier),
        [sds(weights.shape, F32)] * 5,
        [own] * 5,
        full.scratch + right.scratch,
        2.0 + 3.0 * count,
        "shampoo",
        {len(inputs) + at: at for at in range(len(earlier))},
    )


def split_vector(row_vec):
    ends = (D, D + HEAD_DIM, D + 2 * HEAD_DIM, D + 2 * HEAD_DIM + FF)
    ln_gain, q_gain, k_gain, mlp_bias, out_bias = jnp.split(row_vec, ends)
    return (
        ln_gain[None],
        jnp.stack([jnp.tile(q_gain, HEADS)[None], jnp.tile(k_gain, HEADS)[None]]),
        mlp_bias[None],
        out_bias[None],
    )


def pad_tokens(array):
    return jnp.pad(array, ((0, 0), (0, PAD - SEQ), (0, 0))).reshape(-1, D)


def cut_tokens(array):
    return array.reshape(-1, PAD, D)[:, :SEQ]


QKV, MLP, OUT = 0, 3, IN_COUNT
SIZES = {QKV: 3, MLP: RATIO, OUT: OUT_COUNT}


class Collectives:
    cut = False

    def __init__(self, weights, right_root):
        rows = lax.all_gather(weights.astype(BF), "head", axis=0, tiled=True)
        self.blocks = lax.all_gather(rows, "dp", axis=1, tiled=True)
        self.right = lax.all_gather(right_root.astype(BF), "dp", axis=1, tiled=True)
        self.count = weights.shape[0]
        self.parts = {}

    def group(self, *runs):
        return Blocks(
            [
                [(None, [(self.blocks, depth * PER_LAYER + first + at)])]
                for depth, first, count in runs
                for at in range(count)
            ]
        )

    def next(self, array):
        return array

    def done(self, name, array):
        return array

    def add_grads(self, depth, first, pieces):
        self.parts[depth, first] = pieces[0]

    def finish(self, renew):
        partial = jnp.concatenate([self.parts[key] for key in sorted(self.parts)], axis=0)
        rows = lax.psum_scatter(partial, "dp", scatter_dimension=1, tiled=True)
        own = lax.psum_scatter(rows, "head", scatter_dimension=0, tiled=True)
        full = lax.all_gather(own, "dp", axis=1, tiled=True)
        full, right = (
            Blocks([[(None, [(array, at)])] for at in range(self.count)]) for array in (full, self.right)
        )
        return renew(own.astype(F32), full, right, 0, ())

    def vector_sum(self, vectors):
        return lambda: lax.psum(vectors, ("dp", "head"))


DP, LINE = 8, 4
HALF = 3
STEPS = {"core": (1, 1), "x": (2, 2), "y": (4, 4), "first": (2, 4), "second": (4, 2)}
ROUNDS = ((2, 0, 0, 0), (1, 2, 1, 1), (3, 3, 3, 2))


def swap(array, axis):
    return lax.ppermute(array, "dp", [(i, i ^ STEPS[axis][i % 2]) for i in range(DP)])


def hop(array, *pairs):
    return lax.ppermute(array, "head", pairs)


def along(axis):
    return functools.partial(swap, axis=axis)


def over(*pairs):
    return lambda array: hop(array, *pairs)


class PlaneGather:
    def __init__(self, own):
        self.own = own

    def steps(self):
        own = self.own
        first, second, core = along("first"), along("second"), along("core")
        one, two = yield [(own, first), (own, second)]
        three, *others = yield [(one, second), (own, core), (one, core)]
        more = yield [(two, core), (three, core)]
        self.chips = [own, one, two, three]
        self.others = others + more
        self.chips, self.others = (
            [pltpu.with_memory_space_constraint(array, pltpu.HBM) for array in arrays]
            for arrays in (self.chips, self.others)
        )
        yield []

    def pieces(self, at):
        return [(chip, at) for chip in self.chips + self.others]


STEPS_AFTER = {
    "qkv0": [["place4", "line1", "place3"]],
    "attend0": [["place3", "place4", "place5"], ["place3", "place5"], ["place3", "place6"]],
    "mlp0": [["place5", "place6", "place7"], ["place5"]],
    "project0": [["place6", "place7"], ["place6"]],
    "qkv1": [["place7", "right0"]],
    "attend1": [["place7"]],
    "mlp1": [["right0", "right1"]],
    "project1": [["out1", "right0", "right1"]],
    "mlp_back1": [["right0", "right1"]],
    "grad_mlp1": [["out1", "right1"]],
    "attend_back1": [["out1", "mlp1"]],
    "stream_back1": [["out1", "mlp1", "qkv1"]],
    "mlp_back0": [["mlp1"]],
    "grad_out0": [["out1", "mlp1", "qkv1"]],
    "grad_mlp0": [["out0", "qkv1"]],
    "attend_back0": [["mlp1", "qkv1"]],
    "grad_qkv0": [["out0", "mlp0", "qkv1"]],
    "stream_back0": [["out0", "qkv0"]],
}
FIRST_STEPS = [
    ["line0", "line1"],
    ["place0", "place1"],
    ["place0"],
    ["place1"],
    ["place0", "place1", "line0", "place2"],
    ["place0", "place1", "place2", "place4"],
    ["place2"],
    ["place2", "place4"],
]
LAST_STEPS = [
    ["mlp0"],
    ["qkv0", "sums"],
    ["mlp0", "sums"],
    ["qkv0", "out0", "sums"],
    ["mlp0"],
    ["qkv0"],
    ["out0", "mlp0", "full3"],
    ["qkv0", "full0"],
    ["full3", "sums"],
    ["full3", "full0", "sums"],
    ["full3", "full0", "sums"],
    ["full0"],
]


class Permutes:
    cut = True

    def __init__(self, weights, right_root):
        self.parts, self.chains, self.asked, self.sent = {}, {}, {}, {}
        own = weights.astype(BF)
        right_root = right_root.astype(BF)
        self.plan = [PlaneGather(own[:HALF]), PlaneGather(own[HALF:])] + [PlaneGather(None) for _ in range(6)]
        self.right = [PlaneGather(right_root[:HALF]), PlaneGather(right_root[HALF:])]
        for at, part in enumerate(self.plan):
            self.chains[f"place{at}"] = part.steps()
        for side in (0, 1):
            self.chains[f"line{side}"] = self.gather_line(side)
            self.chains[f"right{side}"] = self.right[side].steps()
        for group in FIRST_STEPS:
            self.step(group)

    def gather_line(self, side):
        (halves,) = yield [(self.plan[side].own, lambda array: lax.all_gather(array, "head"))]
        head = lax.axis_index("head")
        for at in (0, 1, 2):
            owner = functools.reduce(
                lambda value, z: jnp.where(head == z, ROUNDS[at][z], value), range(1, LINE), ROUNDS[at][0]
            )
            self.plan[2 + 2 * at + side].own = lax.dynamic_index_in_dim(halves, owner, 0, keepdims=False)
        yield []

    def send(self, array=None):
        names = [name for name in self.asked if name not in self.sent]
        asked = [entry for name in names for entry in self.asked[name]]
        operands = [operand for operand, _ in asked]
        if array is not None and operands:
            array, *operands = lax.optimization_barrier((array, *operands))
        for name in names:
            self.sent[name] = [how(operands.pop(0)) for _, how in self.asked[name]]
        return array

    def step(self, group, event=None):
        if any(name in self.asked and name not in self.sent for name in group):
            self.send()
        arrived = [array for name in group for array in self.sent.get(name, [])]
        if arrived:
            event, *arrived = (
                lax.optimization_barrier((event, *arrived))
                if event is not None
                else (None, *lax.optimization_barrier(tuple(arrived)))
            )
        for name in group:
            chain = self.chains[name]
            if name in self.sent:
                self.asked[name] = chain.send([arrived.pop(0) for _ in self.sent.pop(name)])
            else:
                self.asked[name] = next(chain)
        return event

    def done(self, name, array):
        for group in STEPS_AFTER.get(name, ()):
            array = self.step(group, array)
        return array

    def next(self, array):
        return self.send(array)

    def place(self, owner, side, head):
        if head == owner:
            return side
        return next(2 + 2 * at + side for at in (0, 1, 2) if ROUNDS[at][head] == owner)

    def group(self, *runs):
        steps = []
        for depth, first, count in runs:
            for block in range(first, first + count):
                owner, at = 2 * depth + block // (2 * HALF), block % (2 * HALF)
                side, at = at // HALF, at % HALF
                places = [self.place(owner, side, head) for head in range(LINE)]
                steps.append(
                    [
                        (
                            [head for head in range(LINE) if places[head] == place],
                            self.plan[place].pieces(at),
                        )
                        for place in sorted(set(places))
                    ]
                )
        return Blocks(steps)

    def add_grads(self, depth, first, pieces):
        name = {QKV: "qkv", MLP: "mlp"}.get(first, "out") + str(depth)
        self.chains[name] = self.reduce(depth, first, pieces[:4], pieces[4])
        self.step([name])

    def reduce(self, depth, first_block, mine, theirs):
        count = mine[0].shape[0]
        first, second = along("first"), along("second")
        (core,) = yield [(theirs, along("core"))]
        far, to_two = ((mine[way].astype(F32) + core[way].astype(F32)).astype(BF) for way in (3, 2))
        far, two = yield [(far, second), (to_two, second)]
        to_one = (mine[1].astype(F32) + core[1].astype(F32) + far.astype(F32)).astype(BF)
        (one,) = yield [(to_one, first)]
        total = mine[0].astype(F32) + core[0].astype(F32) + one.astype(F32) + two.astype(F32)
        total = total.astype(BF)
        split = min(max(2 * HALF - first_block, 0), count)
        runs = [(side, low, high) for side, low, high in ((0, 0, split), (1, split, count)) if low < high]
        parts = [total[low:high] for _, low, high in runs]
        outer, inner, far_in, far_out = (0, 1, 2, 3) if depth == 0 else (3, 2, 1, 0)
        owners = [2 * depth + side for side, _, _ in runs]
        arrived = yield [
            (part, over((far_out, far_in), (outer if owner == inner else inner, owner)))
            for part, owner in zip(parts, owners)
        ]
        parts = [(part.astype(F32) + other.astype(F32)).astype(BF) for part, other in zip(parts, arrived)]
        arrived = yield [(part, over((far_in, owner))) for part, owner in zip(parts, owners)]
        for (_, low, high), part, other in zip(runs, parts, arrived):
            part = part.astype(F32) + other.astype(F32)
            for at in range(low, high):
                self.parts[depth, first_block + at] = (part, at - low)
        yield []

    def own_blocks(self, low, high):
        head = lax.axis_index("head")
        own = None
        for owner in range(LINE):
            runs = []
            for at in range(low, high):
                part, block = self.parts[owner // 2, 2 * HALF * (owner % 2) + at]
                if runs and runs[-1][0] is part:
                    runs[-1][2] = block + 1
                else:
                    runs.append([part, block, block + 1])
            values = [part[start:stop] for part, start, stop in runs]
            value = values[0] if len(values) == 1 else jnp.concatenate(values, axis=0)
            own = value if own is None else jnp.where(head == owner, value, own)
        return own

    def finish(self, renew):
        self.full = {}
        for low in (HALF, 0):
            self.chains[f"full{low}"] = self.gather_own(low)
        for group in LAST_STEPS:
            self.step(group)
        results = ()
        for low in (HALF, 0):
            own, full = self.full[low]
            results = renew(
                own,
                Blocks([[(None, full.pieces(at))] for at in range(HALF)]),
                Blocks([[(None, self.right[low // HALF].pieces(at))] for at in range(HALF)]),
                low,
                results,
            )
        return results

    def gather_own(self, low):
        own = self.own_blocks(low, low + HALF)
        full = PlaneGather(own.astype(BF))
        self.full[low] = own, full
        yield from full.steps()

    def vector_sum(self, vectors):
        self.chains["sums"] = self.sum_vectors(vectors)
        return lambda: self.summed

    def sum_vectors(self, vectors):
        for axis in ("core", "x", "y"):
            (other,) = yield [(vectors, along(axis))]
            vectors = vectors + other
        for step in (1, 2):
            (other,) = yield [(vectors, over(*((i, i ^ step) for i in range(LINE))))]
            vectors = vectors + other
        self.summed = vectors
        yield []


def on_device(
    image_tokens,
    cotangent,
    weights,
    weights_ema,
    left_stats,
    right_stats,
    left_root,
    right_root,
    vectors,
    vec_first,
    vec_second,
):
    fits = lax.axis_size("dp") == DP and lax.axis_size("head") == LINE
    links = (Permutes if fits else Collectives)(weights, right_root)
    stream = pad_tokens(image_tokens)
    grad = pad_tokens(cotangent)
    saved = []
    top = LAYERS - 1
    for depth in range(LAYERS):
        ln_gain, gains, mlp_bias, out_bias = split_vector(vectors[depth])
        normed, qkv, unit, inverse = qkv_in(
            links.next(stream), ln_gain, gains, links.group((depth, QKV, 3))
        )
        qkv = links.done(f"qkv{depth}", qkv)
        attended = attend(links.next(qkv))
        attended = links.done(f"attend{depth}", attended)
        hidden, slope = mlp_in(links.next(normed), mlp_bias, links.group((depth, MLP, RATIO)))
        hidden = links.done(f"mlp{depth}", hidden)
        saved.append((stream, normed, hidden, slope, qkv, unit, inverse, attended))
        if depth == top:
            pieces = weight_grads(
                [(links.next(attended), grad, 1), ((hidden, 0), grad, RATIO)], links.cut, "grad_out"
            )
            pieces[0] = links.done(f"grad_out{depth}", pieces[0])
            links.add_grads(depth, OUT, pieces)
        stream = project(
            links.next(stream), attended, hidden, out_bias, links.group((depth, OUT, OUT_COUNT)), depth == top
        )
        stream = links.done(f"project{depth}", stream)
    block_out = cut_tokens(stream)
    vector_parts = [None] * LAYERS
    for depth in reversed(range(LAYERS)):
        ln_gain, gains, _, _ = split_vector(vectors[depth])
        stream, normed, hidden, slope, qkv, unit, inverse, attended = saved[depth]
        dy, do, du, dbo, dbu = mlp_back(links.next(grad), slope, links.group((depth, OUT, OUT_COUNT)))
        dy = links.done(f"mlp_back{depth}", dy)
        share = RATIO if depth == top else RATIO - 1
        if depth < top:
            segments = [(normed, (du, share), RATIO - share), (links.next(attended), dy, 1), ((hidden, 0), dy, RATIO)]
            pieces = weight_grads(segments, links.cut, "grad_out")
            pieces[0] = links.done(f"grad_out{depth}", pieces[0])
            links.add_grads(depth, MLP + share, pieces)
        pieces = weight_grads([(links.next(normed), (du, 0), share)], links.cut, "grad_mlp")
        pieces[0] = links.done(f"grad_mlp{depth}", pieces[0])
        links.add_grads(depth, MLP, pieces)
        dqkv, dgains = attend_back(links.next(do), qkv, unit, inverse, gains)
        dqkv = links.done(f"attend_back{depth}", dqkv)
        pieces = weight_grads([(links.next(normed), (dqkv, 0), 3)], links.cut, "grad_qkv")
        pieces[0] = links.done(f"grad_qkv{depth}", pieces[0])
        links.add_grads(depth, QKV, pieces)
        grad, dg = stream_back(
            links.next(grad), stream, ln_gain, du, dqkv, links.group((depth, MLP, RATIO), (depth, QKV, 3))
        )
        grad = links.done(f"stream_back{depth}", grad)
        vector_parts[depth] = jnp.concatenate(
            [
                dg[0],
                dgains.reshape(2, HEADS, HEAD_DIM).sum(1).reshape(-1),
                dbu[0],
                dbo[0],
            ]
        )
    grad_stream = cut_tokens(grad)
    vector_sum = links.vector_sum(jnp.stack(vector_parts))

    def renew(own, full, right, first, earlier):
        return shampoo(
            own, full, right, left_root, left_stats, right_stats, weights, weights_ema, first, earlier
        )

    weight_grad, left_new, right_new, weight_new, ema_new = links.finish(renew)
    vector_grad = vector_sum()
    first_new = BETA_ONE * vec_first + (1.0 - BETA_ONE) * vector_grad
    second_new = BETA_TWO * vec_second + (1.0 - BETA_TWO) * vector_grad * vector_grad
    first_hat = first_new / (1.0 - BETA_ONE**STEP)
    second_hat = second_new / (1.0 - BETA_TWO**STEP)
    vec_new = vectors - RATE_VEC * first_hat / (jnp.sqrt(second_hat) + ADAM_EPS)
    return (
        block_out,
        grad_stream,
        weight_grad,
        left_new,
        right_new,
        weight_new,
        ema_new,
        first_new,
        second_new,
        vec_new,
    )


def solution(mesh):
    tokens, blocks = P(("dp", "head"), None, None), P("head", "dp", None)
    return jax.shard_map(
        on_device,
        mesh=mesh,
        in_specs=(tokens, tokens) + (blocks,) * 6 + (P(),) * 3,
        out_specs=(tokens, tokens) + (blocks,) * 5 + (P(),) * 3,
        check_vma=False,
    )
```

time: 706 us -> 538 us (0.76)
  Pallas kernels: 278 us -> 174 us
  waiting for transfers between devices: 231 us -> 181 us
  other arithmetic: 30.5 us -> 20.5 us
    pallas_call x19 -> x22, Pallas kernels: 278 us -> 174 us  [call(): pl.pallas_call(kernel, grid=grid, in_specs=in_specs, out_specs=out_specs,...]
    ppermute x118 -> x111, waiting for transfers between devices: 158 us -> 128 us  [swap(): lax.ppermute(array, 'dp', [(i, i ^ STEPS[axis][i % 2]) for i in range(DP)])]
    unnamed x236 -> x322, local copies, waits for them, and re-layouts: 7.58 us -> 30.2 us
    ppermute x16, waiting for transfers between devices: 56.7 us -> 41.8 us  [hop(): return lax.ppermute(array, 'head', pairs)]
    slice x34 -> x6, local copies, waits for them, and re-layouts: 9.36 us -> 0.98 us  [the longest x1 0.87 us: __init__(): own[HALF:]]
    ppermute x118 -> x111, starting transfers between devices: 82.8 us -> 74.4 us  [swap(): lax.ppermute(array, 'dp', [(i, i ^ STEPS[axis][i % 2]) for i in range(DP)])]
    all_gather x3 -> x2, waiting for transfers between devices: 15.8 us -> 10.6 us  [gather_line(): lax.all_gather(array, 'head')]
    convert_element_type x19 -> x20, other arithmetic: 16.3 us -> 12 us  [the longest x6 4.68 us: reduce(): (mine[1].astype(F32) + core[1].astype(F32) + far.astype(F32)).astype(BF)]
  transfers between devices with their start and end apart: 137 -> 129, of which waited for: 38 -> 39; matrix products, arithmetic and copies ran while one was open for 8% -> 4% of each run, Pallas kernels for 30% -> 29%
where the time goes in v3:
time: 538 us; the launch traced here: 533 us
  waiting for transfers between devices  181 us (34%)
  Pallas kernels  174 us (32%)
  starting transfers between devices  102 us (19%)
  local copies, waits for them, and re-layouts  40.4 us (8%)
  other arithmetic  20.5 us (4%)
  between operations  16.7 us (3%)
    pallas_call x22, Pallas kernels, call(): pl.pallas_call(kernel, grid=grid, in_specs=in_specs, out_specs=out_specs,...  174 us
    ppermute x111, waiting for transfers between devices, swap(): lax.ppermute(array, 'dp', [(i, i ^ STEPS[axis][i % 2]) for i in range(DP)])  128 us
    ppermute x111, starting transfers between devices, swap(): lax.ppermute(array, 'dp', [(i, i ^ STEPS[axis][i % 2]) for i in range(DP)])  74.4 us
    ppermute x16, waiting for transfers between devices, hop(): return lax.ppermute(array, 'head', pairs)  41.8 us
    unnamed x322, local copies, waits for them, and re-layouts  30.2 us
    ppermute x16, starting transfers between devices, hop(): return lax.ppermute(array, 'head', pairs)  27 us
  transfers between devices with their start and end apart: 129, of which 39 were waited for; matrix products, arithmetic and copies ran while one was open for 4% of the time, Pallas kernels for 29%

profile of v3, /device:TPU:0, one launch (start us, length us, event | category | flops | bytes accessed | tf_op | source)
XLA Modules:
  0.0 533.4 jit_solution(220863990174260719)
XLA Ops:
  14.9 8.7 %collective-permute-done.refs_1_.refs_17_.refs_33_ = bf16[3,96,768]{2,1,0:T(8,128)(2,1)S(1)} collective-permute-done((bf16[3,96,768]{2,1,0:T(8,128)(2,1)}, bf16[3,96,768]{2,1,0:T(8,128)(2,1)S(1)}, u32[]{:S(2)}, u32[]{:S(2)}) %collective-permute-start) | collective-permute-done | bytes 442400 | tf_op jit(solution)/shard_map/ppermute | solution.py:760
  27.6 5.3 collective-permute-done.6.refs_1_.refs_17_
  42.2 10.6 %all-gather.5.cloned.1.call-done = bf16[12,96,768]{2,1,0:T(8,128)(2,1)} async-done(((bf16[3,96,768]{2,1,0:T(8,128)(2,1)}), bf16[12,96,768]{2,1,0:T(8,128)(2,1)}) %all-gather.5.cloned.1.call-update) | async-done | bytes 1769488 | tf_op jit(solution)/shard_map/all_gather | solution.py:861
  58.5 9.9 %collective-permute-done.14.refs_9_.refs_49_.refs_33_ = bf16[3,96,768]{2,1,0:T(8,128)(2,1)} collective-permute-done((bf16[3,96,768]{2,1,0:T(8,128)(2,1)S(1)}, bf16[3,96,768]{2,1,0:T(8,128)(2,1)}, u32[]{:S(2)}, u32[]{:S(2)}) %collective-permute-start.14) | collective-permute-done | bytes 442400 | tf_op jit(solution)/shard_map/ppermute | solution.py:760
  72.4 8.7 %collective-permute-done.17.refs_11_.refs_51_.refs_35_ = bf16[3,96,768]{2,1,0:T(8,128)(2,1)} collective-permute-done((bf16[3,96,768]{2,1,0:T(8,128)(2,1)}, bf16[3,96,768]{2,1,0:T(8,128)(2,1)}, u32[]{:S(2)}, u32[]{:S(2)}) %collective-permute-start.17) | collective-permute-done | bytes 442400 | tf_op jit(solution)/shard_map/ppermute | solution.py:760
  88.2 8.2 %qkv_in.2 = (bf16[624,768]{1,0:T(8,128)(2,1)S(1)}, bf16[624,2304]{1,0:T(8,128)(2,1)S(1)}, bf16[624,1536]{1,0:T(8,128)(2,1)S(1)}, f32[624,1536]{1,0:T(8,128)S(1)}) custom-call(bf16[624,768]{1,0:T(8,128)(2,1)S(1)} %bitcast.101, f32[1,768]{1,0:T(1,128)S(1)} %get-tuple-element.616.g_ref.c_ref, f32[2,1,768]{2,1,0:T(1,128)S(1)} %constant_dynamic-update-slice_fusion.c_ref, ...), custom_call_target="tpu_custom_call" | custom-call | flops 9900000256 | bytes 17630208 | tf_op jit(solution)/shard_map/qkv_in/pallas_call | solution.py:53
  112.1 5.1 collective-permute-done.26.refs_9_
  121.3 8.9 %collective-permute-done.33.refs_25_.refs_17_ = bf16[3,96,768]{2,1,0:T(8,128)(2,1)S(1)} collective-permute-done((bf16[3,96,768]{2,1,0:T(8,128)(2,1)S(1)}, bf16[3,96,768]{2,1,0:T(8,128)(2,1)S(1)}, u32[]{:S(2)}, u32[]{:S(2)}) %collective-permute-start.33) | collective-permute-done | bytes 442400 | tf_op jit(solution)/shard_map/ppermute | solution.py:760
  138.5 10.0 %mlp_in.2 = (bf16[624,3072]{1,0:T(8,128)(2,1)S(1)}, bf16[624,3072]{1,0:T(8,128)(2,1)S(1)}) custom-call(bf16[624,768]{1,0:T(8,128)(2,1)S(1)} %get-tuple-element.495.h_ref.refs_0_, f32[1,3072]{1,0:T(1,128)S(1)} %get-tuple-element.618.b_ref, bf16[3,96,768]{2,1,0:T(8,128)(2,1)} %copy-done.37, bf16[3,96,768]{2,1,0:T(8,128)(2,1)} %copy-done.92, ...), custom_call_target="tpu_custom_call" | custom-call | flops 12099999744 | bytes 22794240 | tf_op jit(solution)/shard_map/mlp_in/pallas_call | solution.py:53
  160.8 8.0 %project.2.x_ref = f32[624,768]{1,0:T(8,128)S(1)} custom-call(bf16[624,768]{1,0:T(8,128)(2,1)S(1)} %bitcast.102, bf16[624,768]{1,0:T(8,128)(2,1)S(1)} %attend.2.o_ref.refs_2_, bf16[624,3072]{1,0:T(8,128)(2,1)S(1)} %copy-done.14, f32[1,768]{1,0:T(1,128)S(1)} %get-tuple-element.615.b_ref, bf16[3,96,768]{2,1,0:T(8,128)(2,1)} %get-tuple-element.612.refs_0_.refs_16_.refs_32_, ...), custom_call_target="tpu_custom_call" | custom-call | flops 8800000000 | bytes 21826560 | tf_op jit(solution)/shard_map/project/pallas_call | solution.py:53
  176.9 7.8 %qkv_in.3 = (bf16[624,768]{1,0:T(8,128)(2,1)S(1)}, bf16[624,2304]{1,0:T(8,128)(2,1)S(1)}, bf16[624,1536]{1,0:T(8,128)(2,1)S(1)}, f32[624,1536]{1,0:T(8,128)S(1)}) custom-call(f32[624,768]{1,0:T(8,128)S(1)} %project.2.x_ref, f32[1,768]{1,0:T(1,128)S(1)} %get-tuple-element.614.g_ref.c_ref, f32[2,1,768]{2,1,0:T(1,128)S(1)} %constant_dynamic-update-slice_fusion.2.c_ref, ...), custom_call_target="tpu_custom_call" | custom-call | flops 9900000256 | bytes 25666560 | tf_op jit(solution)/shard_map/qkv_in/pallas_call | solution.py:53
  191.6 10.6 %mlp_in.3 = (bf16[624,3072]{1,0:T(8,128)(2,1)S(1)}, bf16[624,3072]{1,0:T(8,128)(2,1)S(1)}) custom-call(bf16[624,768]{1,0:T(8,128)(2,1)S(1)} %get-tuple-element.437.h_ref.refs_0_, f32[1,3072]{1,0:T(1,128)S(1)} %get-tuple-element.617.b_ref, bf16[3,96,768]{2,1,0:T(8,128)(2,1)} %copy-done.37, bf16[3,96,768]{2,1,0:T(8,128)(2,1)} %copy-done.92, ...), custom_call_target="tpu_custom_call" | custom-call | flops 12099999744 | bytes 29872128 | tf_op jit(solution)/shard_map/mlp_in/pallas_call | solution.py:53
  202.2 7.6 %grad_out.2 = (bf16[5,96,768]{2,1,0:T(8,128)(2,1)}, bf16[5,96,768]{2,1,0:T(8,128)(2,1)}, bf16[5,96,768]{2,1,0:T(8,128)(2,1)}, bf16[5,96,768]{2,1,0:T(8,128)(2,1)}, bf16[4,5,96,768]{3,2,1,0:T(8,128)(2,1)}) custom-call(bf16[624,768]{1,0:T(8,128)(2,1)S(1)} %attend.3.refs_0_.o_ref, bf16[624,768]{1,0:T(8,128)(2,1)S(1)} %bitcast.104, ...), custom_call_target="tpu_custom_call" | custom-call | flops 8800000000 | bytes 12607488 | tf_op jit(solution)/shard_map/grad_out/pallas_call | solution.py:53
  212.5 10.0 %collective-permute-done.59.refs_11_ = bf16[3,96,768]{2,1,0:T(8,128)(2,1)S(1)} collective-permute-done((bf16[3,96,768]{2,1,0:T(8,128)(2,1)S(1)}, bf16[3,96,768]{2,1,0:T(8,128)(2,1)S(1)}, u32[]{:S(2)}, u32[]{:S(2)}) %collective-permute-start.59) | collective-permute-done | bytes 442400 | tf_op jit(solution)/shard_map/ppermute | solution.py:760
  223.4 8.1 %project.3 = bf16[624,768]{1,0:T(8,128)(2,1)S(1)} custom-call(f32[624,768]{1,0:T(8,128)S(1)} %project.2.x_ref, bf16[624,768]{1,0:T(8,128)(2,1)S(1)} %attend.3.refs_0_.o_ref, bf16[624,3072]{1,0:T(8,128)(2,1)S(1)} %get-tuple-element.389.refs_2_.a_ref, f32[1,768]{1,0:T(1,128)S(1)} %get-tuple-element.613.b_ref, ...), custom_call_target="tpu_custom_call" | custom-call | flops 8800000000 | bytes 21826560 | tf_op jit(solution)/shard_map/project/pallas_call | solution.py:53
  237.4 9.0 %mlp_back.2 = (bf16[624,768]{1,0:T(8,128)(2,1)}, bf16[624,768]{1,0:T(8,128)(2,1)S(1)}, bf16[624,3072]{1,0:T(8,128)(2,1)S(1)}, f32[1,768]{1,0:T(1,128)S(1)}, f32[1,3072]{1,0:T(1,128)S(1)}) custom-call(bf16[624,768]{1,0:T(8,128)(2,1)S(1)} %bitcast.106, bf16[624,3072]{1,0:T(8,128)(2,1)S(1)} %get-tuple-element.407.s_ref, ...), custom_call_target="tpu_custom_call" | custom-call | flops 9900000256 | bytes 24714240 | tf_op jit(solution)/shard_map/mlp_back/pallas_call | solution.py:53
  247.3 6.2 %grad_mlp.2 = (bf16[4,96,768]{2,1,0:T(8,128)(2,1)}, bf16[4,96,768]{2,1,0:T(8,128)(2,1)}, bf16[4,96,768]{2,1,0:T(8,128)(2,1)}, bf16[4,96,768]{2,1,0:T(8,128)(2,1)}, bf16[4,4,96,768]{3,2,1,0:T(8,128)(2,1)}) custom-call(bf16[624,768]{1,0:T(8,128)(2,1)S(1)} %get-tuple-element.437.h_ref.refs_0_, bf16[624,3072]{1,0:T(8,128)(2,1)S(1)} %get-tuple-element.418.refs_1_.du_ref), custom_call_target="tpu_custom_call" | custom-call | flops 7260000256 | bytes 9510912 | tf_op jit(solution)/shard_map/grad_mlp/pallas_call | solution.py:53
  259.7 8.6 %attend_back.2 = (bf16[624,2304]{1,0:T(8,128)(2,1)S(1)}, f32[2,1,768]{2,1,0:T(1,128)S(1)}) custom-call(bf16[624,768]{1,0:T(8,128)(2,1)S(1)} %get-tuple-element.426.do_ref, bf16[624,2304]{1,0:T(8,128)(2,1)S(1)} %get-tuple-element.375.z_ref, bf16[624,1536]{1,0:T(8,128)(2,1)S(1)} %get-tuple-element.427.u_ref, f32[624,1536]{1,0:T(8,128)S(1)} %get-tuple-element.428.i_ref, ...), custom_call_target="tpu_custom_call" | custom-call | flops 15399999488 | bytes 12472320 | tf_op jit(solution)/shard_map/attend_back/pallas_call | solution.py:53
  281.3 12.5 %stream_back.2 = (f32[624,768]{1,0:T(8,128)S(1)}, f32[1,768]{1,0:T(1,128)S(1)}) custom-call(bf16[624,768]{1,0:T(8,128)(2,1)S(1)} %bitcast.107, f32[624,768]{1,0:T(8,128)S(1)} %project.2.x_ref, f32[1,768]{1,0:T(1,128)S(1)} %get-tuple-element.614.g_ref.c_ref, bf16[624,3072]{1,0:T(8,128)(2,1)S(1)} %get-tuple-element.418.refs_1_.du_ref, ...), custom_call_target="tpu_custom_call" | custom-call | flops 13200000000 | bytes 39819264 | tf_op jit(solution)/shard_map/stream_back/pallas_call | solution.py:53
  300.7 8.0 %mlp_back.3 = (bf16[624,768]{1,0:T(8,128)(2,1)S(1)}, bf16[624,768]{1,0:T(8,128)(2,1)S(1)}, bf16[624,3072]{1,0:T(8,128)(2,1)S(1)}, f32[1,768]{1,0:T(1,128)S(1)}, f32[1,3072]{1,0:T(1,128)S(1)}) custom-call(f32[624,768]{1,0:T(8,128)S(1)} %get-tuple-element.507.g_ref, bf16[624,3072]{1,0:T(8,128)(2,1)S(1)} %copy-done.20, ...), custom_call_target="tpu_custom_call" | custom-call | flops 9900000256 | bytes 25672704 | tf_op jit(solution)/shard_map/mlp_back/pallas_call | solution.py:53
  317.7 9.4 %grad_out.3 = (bf16[6,96,768]{2,1,0:T(8,128)(2,1)}, bf16[6,96,768]{2,1,0:T(8,128)(2,1)}, bf16[6,96,768]{2,1,0:T(8,128)(2,1)}, bf16[6,96,768]{2,1,0:T(8,128)(2,1)}, bf16[4,6,96,768]{3,2,1,0:T(8,128)(2,1)}) custom-call(bf16[624,768]{1,0:T(8,128)(2,1)S(1)} %copy-done.26, bf16[624,3072]{1,0:T(8,128)(2,1)S(1)} %get-tuple-element.455.refs_1_.du_ref, ...), custom_call_target="tpu_custom_call" | custom-call | flops 10339999744 | bytes 18579456 | tf_op jit(solution)/shard_map/grad_out/pallas_call | solution.py:53
  338.9 6.3 %collective-permute-start.89 = (bf16[3,96,768]{2,1,0:T(8,128)(2,1)S(1)}, bf16[3,96,768]{2,1,0:T(8,128)(2,1)S(1)}, u32[]{:S(2)}, u32[]{:S(2)}) collective-permute-start(bf16[3,96,768]{2,1,0:T(8,128)(2,1)S(1)} %fusion.41), channel_id=1, source_target_pairs={{0,1},{3,2},{4,5},{7,6},{8,9},{11,10},{12,13},{15,14},{16,17},{19,... | collective-permute-start | bytes 1327112 | tf_op jit(solution)/shard_map/ppermute | solution.py:764
  347.4 8.4 %attend_back.3 = (bf16[624,2304]{1,0:T(8,128)(2,1)S(1)}, f32[2,1,768]{2,1,0:T(1,128)S(1)}) custom-call(bf16[624,768]{1,0:T(8,128)(2,1)S(1)} %get-tuple-element.487.do_ref, bf16[624,2304]{1,0:T(8,128)(2,1)S(1)} %copy-done.29, bf16[624,1536]{1,0:T(8,128)(2,1)S(1)} %copy-done.31, f32[624,1536]{1,0:T(8,128)S(1)} %copy-done.24, f32[2,1,768]{2,1,0:T(1,128)S(1)} %copy-done.8), custom_call_target="tpu_custom_call" | custom-call | flops 15399999488 | bytes 12472320 | tf_op jit(solution)/shard_map/attend_back/pallas_call | solution.py:53
  357.7 5.1 grad_qkv.3
  380.1 12.0 %stream_back.3 = (f32[624,768]{1,0:T(8,128)S(1)}, f32[1,768]{1,0:T(1,128)S(1)}) custom-call(f32[624,768]{1,0:T(8,128)S(1)} %copy-done.16, bf16[624,768]{1,0:T(8,128)(2,1)S(1)} %bitcast.103, f32[1,768]{1,0:T(1,128)S(1)} %copy-done.6, bf16[624,3072]{1,0:T(8,128)(2,1)S(1)} %copy-done.18, bf16[624,2304]{1,0:T(8,128)(2,1)S(1)} %copy-done.22, ...), custom_call_target="tpu_custom_call" | custom-call | flops 13200000000 | bytes 29202432 | tf_op jit(solution)/shard_map/stream_back/pallas_call | solution.py:53
  401.6 5.8 %collective-permute-done.102 = bf16[3,96,768]{2,1,0:T(8,128)(2,1)S(1)} collective-permute-done((bf16[3,96,768]{2,1,0:T(8,128)(2,1)S(1)}, bf16[3,96,768]{2,1,0:T(8,128)(2,1)S(1)}, u32[]{:S(2)}, u32[]{:S(2)}) %collective-permute-start.102) | collective-permute-done | bytes 442400 | tf_op jit(solution)/shard_map/ppermute | solution.py:760
  424.0 5.9 %collective-permute-done.99 = bf16[6,96,768]{2,1,0:T(8,128)(2,1)S(1)} collective-permute-done((bf16[6,96,768]{2,1,0:T(8,128)(2,1)S(1)}, bf16[6,96,768]{2,1,0:T(8,128)(2,1)S(1)}, u32[]{:S(2)}, u32[]{:S(2)}) %collective-permute-start.99) | collective-permute-done | bytes 884768 | tf_op jit(solution)/shard_map/ppermute | solution.py:764
  435.1 7.7 %collective-permute-done.108 = bf16[3,96,768]{2,1,0:T(8,128)(2,1)S(1)} collective-permute-done((bf16[3,96,768]{2,1,0:T(8,128)(2,1)S(1)}, bf16[3,96,768]{2,1,0:T(8,128)(2,1)S(1)}, u32[]{:S(2)}, u32[]{:S(2)}) %collective-permute-start.108) | collective-permute-done | bytes 442400 | tf_op jit(solution)/shard_map/ppermute | solution.py:764
  444.6 21.1 %collective-permute-done.107 = bf16[3,96,768]{2,1,0:T(8,128)(2,1)S(1)} collective-permute-done((bf16[3,96,768]{2,1,0:T(8,128)(2,1)S(1)}, bf16[3,96,768]{2,1,0:T(8,128)(2,1)S(1)}, u32[]{:S(2)}, u32[]{:S(2)}) %collective-permute-start.107) | collective-permute-done | bytes 442400 | tf_op jit(solution)/shard_map/ppermute | solution.py:764
  475.4 9.1 %collective-permute-done.112 = f32[2,4736]{1,0:T(2,128)S(1)} collective-permute-done((f32[2,4736]{1,0:T(2,128)S(1)}, f32[2,4736]{1,0:T(2,128)S(1)}, u32[]{:S(2)}, u32[]{:S(2)}) %collective-permute-start.112) | collective-permute-done | bytes 37920 | tf_op jit(solution)/shard_map/ppermute | solution.py:760
  506.4 9.1 %shampoo.2 = (f32[6,96,768]{2,1,0:T(8,128)}, f32[6,96,768]{2,1,0:T(8,128)}, f32[6,96,768]{2,1,0:T(8,128)}, f32[6,96,768]{2,1,0:T(8,128)}, f32[6,96,768]{2,1,0:T(8,128)}) custom-call(f32[3,96,768]{2,1,0:T(8,128)S(1)} %get-tuple-element.586.g_ref, f32[6,96,768]{2,1,0:T(8,128)S(1)} %copy-done.9, f32[6,96,768]{2,1,0:T(8,128)S(1)} %copy-done.10, ...), custom_call_target="tpu_custom_call" | custom-call | flops 12099999744 | bytes 25657344 | tf_op jit(solution)/shard_map/shampoo/pallas_call | solution.py:53
  517.3 9.0 %shampoo.3 = (f32[6,96,768]{2,1,0:T(8,128)}, f32[6,96,768]{2,1,0:T(8,128)}, f32[6,96,768]{2,1,0:T(8,128)}, f32[6,96,768]{2,1,0:T(8,128)}, f32[6,96,768]{2,1,0:T(8,128)}) custom-call(f32[3,96,768]{2,1,0:T(8,128)S(1)} %get-tuple-element.596.g_ref, ...), custom_call_target="tpu_custom_call", output_to_operand_aliasing={{0}: (22, {}), {1}: (23, {}), {2}: (24, {}), {3}: (25, {}),... | custom-call | flops 12099999744 | bytes 34504704 | tf_op jit(solution)/shard_map/shampoo/pallas_call | solution.py:53
  (649 shorter events, 235.8 us)
Async XLA Ops:
  7.2 45.7 %all-gather.5.cloned.1.call-start = ((), (), s32[]{:S(2)}) async-start(), calls=%async_computation | async-start | bytes 2211840 | tf_op jit(solution)/shard_map/all_gather | solution.py:861
  9.7 92.0 %all-gather.7.cloned.1.call-start = ((), (), s32[]{:S(2)}) async-start(), calls=%async_computation.1 | async-start | bytes 2211840 | tf_op jit(solution)/shard_map/all_gather | solution.py:861
  14.3 18.6 %collective-permute-start.6 = (bf16[3,96,768]{2,1,0:T(8,128)(2,1)S(1)}, bf16[3,96,768]{2,1,0:T(8,128)(2,1)S(1)}, u32[]{:S(2)}, u32[]{:S(2)}) collective-permute-start(bf16[3,96,768]{2,1,0:T(8,128)(2,1)S(1)} %get-tuple-element.611.refs_0_.refs_16_), channel_id=1, source_target_pairs={{0,8},{4,20},{8,0},{12,28},{16,24},{20,4},{24,16},{28,12},{1,9},{5... | collective-permute-start | bytes 1327112 | tf_op jit(solution)/shard_map/ppermute | solution.py:760
  14.8 18.1 %collective-permute-start.7 = (bf16[3,96,768]{2,1,0:T(8,128)(2,1)S(1)}, bf16[3,96,768]{2,1,0:T(8,128)(2,1)S(1)}, u32[]{:S(2)}, u32[]{:S(2)}) collective-permute-start(bf16[3,96,768]{2,1,0:T(8,128)(2,1)S(1)} %get-tuple-element.611.refs_0_.refs_16_), channel_id=1, source_target_pairs={{0,16},{4,12},{8,24},{12,4},{16,0},{20,28},{24,8},{28,20},{1,17},{... | collective-permute-start | bytes 1327112 | tf_op jit(solution)/shard_map/ppermute | solution.py:760
  14.9 20.7 %collective-permute-start.4 = (bf16[3,96,768]{2,1,0:T(8,128)(2,1)}, bf16[3,96,768]{2,1,0:T(8,128)(2,1)S(1)}, u32[]{:S(2)}, u32[]{:S(2)}) collective-permute-start(bf16[3,96,768]{2,1,0:T(8,128)(2,1)} %get-tuple-element.612.refs_0_.refs_16_.refs_32_), channel_id=1, source_target_pairs={{0,4},{4,0},{8,12},{12,8},{16,20},{20,16},{24,28},{28,24},{1,5},{5... | collective-permute-start | bytes 1327112 | tf_op jit(solution)/shard_map/ppermute | solution.py:760
  37.1 19.9 %collective-permute-start.2 = (bf16[3,96,768]{2,1,0:T(8,128)(2,1)S(1)}, bf16[3,96,768]{2,1,0:T(8,128)(2,1)}, u32[]{:S(2)}, u32[]{:S(2)}) collective-permute-start(bf16[3,96,768]{2,1,0:T(8,128)(2,1)S(1)} %collective-permute-done.1.refs_2_.refs_18_.refs_34_), channel_id=1, source_target_pairs={{0,4},{4,0},{8,12},{12,8},{16,20},{20,16},{24,28},{28,24},{1,5},{5... | collective-permute-start | bytes 1327112 | tf_op jit(solution)/shard_map/ppermute | solution.py:760
  37.5 21.0 %collective-permute-start.12 = (bf16[3,96,768]{2,1,0:T(8,128)(2,1)S(1)}, bf16[3,96,768]{2,1,0:T(8,128)(2,1)}, u32[]{:S(2)}, u32[]{:S(2)}) collective-permute-start(bf16[3,96,768]{2,1,0:T(8,128)(2,1)S(1)} %collective-permute-done.7.refs_2_.refs_18_), channel_id=1, source_target_pairs={{0,4},{4,0},{8,12},{12,8},{16,20},{20,16},{24,28},{28,24},{1,5},{5... | collective-permute-start | bytes 1327112 | tf_op jit(solution)/shard_map/ppermute | solution.py:760
  134.0 18.2 %collective-permute-start.40 = (bf16[3,96,768]{2,1,0:T(8,128)(2,1)S(1)}, bf16[3,96,768]{2,1,0:T(8,128)(2,1)S(1)}, u32[]{:S(2)}, u32[]{:S(2)}) collective-permute-start(bf16[3,96,768]{2,1,0:T(8,128)(2,1)S(1)} %copy-done.65), channel_id=1, source_target_pairs={{0,8},{4,20},{8,0},{12,28},{16,24},{20,4},{24,16},{28,12},{1,9},{5... | collective-permute-start | bytes 1327112 | tf_op jit(solution)/shard_map/ppermute | solution.py:760
  209.9 21.8 %collective-permute-start.58 = (bf16[4,5,96,768]{3,2,1,0:T(8,128)(2,1)}, bf16[4,5,96,768]{3,2,1,0:T(8,128)(2,1)S(1)}, u32[]{:S(2)}, u32[]{:S(2)}) collective-permute-start(bf16[4,5,96,768]{3,2,1,0:T(8,128)(2,1)} %get-tuple-element.392), channel_id=1, source_target_pairs={{0,4},{4,0},{8,12},{12,8},{16,20},{20,16},{24,28},{28,24},{1,5},{5... | collective-permute-start | bytes 8847368 | tf_op jit(solution)/shard_map/ppermute | solution.py:760
  211.0 20.6 %collective-permute-start.60 = (bf16[3,96,768]{2,1,0:T(8,128)(2,1)S(1)}, bf16[3,96,768]{2,1,0:T(8,128)(2,1)S(1)}, u32[]{:S(2)}, u32[]{:S(2)}) collective-permute-start(bf16[3,96,768]{2,1,0:T(8,128)(2,1)S(1)} %get-tuple-element.394.refs_8_), channel_id=1, source_target_pairs={{0,4},{4,0},{8,12},{12,8},{16,20},{20,16},{24,28},{28,24},{1,5},{5... | collective-permute-start | bytes 1327112 | tf_op jit(solution)/shard_map/ppermute | solution.py:760
  211.1 20.5 %collective-permute-start.61 = (bf16[3,96,768]{2,1,0:T(8,128)(2,1)S(1)}, bf16[3,96,768]{2,1,0:T(8,128)(2,1)S(1)}, u32[]{:S(2)}, u32[]{:S(2)}) collective-permute-start(bf16[3,96,768]{2,1,0:T(8,128)(2,1)S(1)} %collective-permute-done.56.refs_9_), channel_id=1, source_target_pairs={{0,4},{4,0},{8,12},{12,8},{16,20},{20,16},{24,28},{28,24},{1,5},{5... | collective-permute-start | bytes 1327112 | tf_op jit(solution)/shard_map/ppermute | solution.py:760
  211.5 20.1 %collective-permute-start.62 = (bf16[3,96,768]{2,1,0:T(8,128)(2,1)S(1)}, bf16[3,96,768]{2,1,0:T(8,128)(2,1)S(1)}, u32[]{:S(2)}, u32[]{:S(2)}) collective-permute-start(bf16[3,96,768]{2,1,0:T(8,128)(2,1)S(1)} %get-tuple-element.414.refs_8_), channel_id=1, source_target_pairs={{0,8},{4,20},{8,0},{12,28},{16,24},{20,4},{24,16},{28,12},{1,9},{5... | collective-permute-start | bytes 1327112 | tf_op jit(solution)/shard_map/ppermute | solution.py:760
  235.4 18.1 %collective-permute-start.69 = (bf16[5,96,768]{2,1,0:T(8,128)(2,1)S(1)}, bf16[5,96,768]{2,1,0:T(8,128)(2,1)S(1)}, u32[]{:S(2)}, u32[]{:S(2)}) collective-permute-start(bf16[5,96,768]{2,1,0:T(8,128)(2,1)S(1)} %get-tuple-element.420), channel_id=1, source_target_pairs={{0,16},{4,12},{8,24},{12,4},{16,0},{20,28},{24,8},{28,20},{1,17},{... | collective-permute-start | bytes 2211848 | tf_op jit(solution)/shard_map/ppermute | solution.py:760
  236.3 21.5 %collective-permute-start.70 = (bf16[5,96,768]{2,1,0:T(8,128)(2,1)S(1)}, bf16[5,96,768]{2,1,0:T(8,128)(2,1)S(1)}, u32[]{:S(2)}, u32[]{:S(2)}) collective-permute-start(bf16[5,96,768]{2,1,0:T(8,128)(2,1)S(1)} %get-tuple-element.421), channel_id=1, source_target_pairs={{0,16},{4,12},{8,24},{12,4},{16,0},{20,28},{24,8},{28,20},{1,17},{... | collective-permute-start | bytes 2211848 | tf_op jit(solution)/shard_map/ppermute | solution.py:760
  276.7 18.7 %collective-permute-start.78 = (bf16[4,3,96,768]{3,2,1,0:T(8,128)(2,1)}, bf16[4,3,96,768]{3,2,1,0:T(8,128)(2,1)S(1)}, u32[]{:S(2)}, u32[]{:S(2)}) collective-permute-start(bf16[4,3,96,768]{3,2,1,0:T(8,128)(2,1)} %get-tuple-element.445), channel_id=1, source_target_pairs={{0,4},{4,0},{8,12},{12,8},{16,20},{20,16},{24,28},{28,24},{1,5},{5... | collective-permute-start | bytes 5308424 | tf_op jit(solution)/shard_map/ppermute | solution.py:760
  276.8 18.7 %collective-permute-start.75 = (bf16[5,96,768]{2,1,0:T(8,128)(2,1)S(1)}, bf16[5,96,768]{2,1,0:T(8,128)(2,1)S(1)}, u32[]{:S(2)}, u32[]{:S(2)}) collective-permute-start(bf16[5,96,768]{2,1,0:T(8,128)(2,1)S(1)} %fusion.13), channel_id=1, source_target_pairs={{0,1},{2,3},{4,5},{6,7},{8,9},{10,11},{12,13},{14,15},{16,17},{18,... | collective-permute-start | bytes 2211848 | tf_op jit(solution)/shard_map/ppermute | solution.py:764
  297.9 29.2 %collective-permute-start.80 = (bf16[5,96,768]{2,1,0:T(8,128)(2,1)S(1)}, bf16[5,96,768]{2,1,0:T(8,128)(2,1)S(1)}, u32[]{:S(2)}, u32[]{:S(2)}) collective-permute-start(bf16[5,96,768]{2,1,0:T(8,128)(2,1)S(1)} %add_convert_fusion.1), channel_id=1, source_target_pairs={{1,3},{5,7},{9,11},{13,15},{17,19},{21,23},{25,27},{29,31}} | collective-permute-start | bytes 2211848 | tf_op jit(solution)/shard_map/ppermute | solution.py:764
  298.6 28.4 %collective-permute-start.83 = (bf16[3,96,768]{2,1,0:T(8,128)(2,1)S(1)}, bf16[3,96,768]{2,1,0:T(8,128)(2,1)S(1)}, u32[]{:S(2)}, u32[]{:S(2)}) collective-permute-start(bf16[3,96,768]{2,1,0:T(8,128)(2,1)S(1)} %get-tuple-element.468), channel_id=1, source_target_pairs={{0,16},{4,12},{8,24},{12,4},{16,0},{20,28},{24,8},{28,20},{1,17},{... | collective-permute-start | bytes 1327112 | tf_op jit(solution)/shard_map/ppermute | solution.py:760
  299.6 27.5 %collective-permute-start.84 = (bf16[3,96,768]{2,1,0:T(8,128)(2,1)S(1)}, bf16[3,96,768]{2,1,0:T(8,128)(2,1)S(1)}, u32[]{:S(2)}, u32[]{:S(2)}) collective-permute-start(bf16[3,96,768]{2,1,0:T(8,128)(2,1)S(1)} %get-tuple-element.469), channel_id=1, source_target_pairs={{0,16},{4,12},{8,24},{12,4},{16,0},{20,28},{24,8},{28,20},{1,17},{... | collective-permute-start | bytes 1327112 | tf_op jit(solution)/shard_map/ppermute | solution.py:760
  330.5 25.4 %collective-permute-start.87 = (bf16[3,96,768]{2,1,0:T(8,128)(2,1)S(1)}, bf16[3,96,768]{2,1,0:T(8,128)(2,1)S(1)}, u32[]{:S(2)}, u32[]{:S(2)}) collective-permute-start(bf16[3,96,768]{2,1,0:T(8,128)(2,1)S(1)} %get-tuple-element.491), channel_id=1, source_target_pairs={{1,2},{5,6},{9,10},{13,14},{17,18},{21,22},{25,26},{29,30}} | collective-permute-start | bytes 1327112 | tf_op jit(solution)/shard_map/ppermute | solution.py:764
  338.9 17.0 %collective-permute-start.89 = (bf16[3,96,768]{2,1,0:T(8,128)(2,1)S(1)}, bf16[3,96,768]{2,1,0:T(8,128)(2,1)S(1)}, u32[]{:S(2)}, u32[]{:S(2)}) collective-permute-start(bf16[3,96,768]{2,1,0:T(8,128)(2,1)S(1)} %fusion.41), channel_id=1, source_target_pairs={{0,1},{3,2},{4,5},{7,6},{8,9},{11,10},{12,13},{15,14},{16,17},{19,... | collective-permute-start | bytes 1327112 | tf_op jit(solution)/shard_map/ppermute | solution.py:764
  345.3 17.5 %collective-permute-start.90 = (bf16[6,96,768]{2,1,0:T(8,128)(2,1)S(1)}, bf16[6,96,768]{2,1,0:T(8,128)(2,1)S(1)}, u32[]{:S(2)}, u32[]{:S(2)}) collective-permute-start(bf16[6,96,768]{2,1,0:T(8,128)(2,1)S(1)} %get-tuple-element.498), channel_id=1, source_target_pairs={{0,16},{4,12},{8,24},{12,4},{16,0},{20,28},{24,8},{28,20},{1,17},{... | collective-permute-start | bytes 2654216 | tf_op jit(solution)/shard_map/ppermute | solution.py:760
  346.1 21.8 %collective-permute-start.91 = (bf16[6,96,768]{2,1,0:T(8,128)(2,1)S(1)}, bf16[6,96,768]{2,1,0:T(8,128)(2,1)S(1)}, u32[]{:S(2)}, u32[]{:S(2)}) collective-permute-start(bf16[6,96,768]{2,1,0:T(8,128)(2,1)S(1)} %get-tuple-element.499), channel_id=1, source_target_pairs={{0,16},{4,12},{8,24},{12,4},{16,0},{20,28},{24,8},{28,20},{1,17},{... | collective-permute-start | bytes 2654216 | tf_op jit(solution)/shard_map/ppermute | solution.py:760
  347.4 20.5 %collective-permute-start.92 = (bf16[4,3,96,768]{3,2,1,0:T(8,128)(2,1)}, bf16[4,3,96,768]{3,2,1,0:T(8,128)(2,1)S(1)}, u32[]{:S(2)}, u32[]{:S(2)}) collective-permute-start(bf16[4,3,96,768]{3,2,1,0:T(8,128)(2,1)} %get-tuple-element.500), channel_id=1, source_target_pairs={{0,4},{4,0},{8,12},{12,8},{16,20},{20,16},{24,28},{28,24},{1,5},{5... | collective-permute-start | bytes 5308424 | tf_op jit(solution)/shard_map/ppermute | solution.py:760
  371.5 25.0 %collective-permute-start.95 = (bf16[4,3,96,768]{3,2,1,0:T(8,128)(2,1)}, bf16[4,3,96,768]{3,2,1,0:T(8,128)(2,1)}, u32[]{:S(2)}, u32[]{:S(2)}) collective-permute-start(bf16[4,3,96,768]{3,2,1,0:T(8,128)(2,1)} %get-tuple-element.510), channel_id=1, source_target_pairs={{0,4},{4,0},{8,12},{12,8},{16,20},{20,16},{24,28},{28,24},{1,5},{5... | collective-permute-start | bytes 5308424 | tf_op jit(solution)/shard_map/ppermute | solution.py:760
  372.0 24.5 %collective-permute-start.94 = (bf16[6,96,768]{2,1,0:T(8,128)(2,1)}, bf16[6,96,768]{2,1,0:T(8,128)(2,1)}, u32[]{:S(2)}, u32[]{:S(2)}) collective-permute-start(bf16[6,96,768]{2,1,0:T(8,128)(2,1)} %fusion.6), channel_id=1, source_target_pairs={{0,8},{4,20},{8,0},{12,28},{16,24},{20,4},{24,16},{28,12},{1,9},{5... | collective-permute-start | bytes 2654216 | tf_op jit(solution)/shard_map/ppermute | solution.py:760
  372.6 19.5 %collective-permute-start.100 = (bf16[3,96,768]{2,1,0:T(8,128)(2,1)}, bf16[3,96,768]{2,1,0:T(8,128)(2,1)}, u32[]{:S(2)}, u32[]{:S(2)}) collective-permute-start(bf16[3,96,768]{2,1,0:T(8,128)(2,1)} %get-tuple-element.532), channel_id=1, source_target_pairs={{0,16},{4,12},{8,24},{12,4},{16,0},{20,28},{24,8},{28,20},{1,17},{... | collective-permute-start | bytes 1327112 | tf_op jit(solution)/shard_map/ppermute | solution.py:760
  374.3 20.2 %collective-permute-start.101 = (bf16[3,96,768]{2,1,0:T(8,128)(2,1)}, bf16[3,96,768]{2,1,0:T(8,128)(2,1)}, u32[]{:S(2)}, u32[]{:S(2)}) collective-permute-start(bf16[3,96,768]{2,1,0:T(8,128)(2,1)} %get-tuple-element.533), channel_id=1, source_target_pairs={{0,16},{4,12},{8,24},{12,4},{16,0},{20,28},{24,8},{28,20},{1,17},{... | collective-permute-start | bytes 1327112 | tf_op jit(solution)/shard_map/ppermute | solution.py:760
  409.3 20.6 %collective-permute-start.99 = (bf16[6,96,768]{2,1,0:T(8,128)(2,1)S(1)}, bf16[6,96,768]{2,1,0:T(8,128)(2,1)S(1)}, u32[]{:S(2)}, u32[]{:S(2)}) collective-permute-start(bf16[6,96,768]{2,1,0:T(8,128)(2,1)S(1)} %fusion.2), channel_id=1, source_target_pairs={{3,2},{0,1},{7,6},{4,5},{11,10},{8,9},{15,14},{12,13},{19,18},{16,... | collective-permute-start | bytes 2654216 | tf_op jit(solution)/shard_map/ppermute | solution.py:764
  430.1 35.6 %collective-permute-start.105 = (bf16[6,96,768]{2,1,0:T(8,128)(2,1)S(1)}, bf16[6,96,768]{2,1,0:T(8,128)(2,1)S(1)}, u32[]{:S(2)}, u32[]{:S(2)}) collective-permute-start(bf16[6,96,768]{2,1,0:T(8,128)(2,1)S(1)} %add_convert_fusion), channel_id=1, source_target_pairs={{2,1},{6,5},{10,9},{14,13},{18,17},{22,21},{26,25},{30,29}} | collective-permute-start | bytes 2654216 | tf_op jit(solution)/shard_map/ppermute | solution.py:764
  433.7 32.0 %collective-permute-start.107 = (bf16[3,96,768]{2,1,0:T(8,128)(2,1)S(1)}, bf16[3,96,768]{2,1,0:T(8,128)(2,1)S(1)}, u32[]{:S(2)}, u32[]{:S(2)}) collective-permute-start(bf16[3,96,768]{2,1,0:T(8,128)(2,1)S(1)} %add_convert_fusion.3), channel_id=1, source_target_pairs={{2,0},{6,4},{10,8},{14,12},{18,16},{22,20},{26,24},{30,28}} | collective-permute-start | bytes 1327112 | tf_op jit(solution)/shard_map/ppermute | solution.py:764
  443.0 27.5 %collective-permute-start.109 = (bf16[3,96,768]{2,1,0:T(8,128)(2,1)S(1)}, bf16[3,96,768]{2,1,0:T(8,128)(2,1)S(1)}, u32[]{:S(2)}, u32[]{:S(2)}) collective-permute-start(bf16[3,96,768]{2,1,0:T(8,128)(2,1)S(1)} %add_convert_fusion.2), channel_id=1, source_target_pairs={{2,0},{6,4},{10,8},{14,12},{18,16},{22,20},{26,24},{30,28}} | collective-permute-start | bytes 1327112 | tf_op jit(solution)/shard_map/ppermute | solution.py:764
  (258 other events, 2981.7 us)
Sparse Core Ops, SparseCore 0:
  9.8 43.0 all-gather.4
  54.4 39.1 all-gather.6

commit v4 on v3

--- a/solution.py
+++ b/solution.py
@@ -671,7 +671,7 @@
     part = pl.BlockSpec((1, rows, D), lambda j: (j, 0, 0))
     own = pl.BlockSpec((1, rows, D), lambda j: (first + j, 0, 0))
     inputs = [grad, left_root, left_stats, right_stats, weights, ema] + full.arrays + right.arrays
-    return call(
+    return list(call(
         kernel,
         (count,),
         inputs + list(earlier),
@@ -682,7 +682,7 @@
         2.0 + 3.0 * count,
         "shampoo",
         {len(inputs) + at: at for at in range(len(earlier))},
-    )
+    ))
 
 
 def split_vector(row_vec):
@@ -795,48 +795,41 @@
 
 
 STEPS_AFTER = {
-    "qkv0": [["place4", "line1", "place3"]],
-    "attend0": [["place3", "place4", "place5"], ["place3", "place5"], ["place3", "place6"]],
+    "qkv0": [["place4", "line1", "place3", "place5"]],
+    "attend0": [["place3", "place4"], ["place3", "place5", "place6"], ["place3"]],
     "mlp0": [["place5", "place6", "place7"], ["place5"]],
     "project0": [["place6", "place7"], ["place6"]],
-    "qkv1": [["place7", "right0"]],
+    "qkv1": [["place7", "right0", "right1"]],
     "attend1": [["place7"]],
     "mlp1": [["right0", "right1"]],
     "project1": [["out1", "right0", "right1"]],
-    "mlp_back1": [["right0", "right1"]],
     "grad_mlp1": [["out1", "right1"]],
     "attend_back1": [["out1", "mlp1"]],
     "stream_back1": [["out1", "mlp1", "qkv1"]],
     "mlp_back0": [["mlp1"]],
     "grad_out0": [["out1", "mlp1", "qkv1"]],
     "grad_mlp0": [["out0", "qkv1"]],
-    "attend_back0": [["mlp1", "qkv1"]],
-    "grad_qkv0": [["out0", "mlp0", "qkv1"]],
-    "stream_back0": [["out0", "qkv0"]],
+    "attend_back0": [["mlp1", "qkv1", "mlp0"]],
+    "grad_qkv0": [["out0", "qkv1"], ["out0", "mlp0"]],
+    "stream_back0": [["out0", "mlp0", "qkv0"]],
 }
 FIRST_STEPS = [
     ["line0", "line1"],
     ["place0", "place1"],
     ["place0"],
     ["place1"],
-    ["place0", "place1", "line0", "place2"],
-    ["place0", "place1", "place2", "place4"],
+    ["place0", "place1", "line0", "place2", "place4"],
+    ["place0", "place1", "place2"],
+    ["place2", "place4", "right0"],
     ["place2"],
-    ["place2", "place4"],
 ]
 LAST_STEPS = [
-    ["mlp0"],
-    ["qkv0", "sums"],
-    ["mlp0", "sums"],
-    ["qkv0", "out0", "sums"],
-    ["mlp0"],
-    ["qkv0"],
-    ["out0", "mlp0", "full3"],
-    ["qkv0", "full0"],
-    ["full3", "sums"],
+    ["sums"],
+    ["out0", "mlp0", "qkv0", "sums"],
+    ["mlp0", "full3", "qkv0", "sums"],
+    ["full3", "qkv0", "sums"],
+    ["qkv0", "full3", "full0", "sums"],
     ["full3", "full0", "sums"],
-    ["full3", "full0", "sums"],
-    ["full0"],
 ]
 
 
@@ -983,8 +976,11 @@
         results = ()
         for low in (HALF, 0):
             own, full = self.full[low]
+            if low == 0:
+                results[0] = self.step(["full0"], results[0])
+                self.step(["full0"])
             results = renew(
-                own,
+                self.next(own),
                 Blocks([[(None, full.pieces(at))] for at in range(HALF)]),
                 Blocks([[(None, self.right[low // HALF].pieces(at))] for at in range(HALF)]),
                 low,

time: 538 us -> 521 us (0.968)
  waiting for transfers between devices: 181 us -> 165 us
    ppermute x16, waiting for transfers between devices: 41.8 us -> 29.3 us  [hop(): return lax.ppermute(array, 'head', pairs)]
    unnamed x322 -> x326, local copies, waits for them, and re-layouts: 30.2 us -> 28.7 us
  transfers between devices with their start and end apart: 129 -> 129, of which waited for: 39 -> 42; matrix products, arithmetic and copies ran while one was open for 4% -> 3% of each run, Pallas kernels for 29% -> 30%
where the time goes in v4:
time: 521 us; the launch traced here: 516 us
  Pallas kernels  174 us (33%)
  waiting for transfers between devices  165 us (32%)
  starting transfers between devices  106 us (20%)
  local copies, waits for them, and re-layouts  37.6 us (7%)
  other arithmetic  17.5 us (3%)
  between operations  16.5 us (3%)
    pallas_call x22, Pallas kernels, call(): pl.pallas_call(kernel, grid=grid, in_specs=in_specs, out_specs=out_specs,...  174 us
    ppermute x111, waiting for transfers between devices, swap(): lax.ppermute(array, 'dp', [(i, i ^ STEPS[axis][i % 2]) for i in range(DP)])  125 us
    ppermute x111, starting transfers between devices, swap(): lax.ppermute(array, 'dp', [(i, i ^ STEPS[axis][i % 2]) for i in range(DP)])  78.2 us
    ppermute x16, waiting for transfers between devices, hop(): return lax.ppermute(array, 'head', pairs)  29.3 us
    unnamed x326, local copies, waits for them, and re-layouts  28.7 us
    ppermute x16, starting transfers between devices, hop(): return lax.ppermute(array, 'head', pairs)  27.3 us
    all_gather x2, waiting for transfers between devices, gather_line(): lax.all_gather(array, 'head')  10.6 us
  transfers between devices with their start and end apart: 129, of which 42 were waited for; matrix products, arithmetic and copies ran while one was open for 3% of the time, Pallas kernels for 30%

profile of v4, /device:TPU:0, one launch (start us, length us, event | category | flops | bytes accessed | tf_op | source)
XLA Modules:
  0.0 515.9 jit_solution(7522917052553256303)
XLA Ops:
  14.8 8.7 %collective-permute-done.refs_1_.refs_17_.refs_33_ = bf16[3,96,768]{2,1,0:T(8,128)(2,1)S(1)} collective-permute-done((bf16[3,96,768]{2,1,0:T(8,128)(2,1)}, bf16[3,96,768]{2,1,0:T(8,128)(2,1)S(1)}, u32[]{:S(2)}, u32[]{:S(2)}) %collective-permute-start) | collective-permute-done | bytes 442400 | tf_op jit(solution)/shard_map/ppermute | solution.py:760
  27.5 5.3 %collective-permute-done.5.refs_1_.refs_17_ = bf16[3,96,768]{2,1,0:T(8,128)(2,1)S(1)} collective-permute-done((bf16[3,96,768]{2,1,0:T(8,128)(2,1)S(1)}, bf16[3,96,768]{2,1,0:T(8,128)(2,1)S(1)}, u32[]{:S(2)}, u32[]{:S(2)}) %collective-permute-start.5) | collective-permute-done | bytes 442400 | tf_op jit(solution)/shard_map/ppermute | solution.py:760
  42.2 10.6 %all-gather.5.cloned.1.call-done = bf16[12,96,768]{2,1,0:T(8,128)(2,1)} async-done(((bf16[3,96,768]{2,1,0:T(8,128)(2,1)}), bf16[12,96,768]{2,1,0:T(8,128)(2,1)}) %all-gather.5.cloned.1.call-update) | async-done | bytes 1769488 | tf_op jit(solution)/shard_map/all_gather | solution.py:854
  59.6 8.7 %collective-permute-done.14.refs_9_.refs_49_.refs_33_ = bf16[3,96,768]{2,1,0:T(8,128)(2,1)} collective-permute-done((bf16[3,96,768]{2,1,0:T(8,128)(2,1)S(1)}, bf16[3,96,768]{2,1,0:T(8,128)(2,1)}, u32[]{:S(2)}, u32[]{:S(2)}) %collective-permute-start.14) | collective-permute-done | bytes 442400 | tf_op jit(solution)/shard_map/ppermute | solution.py:760
  85.7 8.2 %qkv_in.2 = (bf16[624,768]{1,0:T(8,128)(2,1)S(1)}, bf16[624,2304]{1,0:T(8,128)(2,1)S(1)}, bf16[624,1536]{1,0:T(8,128)(2,1)S(1)}, f32[624,1536]{1,0:T(8,128)S(1)}) custom-call(bf16[624,768]{1,0:T(8,128)(2,1)S(1)} %bitcast.101, f32[1,768]{1,0:T(1,128)S(1)} %get-tuple-element.618.g_ref.c_ref, f32[2,1,768]{2,1,0:T(1,128)S(1)} %constant_dynamic-update-slice_fusion.c_ref, ...), custom_call_target="tpu_custom_call" | custom-call | flops 9900000256 | bytes 17630208 | tf_op jit(solution)/shard_map/qkv_in/pallas_call | solution.py:53
  108.8 5.4 %collective-permute-done.26.refs_9_ = bf16[3,96,768]{2,1,0:T(8,128)(2,1)S(1)} collective-permute-done((bf16[3,96,768]{2,1,0:T(8,128)(2,1)S(1)}, bf16[3,96,768]{2,1,0:T(8,128)(2,1)S(1)}, u32[]{:S(2)}, u32[]{:S(2)}) %collective-permute-start.26) | collective-permute-done | bytes 442400 | tf_op jit(solution)/shard_map/ppermute | solution.py:760
  118.1 9.2 %collective-permute-done.33.refs_25_.refs_17_ = bf16[3,96,768]{2,1,0:T(8,128)(2,1)S(1)} collective-permute-done((bf16[3,96,768]{2,1,0:T(8,128)(2,1)S(1)}, bf16[3,96,768]{2,1,0:T(8,128)(2,1)S(1)}, u32[]{:S(2)}, u32[]{:S(2)}) %collective-permute-start.33) | collective-permute-done | bytes 442400 | tf_op jit(solution)/shard_map/ppermute | solution.py:760
  135.0 10.1 %mlp_in.2 = (bf16[624,3072]{1,0:T(8,128)(2,1)S(1)}, bf16[624,3072]{1,0:T(8,128)(2,1)S(1)}) custom-call(bf16[624,768]{1,0:T(8,128)(2,1)S(1)} %get-tuple-element.493.h_ref.refs_0_, f32[1,3072]{1,0:T(1,128)S(1)} %get-tuple-element.620.b_ref, bf16[3,96,768]{2,1,0:T(8,128)(2,1)} %copy-done.36, bf16[3,96,768]{2,1,0:T(8,128)(2,1)} %copy-done.97, ...), custom_call_target="tpu_custom_call" | custom-call | flops 12099999744 | bytes 22794240 | tf_op jit(solution)/shard_map/mlp_in/pallas_call | solution.py:53
  152.8 8.0 %project.2.x_ref = f32[624,768]{1,0:T(8,128)S(1)} custom-call(bf16[624,768]{1,0:T(8,128)(2,1)S(1)} %bitcast.102, bf16[624,768]{1,0:T(8,128)(2,1)S(1)} %attend.2.o_ref.refs_2_, bf16[624,3072]{1,0:T(8,128)(2,1)S(1)} %get-tuple-element.353.a_ref.refs_4_, f32[1,768]{1,0:T(1,128)S(1)} %get-tuple-element.617.b_ref, ...), custom_call_target="tpu_custom_call" | custom-call | flops 8800000000 | bytes 21826560 | tf_op jit(solution)/shard_map/project/pallas_call | solution.py:53
  171.9 8.0 %qkv_in.3 = (bf16[624,768]{1,0:T(8,128)(2,1)S(1)}, bf16[624,2304]{1,0:T(8,128)(2,1)S(1)}, bf16[624,1536]{1,0:T(8,128)(2,1)S(1)}, f32[624,1536]{1,0:T(8,128)S(1)}) custom-call(f32[624,768]{1,0:T(8,128)S(1)} %project.2.x_ref, f32[1,768]{1,0:T(1,128)S(1)} %get-tuple-element.616.g_ref.c_ref, f32[2,1,768]{2,1,0:T(1,128)S(1)} %constant_dynamic-update-slice_fusion.2.c_ref, ...), custom_call_target="tpu_custom_call" | custom-call | flops 9900000256 | bytes 25666560 | tf_op jit(solution)/shard_map/qkv_in/pallas_call | solution.py:53
  191.8 10.6 %mlp_in.3 = (bf16[624,3072]{1,0:T(8,128)(2,1)S(1)}, bf16[624,3072]{1,0:T(8,128)(2,1)S(1)}) custom-call(bf16[624,768]{1,0:T(8,128)(2,1)S(1)} %get-tuple-element.431.h_ref.refs_0_, f32[1,3072]{1,0:T(1,128)S(1)} %get-tuple-element.619.b_ref, bf16[3,96,768]{2,1,0:T(8,128)(2,1)} %copy-done.36, bf16[3,96,768]{2,1,0:T(8,128)(2,1)} %copy-done.97, ...), custom_call_target="tpu_custom_call" | custom-call | flops 12099999744 | bytes 29872128 | tf_op jit(solution)/shard_map/mlp_in/pallas_call | solution.py:53
  202.9 7.6 %grad_out.2 = (bf16[5,96,768]{2,1,0:T(8,128)(2,1)}, bf16[5,96,768]{2,1,0:T(8,128)(2,1)}, bf16[5,96,768]{2,1,0:T(8,128)(2,1)}, bf16[5,96,768]{2,1,0:T(8,128)(2,1)}, bf16[4,5,96,768]{3,2,1,0:T(8,128)(2,1)}) custom-call(bf16[624,768]{1,0:T(8,128)(2,1)S(1)} %attend.3.refs_0_.o_ref, bf16[624,768]{1,0:T(8,128)(2,1)S(1)} %bitcast.104, ...), custom_call_target="tpu_custom_call" | custom-call | flops 8800000000 | bytes 12607488 | tf_op jit(solution)/shard_map/grad_out/pallas_call | solution.py:53
  217.5 7.9 %project.3 = bf16[624,768]{1,0:T(8,128)(2,1)S(1)} custom-call(f32[624,768]{1,0:T(8,128)S(1)} %project.2.x_ref, bf16[624,768]{1,0:T(8,128)(2,1)S(1)} %attend.3.refs_0_.o_ref, bf16[624,3072]{1,0:T(8,128)(2,1)S(1)} %get-tuple-element.392.refs_2_.a_ref, f32[1,768]{1,0:T(1,128)S(1)} %get-tuple-element.615.b_ref, ...), custom_call_target="tpu_custom_call" | custom-call | flops 8800000000 | bytes 21826560 | tf_op jit(solution)/shard_map/project/pallas_call | solution.py:53
  229.7 9.0 %mlp_back.2 = (bf16[624,768]{1,0:T(8,128)(2,1)}, bf16[624,768]{1,0:T(8,128)(2,1)S(1)}, bf16[624,3072]{1,0:T(8,128)(2,1)S(1)}, f32[1,768]{1,0:T(1,128)S(1)}, f32[1,3072]{1,0:T(1,128)S(1)}) custom-call(bf16[624,768]{1,0:T(8,128)(2,1)S(1)} %bitcast.106, bf16[624,3072]{1,0:T(8,128)(2,1)S(1)} %get-tuple-element.409.s_ref, ...), custom_call_target="tpu_custom_call" | custom-call | flops 9900000256 | bytes 24714240 | tf_op jit(solution)/shard_map/mlp_back/pallas_call | solution.py:53
  238.7 6.2 %grad_mlp.2 = (bf16[4,96,768]{2,1,0:T(8,128)(2,1)}, bf16[4,96,768]{2,1,0:T(8,128)(2,1)}, bf16[4,96,768]{2,1,0:T(8,128)(2,1)}, bf16[4,96,768]{2,1,0:T(8,128)(2,1)}, bf16[4,4,96,768]{3,2,1,0:T(8,128)(2,1)}) custom-call(bf16[624,768]{1,0:T(8,128)(2,1)S(1)} %get-tuple-element.431.h_ref.refs_0_, bf16[624,3072]{1,0:T(8,128)(2,1)S(1)} %get-tuple-element.412.refs_1_.du_ref), custom_call_target="tpu_custom_call" | custom-call | flops 7260000256 | bytes 9510912 | tf_op jit(solution)/shard_map/grad_mlp/pallas_call | solution.py:53
  248.2 8.4 %attend_back.2 = (bf16[624,2304]{1,0:T(8,128)(2,1)S(1)}, f32[2,1,768]{2,1,0:T(1,128)S(1)}) custom-call(bf16[624,768]{1,0:T(8,128)(2,1)S(1)} %get-tuple-element.420.do_ref, bf16[624,2304]{1,0:T(8,128)(2,1)S(1)} %get-tuple-element.373.z_ref, bf16[624,1536]{1,0:T(8,128)(2,1)S(1)} %get-tuple-element.421.u_ref, f32[624,1536]{1,0:T(8,128)S(1)} %get-tuple-element.422.i_ref, ...), custom_call_target="tpu_custom_call" | custom-call | flops 15399999488 | bytes 12472320 | tf_op jit(solution)/shard_map/attend_back/pallas_call | solution.py:53
  269.4 12.5 %stream_back.2 = (f32[624,768]{1,0:T(8,128)S(1)}, f32[1,768]{1,0:T(1,128)S(1)}) custom-call(bf16[624,768]{1,0:T(8,128)(2,1)S(1)} %bitcast.107, f32[624,768]{1,0:T(8,128)S(1)} %project.2.x_ref, f32[1,768]{1,0:T(1,128)S(1)} %get-tuple-element.616.g_ref.c_ref, bf16[624,3072]{1,0:T(8,128)(2,1)S(1)} %get-tuple-element.412.refs_1_.du_ref, ...), custom_call_target="tpu_custom_call" | custom-call | flops 13200000000 | bytes 39819264 | tf_op jit(solution)/shard_map/stream_back/pallas_call | solution.py:53
  289.3 8.4 %mlp_back.3 = (bf16[624,768]{1,0:T(8,128)(2,1)S(1)}, bf16[624,768]{1,0:T(8,128)(2,1)S(1)}, bf16[624,3072]{1,0:T(8,128)(2,1)S(1)}, f32[1,768]{1,0:T(1,128)S(1)}, f32[1,3072]{1,0:T(1,128)S(1)}) custom-call(f32[624,768]{1,0:T(8,128)S(1)} %get-tuple-element.509.g_ref, bf16[624,3072]{1,0:T(8,128)(2,1)S(1)} %copy-done.20, ...), custom_call_target="tpu_custom_call" | custom-call | flops 9900000256 | bytes 25672704 | tf_op jit(solution)/shard_map/mlp_back/pallas_call | solution.py:53
  307.0 9.4 %grad_out.3 = (bf16[6,96,768]{2,1,0:T(8,128)(2,1)}, bf16[6,96,768]{2,1,0:T(8,128)(2,1)}, bf16[6,96,768]{2,1,0:T(8,128)(2,1)}, bf16[6,96,768]{2,1,0:T(8,128)(2,1)}, bf16[4,6,96,768]{3,2,1,0:T(8,128)(2,1)}) custom-call(bf16[624,768]{1,0:T(8,128)(2,1)S(1)} %copy-done.28, bf16[624,3072]{1,0:T(8,128)(2,1)S(1)} %get-tuple-element.449.refs_1_.du_ref, ...), custom_call_target="tpu_custom_call" | custom-call | flops 10339999744 | bytes 18579456 | tf_op jit(solution)/shard_map/grad_out/pallas_call | solution.py:53
  330.0 6.7 %collective-permute-start.89 = (bf16[3,96,768]{2,1,0:T(8,128)(2,1)S(1)}, bf16[3,96,768]{2,1,0:T(8,128)(2,1)S(1)}, u32[]{:S(2)}, u32[]{:S(2)}) collective-permute-start(bf16[3,96,768]{2,1,0:T(8,128)(2,1)S(1)} %fusion.41), channel_id=1, source_target_pairs={{0,1},{3,2},{4,5},{7,6},{8,9},{11,10},{12,13},{15,14},{16,17},{19,... | collective-permute-start | bytes 1327112 | tf_op jit(solution)/shard_map/ppermute | solution.py:764
  337.7 8.5 %attend_back.3 = (bf16[624,2304]{1,0:T(8,128)(2,1)S(1)}, f32[2,1,768]{2,1,0:T(1,128)S(1)}) custom-call(bf16[624,768]{1,0:T(8,128)(2,1)S(1)} %get-tuple-element.481.do_ref, bf16[624,2304]{1,0:T(8,128)(2,1)S(1)} %copy-done.31, bf16[624,1536]{1,0:T(8,128)(2,1)S(1)} %copy-done.33, f32[624,1536]{1,0:T(8,128)S(1)} %copy-done.26, f32[2,1,768]{2,1,0:T(1,128)S(1)} %copy-done.8), custom_call_target="tpu_custom_call" | custom-call | flops 15399999488 | bytes 12472320 | tf_op jit(solution)/shard_map/attend_back/pallas_call | solution.py:53
  363.9 11.1 %collective-permute-done.95 = bf16[3,96,768]{2,1,0:T(8,128)(2,1)S(1)} collective-permute-done((bf16[3,96,768]{2,1,0:T(8,128)(2,1)S(1)}, bf16[3,96,768]{2,1,0:T(8,128)(2,1)S(1)}, u32[]{:S(2)}, u32[]{:S(2)}) %collective-permute-start.95) | collective-permute-done | bytes 442400 | tf_op jit(solution)/shard_map/ppermute | solution.py:760
  375.0 6.0 %collective-permute-done.96 = bf16[3,96,768]{2,1,0:T(8,128)(2,1)S(1)} collective-permute-done((bf16[3,96,768]{2,1,0:T(8,128)(2,1)S(1)}, bf16[3,96,768]{2,1,0:T(8,128)(2,1)S(1)}, u32[]{:S(2)}, u32[]{:S(2)}) %collective-permute-start.96) | collective-permute-done | bytes 442400 | tf_op jit(solution)/shard_map/ppermute | solution.py:760
  394.2 12.2 %stream_back.3 = (f32[624,768]{1,0:T(8,128)S(1)}, f32[1,768]{1,0:T(1,128)S(1)}) custom-call(f32[624,768]{1,0:T(8,128)S(1)} %copy-done.16, bf16[624,768]{1,0:T(8,128)(2,1)S(1)} %bitcast.103, f32[1,768]{1,0:T(1,128)S(1)} %copy-done.6, bf16[624,3072]{1,0:T(8,128)(2,1)S(1)} %copy-done.18, bf16[624,2304]{1,0:T(8,128)(2,1)S(1)} %copy-done.22, ...), custom_call_target="tpu_custom_call" | custom-call | flops 13200000000 | bytes 29202432 | tf_op jit(solution)/shard_map/stream_back/pallas_call | solution.py:53
  416.8 8.1 %collective-permute-done.101 = bf16[3,96,768]{2,1,0:T(8,128)(2,1)S(1)} collective-permute-done((bf16[3,96,768]{2,1,0:T(8,128)(2,1)S(1)}, bf16[3,96,768]{2,1,0:T(8,128)(2,1)S(1)}, u32[]{:S(2)}, u32[]{:S(2)}) %collective-permute-start.101) | collective-permute-done | bytes 442400 | tf_op jit(solution)/shard_map/ppermute | solution.py:764
  431.5 6.4 %collective-permute-done.107 = f32[2,4736]{1,0:T(2,128)S(1)} collective-permute-done((f32[2,4736]{1,0:T(2,128)S(1)}, f32[2,4736]{1,0:T(2,128)S(1)}, u32[]{:S(2)}, u32[]{:S(2)}) %collective-permute-start.107) | collective-permute-done | bytes 37920 | tf_op jit(solution)/shard_map/ppermute | solution.py:760
  437.9 5.8 %collective-permute-done.105 = bf16[3,96,768]{2,1,0:T(8,128)(2,1)S(1)} collective-permute-done((bf16[3,96,768]{2,1,0:T(8,128)(2,1)S(1)}, bf16[3,96,768]{2,1,0:T(8,128)(2,1)S(1)}, u32[]{:S(2)}, u32[]{:S(2)}) %collective-permute-start.105) | collective-permute-done | bytes 442400 | tf_op jit(solution)/shard_map/ppermute | solution.py:764
  450.3 5.0 collective-permute-done.111
  462.9 9.2 %collective-permute-done.116 = f32[2,4736]{1,0:T(2,128)S(1)} collective-permute-done((f32[2,4736]{1,0:T(2,128)S(1)}, f32[2,4736]{1,0:T(2,128)S(1)}, u32[]{:S(2)}, u32[]{:S(2)}) %collective-permute-start.116) | collective-permute-done | bytes 37920 | tf_op jit(solution)/shard_map/ppermute | solution.py:764
  479.9 6.1 %collective-permute-done.119.refs_1_ = bf16[3,96,768]{2,1,0:T(8,128)(2,1)S(1)} collective-permute-done((bf16[3,96,768]{2,1,0:T(8,128)(2,1)S(1)}, bf16[3,96,768]{2,1,0:T(8,128)(2,1)S(1)}, u32[]{:S(2)}, u32[]{:S(2)}) %collective-permute-start.119) | collective-permute-done | bytes 442400 | tf_op jit(solution)/shard_map/ppermute | solution.py:760
  487.7 9.3 %shampoo.2 = (f32[6,96,768]{2,1,0:T(8,128)}, f32[6,96,768]{2,1,0:T(8,128)}, f32[6,96,768]{2,1,0:T(8,128)}, f32[6,96,768]{2,1,0:T(8,128)}, f32[6,96,768]{2,1,0:T(8,128)}) custom-call(f32[3,96,768]{2,1,0:T(8,128)S(1)} %get-tuple-element.553.g_ref, f32[6,96,768]{2,1,0:T(8,128)S(1)} %copy-done.9, f32[6,96,768]{2,1,0:T(8,128)S(1)} %copy-done.10, ...), custom_call_target="tpu_custom_call" | custom-call | flops 12099999744 | bytes 25657344 | tf_op jit(solution)/shard_map/shampoo/pallas_call | solution.py:53
  499.9 9.0 %shampoo.3 = (f32[6,96,768]{2,1,0:T(8,128)}, f32[6,96,768]{2,1,0:T(8,128)}, f32[6,96,768]{2,1,0:T(8,128)}, f32[6,96,768]{2,1,0:T(8,128)}, f32[6,96,768]{2,1,0:T(8,128)}) custom-call(f32[3,96,768]{2,1,0:T(8,128)S(1)} %get-tuple-element.590.g_ref, ...), custom_call_target="tpu_custom_call", output_to_operand_aliasing={{0}: (22, {}), {1}: (23, {}), {2}: (24, {}), {3}: (25, {}),... | custom-call | flops 12099999744 | bytes 34504704 | tf_op jit(solution)/shard_map/shampoo/pallas_call | solution.py:53
  (653 shorter events, 233.8 us)
Async XLA Ops:
  7.2 45.6 %all-gather.5.cloned.1.call-start = ((), (), s32[]{:S(2)}) async-start(), calls=%async_computation | async-start | bytes 2211840 | tf_op jit(solution)/shard_map/all_gather | solution.py:854
  9.6 89.7 %all-gather.7.cloned.1.call-start = ((), (), s32[]{:S(2)}) async-start(), calls=%async_computation.1 | async-start | bytes 2211840 | tf_op jit(solution)/shard_map/all_gather | solution.py:854
  14.2 18.6 %collective-permute-start.5 = (bf16[3,96,768]{2,1,0:T(8,128)(2,1)S(1)}, bf16[3,96,768]{2,1,0:T(8,128)(2,1)S(1)}, u32[]{:S(2)}, u32[]{:S(2)}) collective-permute-start(bf16[3,96,768]{2,1,0:T(8,128)(2,1)S(1)} %get-tuple-element.613.refs_0_.refs_16_), channel_id=1, source_target_pairs={{0,8},{4,20},{8,0},{12,28},{16,24},{20,4},{24,16},{28,12},{1,9},{5... | collective-permute-start | bytes 1327112 | tf_op jit(solution)/shard_map/ppermute | solution.py:760
  14.8 18.1 %collective-permute-start.6 = (bf16[3,96,768]{2,1,0:T(8,128)(2,1)S(1)}, bf16[3,96,768]{2,1,0:T(8,128)(2,1)S(1)}, u32[]{:S(2)}, u32[]{:S(2)}) collective-permute-start(bf16[3,96,768]{2,1,0:T(8,128)(2,1)S(1)} %get-tuple-element.613.refs_0_.refs_16_), channel_id=1, source_target_pairs={{0,16},{4,12},{8,24},{12,4},{16,0},{20,28},{24,8},{28,20},{1,17},{... | collective-permute-start | bytes 1327112 | tf_op jit(solution)/shard_map/ppermute | solution.py:760
  14.8 20.7 %collective-permute-start.3 = (bf16[3,96,768]{2,1,0:T(8,128)(2,1)}, bf16[3,96,768]{2,1,0:T(8,128)(2,1)S(1)}, u32[]{:S(2)}, u32[]{:S(2)}) collective-permute-start(bf16[3,96,768]{2,1,0:T(8,128)(2,1)} %get-tuple-element.614.refs_0_.refs_16_.refs_32_), channel_id=1, source_target_pairs={{0,4},{4,0},{8,12},{12,8},{16,20},{20,16},{24,28},{28,24},{1,5},{5... | collective-permute-start | bytes 1327112 | tf_op jit(solution)/shard_map/ppermute | solution.py:760
  37.1 19.9 %collective-permute-start.10 = (bf16[3,96,768]{2,1,0:T(8,128)(2,1)S(1)}, bf16[3,96,768]{2,1,0:T(8,128)(2,1)}, u32[]{:S(2)}, u32[]{:S(2)}) collective-permute-start(bf16[3,96,768]{2,1,0:T(8,128)(2,1)S(1)} %collective-permute-done.1.refs_2_.refs_18_.refs_34_), channel_id=1, source_target_pairs={{0,4},{4,0},{8,12},{12,8},{16,20},{20,16},{24,28},{28,24},{1,5},{5... | collective-permute-start | bytes 1327112 | tf_op jit(solution)/shard_map/ppermute | solution.py:760
  37.4 21.0 %collective-permute-start.12 = (bf16[3,96,768]{2,1,0:T(8,128)(2,1)S(1)}, bf16[3,96,768]{2,1,0:T(8,128)(2,1)S(1)}, u32[]{:S(2)}, u32[]{:S(2)}) collective-permute-start(bf16[3,96,768]{2,1,0:T(8,128)(2,1)S(1)} %collective-permute-done.6.refs_2_.refs_18_), channel_id=1, source_target_pairs={{0,4},{4,0},{8,12},{12,8},{16,20},{20,16},{24,28},{28,24},{1,5},{5... | collective-permute-start | bytes 1327112 | tf_op jit(solution)/shard_map/ppermute | solution.py:760
  58.4 19.4 %collective-permute-start.19 = (bf16[3,96,768]{2,1,0:T(8,128)(2,1)S(1)}, bf16[3,96,768]{2,1,0:T(8,128)(2,1)}, u32[]{:S(2)}, u32[]{:S(2)}) collective-permute-start(bf16[3,96,768]{2,1,0:T(8,128)(2,1)S(1)} %get-tuple-element.609.refs_24_.refs_8_.refs_16_.refs_56_), channel_id=1, source_target_pairs={{0,8},{4,20},{8,0},{12,28},{16,24},{20,4},{24,16},{28,12},{1,9},{5... | collective-permute-start | bytes 1327112 | tf_op jit(solution)/shard_map/ppermute | solution.py:760
  59.1 18.7 %collective-permute-start.20 = (bf16[3,96,768]{2,1,0:T(8,128)(2,1)S(1)}, bf16[3,96,768]{2,1,0:T(8,128)(2,1)}, u32[]{:S(2)}, u32[]{:S(2)}) collective-permute-start(bf16[3,96,768]{2,1,0:T(8,128)(2,1)S(1)} %get-tuple-element.609.refs_24_.refs_8_.refs_16_.refs_56_), channel_id=1, source_target_pairs={{0,16},{4,12},{8,24},{12,4},{16,0},{20,28},{24,8},{28,20},{1,17},{... | collective-permute-start | bytes 1327112 | tf_op jit(solution)/shard_map/ppermute | solution.py:760
  83.0 16.3 %collective-permute-start.24 = (bf16[3,96,768]{2,1,0:T(8,128)(2,1)S(1)}, bf16[3,96,768]{2,1,0:T(8,128)(2,1)}, u32[]{:S(2)}, u32[]{:S(2)}) collective-permute-start(bf16[3,96,768]{2,1,0:T(8,128)(2,1)S(1)} %get-tuple-element.609.refs_24_.refs_8_.refs_16_.refs_56_), channel_id=1, source_target_pairs={{0,4},{4,0},{8,12},{12,8},{16,20},{20,16},{24,28},{28,24},{1,5},{5... | collective-permute-start | bytes 1327112 | tf_op jit(solution)/shard_map/ppermute | solution.py:760
  101.1 16.5 %collective-permute-start.31 = (bf16[3,96,768]{2,1,0:T(8,128)(2,1)S(1)}, bf16[3,96,768]{2,1,0:T(8,128)(2,1)S(1)}, u32[]{:S(2)}, u32[]{:S(2)}) collective-permute-start(bf16[3,96,768]{2,1,0:T(8,128)(2,1)S(1)} %get-tuple-element.324.refs_8_), channel_id=1, source_target_pairs={{0,4},{4,0},{8,12},{12,8},{16,20},{20,16},{24,28},{28,24},{1,5},{5... | collective-permute-start | bytes 1327112 | tf_op jit(solution)/shard_map/ppermute | solution.py:760
  184.9 17.6 %collective-permute-start.58 = (bf16[3,96,768]{2,1,0:T(8,128)(2,1)}, bf16[3,96,768]{2,1,0:T(8,128)(2,1)S(1)}, u32[]{:S(2)}, u32[]{:S(2)}) collective-permute-start(bf16[3,96,768]{2,1,0:T(8,128)(2,1)} %collective-permute-done.54.refs_9_), channel_id=1, source_target_pairs={{0,16},{4,12},{8,24},{12,4},{16,0},{20,28},{24,8},{28,20},{1,17},{... | collective-permute-start | bytes 1327112 | tf_op jit(solution)/shard_map/ppermute | solution.py:760
  185.9 16.6 %collective-permute-start.59 = (bf16[3,96,768]{2,1,0:T(8,128)(2,1)S(1)}, bf16[3,96,768]{2,1,0:T(8,128)(2,1)S(1)}, u32[]{:S(2)}, u32[]{:S(2)}) collective-permute-start(bf16[3,96,768]{2,1,0:T(8,128)(2,1)S(1)} %get-tuple-element.385.refs_8_), channel_id=1, source_target_pairs={{0,4},{4,0},{8,12},{12,8},{16,20},{20,16},{24,28},{28,24},{1,5},{5... | collective-permute-start | bytes 1327112 | tf_op jit(solution)/shard_map/ppermute | solution.py:760
  227.1 17.8 %collective-permute-start.69 = (bf16[5,96,768]{2,1,0:T(8,128)(2,1)S(1)}, bf16[5,96,768]{2,1,0:T(8,128)(2,1)S(1)}, u32[]{:S(2)}, u32[]{:S(2)}) collective-permute-start(bf16[5,96,768]{2,1,0:T(8,128)(2,1)S(1)} %get-tuple-element.414), channel_id=1, source_target_pairs={{0,16},{4,12},{8,24},{12,4},{16,0},{20,28},{24,8},{28,20},{1,17},{... | collective-permute-start | bytes 2211848 | tf_op jit(solution)/shard_map/ppermute | solution.py:760
  228.1 18.4 %collective-permute-start.70 = (bf16[5,96,768]{2,1,0:T(8,128)(2,1)S(1)}, bf16[5,96,768]{2,1,0:T(8,128)(2,1)S(1)}, u32[]{:S(2)}, u32[]{:S(2)}) collective-permute-start(bf16[5,96,768]{2,1,0:T(8,128)(2,1)S(1)} %get-tuple-element.415), channel_id=1, source_target_pairs={{0,16},{4,12},{8,24},{12,4},{16,0},{20,28},{24,8},{28,20},{1,17},{... | collective-permute-start | bytes 2211848 | tf_op jit(solution)/shard_map/ppermute | solution.py:760
  264.9 18.7 %collective-permute-start.78 = (bf16[4,3,96,768]{3,2,1,0:T(8,128)(2,1)}, bf16[4,3,96,768]{3,2,1,0:T(8,128)(2,1)S(1)}, u32[]{:S(2)}, u32[]{:S(2)}) collective-permute-start(bf16[4,3,96,768]{3,2,1,0:T(8,128)(2,1)} %get-tuple-element.439), channel_id=1, source_target_pairs={{0,4},{4,0},{8,12},{12,8},{16,20},{20,16},{24,28},{28,24},{1,5},{5... | collective-permute-start | bytes 5308424 | tf_op jit(solution)/shard_map/ppermute | solution.py:760
  265.0 18.6 %collective-permute-start.75 = (bf16[5,96,768]{2,1,0:T(8,128)(2,1)S(1)}, bf16[5,96,768]{2,1,0:T(8,128)(2,1)S(1)}, u32[]{:S(2)}, u32[]{:S(2)}) collective-permute-start(bf16[5,96,768]{2,1,0:T(8,128)(2,1)S(1)} %fusion.13), channel_id=1, source_target_pairs={{0,1},{2,3},{4,5},{6,7},{8,9},{10,11},{12,13},{14,15},{16,17},{18,... | collective-permute-start | bytes 2211848 | tf_op jit(solution)/shard_map/ppermute | solution.py:764
  286.5 29.9 %collective-permute-start.80 = (bf16[5,96,768]{2,1,0:T(8,128)(2,1)S(1)}, bf16[5,96,768]{2,1,0:T(8,128)(2,1)S(1)}, u32[]{:S(2)}, u32[]{:S(2)}) collective-permute-start(bf16[5,96,768]{2,1,0:T(8,128)(2,1)S(1)} %add_convert_fusion.1), channel_id=1, source_target_pairs={{1,3},{5,7},{9,11},{13,15},{17,19},{21,23},{25,27},{29,31}} | collective-permute-start | bytes 2211848 | tf_op jit(solution)/shard_map/ppermute | solution.py:764
  287.2 29.2 %collective-permute-start.83 = (bf16[3,96,768]{2,1,0:T(8,128)(2,1)S(1)}, bf16[3,96,768]{2,1,0:T(8,128)(2,1)S(1)}, u32[]{:S(2)}, u32[]{:S(2)}) collective-permute-start(bf16[3,96,768]{2,1,0:T(8,128)(2,1)S(1)} %get-tuple-element.461), channel_id=1, source_target_pairs={{0,16},{4,12},{8,24},{12,4},{16,0},{20,28},{24,8},{28,20},{1,17},{... | collective-permute-start | bytes 1327112 | tf_op jit(solution)/shard_map/ppermute | solution.py:760
  288.3 28.0 %collective-permute-start.84 = (bf16[3,96,768]{2,1,0:T(8,128)(2,1)S(1)}, bf16[3,96,768]{2,1,0:T(8,128)(2,1)S(1)}, u32[]{:S(2)}, u32[]{:S(2)}) collective-permute-start(bf16[3,96,768]{2,1,0:T(8,128)(2,1)S(1)} %get-tuple-element.462), channel_id=1, source_target_pairs={{0,16},{4,12},{8,24},{12,4},{16,0},{20,28},{24,8},{28,20},{1,17},{... | collective-permute-start | bytes 1327112 | tf_op jit(solution)/shard_map/ppermute | solution.py:760
  328.5 18.9 %collective-permute-start.90 = (bf16[4,3,96,768]{3,2,1,0:T(8,128)(2,1)S(1)}, bf16[4,3,96,768]{3,2,1,0:T(8,128)(2,1)S(1)}, u32[]{:S(2)}, u32[]{:S(2)}) collective-permute-start(bf16[4,3,96,768]{3,2,1,0:T(8,128)(2,1)S(1)} %copy-done.94), channel_id=1, source_target_pairs={{0,4},{4,0},{8,12},{12,8},{16,20},{20,16},{24,28},{28,24},{1,5},{5... | collective-permute-start | bytes 5308424 | tf_op jit(solution)/shard_map/ppermute | solution.py:760
  328.5 18.9 %collective-permute-start.87 = (bf16[3,96,768]{2,1,0:T(8,128)(2,1)S(1)}, bf16[3,96,768]{2,1,0:T(8,128)(2,1)S(1)}, u32[]{:S(2)}, u32[]{:S(2)}) collective-permute-start(bf16[3,96,768]{2,1,0:T(8,128)(2,1)S(1)} %get-tuple-element.485), channel_id=1, source_target_pairs={{1,2},{5,6},{9,10},{13,14},{17,18},{21,22},{25,26},{29,30}} | collective-permute-start | bytes 1327112 | tf_op jit(solution)/shard_map/ppermute | solution.py:764
  329.3 16.9 %collective-permute-start.88 = (bf16[1,96,768]{2,1,0:T(8,128)(2,1)S(1)}, bf16[1,96,768]{2,1,0:T(8,128)(2,1)S(1)}, u32[]{:S(2)}, u32[]{:S(2)}) collective-permute-start(bf16[1,96,768]{2,1,0:T(8,128)(2,1)S(1)} %add_convert_fusion.6), channel_id=1, source_target_pairs={{1,3},{5,7},{9,11},{13,15},{17,19},{21,23},{25,27},{29,31}} | collective-permute-start | bytes 442376 | tf_op jit(solution)/shard_map/ppermute | solution.py:764
  330.0 17.4 %collective-permute-start.89 = (bf16[3,96,768]{2,1,0:T(8,128)(2,1)S(1)}, bf16[3,96,768]{2,1,0:T(8,128)(2,1)S(1)}, u32[]{:S(2)}, u32[]{:S(2)}) collective-permute-start(bf16[3,96,768]{2,1,0:T(8,128)(2,1)S(1)} %fusion.41), channel_id=1, source_target_pairs={{0,1},{3,2},{4,5},{7,6},{8,9},{11,10},{12,13},{15,14},{16,17},{19,... | collective-permute-start | bytes 1327112 | tf_op jit(solution)/shard_map/ppermute | solution.py:764
  336.7 17.6 %collective-permute-start.91 = (bf16[6,96,768]{2,1,0:T(8,128)(2,1)S(1)}, bf16[6,96,768]{2,1,0:T(8,128)(2,1)S(1)}, u32[]{:S(2)}, u32[]{:S(2)}) collective-permute-start(bf16[6,96,768]{2,1,0:T(8,128)(2,1)S(1)} %get-tuple-element.496), channel_id=1, source_target_pairs={{0,16},{4,12},{8,24},{12,4},{16,0},{20,28},{24,8},{28,20},{1,17},{... | collective-permute-start | bytes 2654216 | tf_op jit(solution)/shard_map/ppermute | solution.py:760
  360.5 21.3 %collective-permute-start.94 = (bf16[6,96,768]{2,1,0:T(8,128)(2,1)S(1)}, bf16[6,96,768]{2,1,0:T(8,128)(2,1)S(1)}, u32[]{:S(2)}, u32[]{:S(2)}) collective-permute-start(bf16[6,96,768]{2,1,0:T(8,128)(2,1)S(1)} %fusion.1), channel_id=1, source_target_pairs={{0,8},{4,20},{8,0},{12,28},{16,24},{20,4},{24,16},{28,12},{1,9},{5... | collective-permute-start | bytes 2654216 | tf_op jit(solution)/shard_map/ppermute | solution.py:760
  362.8 18.2 %collective-permute-start.96 = (bf16[3,96,768]{2,1,0:T(8,128)(2,1)S(1)}, bf16[3,96,768]{2,1,0:T(8,128)(2,1)S(1)}, u32[]{:S(2)}, u32[]{:S(2)}) collective-permute-start(bf16[3,96,768]{2,1,0:T(8,128)(2,1)S(1)} %get-tuple-element.503), channel_id=1, source_target_pairs={{0,16},{4,12},{8,24},{12,4},{16,0},{20,28},{24,8},{28,20},{1,17},{... | collective-permute-start | bytes 1327112 | tf_op jit(solution)/shard_map/ppermute | solution.py:760
  384.2 22.4 %collective-permute-start.99 = (bf16[4,3,96,768]{3,2,1,0:T(8,128)(2,1)}, bf16[4,3,96,768]{3,2,1,0:T(8,128)(2,1)}, u32[]{:S(2)}, u32[]{:S(2)}) collective-permute-start(bf16[4,3,96,768]{3,2,1,0:T(8,128)(2,1)} %get-tuple-element.513), channel_id=1, source_target_pairs={{0,4},{4,0},{8,12},{12,8},{16,20},{20,16},{24,28},{28,24},{1,5},{5... | collective-permute-start | bytes 5308424 | tf_op jit(solution)/shard_map/ppermute | solution.py:760
  384.7 21.8 %collective-permute-start.97 = (bf16[6,96,768]{2,1,0:T(8,128)(2,1)}, bf16[6,96,768]{2,1,0:T(8,128)(2,1)}, u32[]{:S(2)}, u32[]{:S(2)}) collective-permute-start(bf16[6,96,768]{2,1,0:T(8,128)(2,1)} %fusion.6), channel_id=1, source_target_pairs={{3,2},{0,1},{7,6},{4,5},{11,10},{8,9},{15,14},{12,13},{19,18},{16,... | collective-permute-start | bytes 2654216 | tf_op jit(solution)/shard_map/ppermute | solution.py:764
  387.5 19.0 %collective-permute-start.98 = (bf16[3,96,768]{2,1,0:T(8,128)(2,1)}, bf16[3,96,768]{2,1,0:T(8,128)(2,1)}, u32[]{:S(2)}, u32[]{:S(2)}) collective-permute-start(bf16[3,96,768]{2,1,0:T(8,128)(2,1)} %fusion.36), channel_id=1, source_target_pairs={{0,8},{4,20},{8,0},{12,28},{16,24},{20,4},{24,16},{28,12},{1,9},{5... | collective-permute-start | bytes 1327112 | tf_op jit(solution)/shard_map/ppermute | solution.py:760
  408.3 18.2 %collective-permute-start.100 = (bf16[6,96,768]{2,1,0:T(8,128)(2,1)S(1)}, bf16[6,96,768]{2,1,0:T(8,128)(2,1)S(1)}, u32[]{:S(2)}, u32[]{:S(2)}) collective-permute-start(bf16[6,96,768]{2,1,0:T(8,128)(2,1)S(1)} %add_convert_fusion), channel_id=1, source_target_pairs={{2,1},{6,5},{10,9},{14,13},{18,17},{22,21},{26,25},{30,29}} | collective-permute-start | bytes 2654216 | tf_op jit(solution)/shard_map/ppermute | solution.py:764
  426.6 17.1 %collective-permute-start.105 = (bf16[3,96,768]{2,1,0:T(8,128)(2,1)S(1)}, bf16[3,96,768]{2,1,0:T(8,128)(2,1)S(1)}, u32[]{:S(2)}, u32[]{:S(2)}) collective-permute-start(bf16[3,96,768]{2,1,0:T(8,128)(2,1)S(1)} %add_convert_fusion.3), channel_id=1, source_target_pairs={{2,0},{6,4},{10,8},{14,12},{18,16},{22,20},{26,24},{30,28}} | collective-permute-start | bytes 1327112 | tf_op jit(solution)/shard_map/ppermute | solution.py:764
  (259 other events, 2901.5 us)
Sparse Core Ops, SparseCore 0:
  9.8 43.0 all-gather.4
  54.4 39.1 all-gather.6

commit v5 on v4

--- a/solution.py
+++ b/solution.py
@@ -643,6 +643,12 @@
 def shampoo(grad, full, right, left_root, left_stats, right_stats, weights, ema, first, earlier):
     count, rows, _ = grad.shape
 
+    def products(one, two, block):
+        if rows % 16:
+            return dot(one, block), dot(two, block)
+        both = dot(jnp.concatenate([one, two], axis=0), block)
+        return both[:rows], both[rows:]
+
     def kernel(g_ref, lr_ref, ls_ref, rs_ref, w_ref, e_ref, *refs):
         f_refs, refs = refs[: len(full.arrays)], refs[len(full.arrays) :]
         r_refs, refs = refs[: len(right.arrays)], refs[len(right.arrays) + len(earlier) :]
@@ -654,16 +660,19 @@
         block = full.step(j)[...]
         right_block = right.step(j)[...]
         go_ref[0] = g_ref[0]
-        gram = dot(g_ref[0].astype(BF), block, NT)
-        lo_ref[0] = STAT_DECAY * ls_ref[0] + (1.0 - STAT_DECAY) * gram
         pick = (
             lax.broadcasted_iota(jnp.int32, (rows, D), 1)
             == lax.broadcasted_iota(jnp.int32, (rows, D), 0) + at
         )
-        columns = dot(jnp.where(pick, 1.0, 0.0).astype(BF), block, NT).astype(BF)
-        ro_ref[0] = STAT_DECAY * rs_ref[0] + (1.0 - STAT_DECAY) * dot(columns, block)
-        lifted = dot(lr_ref[0].astype(BF), block).astype(BF)
-        precond = dot(lifted, right_block)
+        grads, picked, root = (
+            part.astype(BF) for part in (g_ref[0], jnp.where(pick, 1.0, 0.0), lr_ref[0])
+        )
+        turned = block.T
+        gram, columns = products(grads, picked, turned)
+        own_columns, lifted = products(columns.astype(BF), root, block)
+        lo_ref[0] = STAT_DECAY * ls_ref[0] + (1.0 - STAT_DECAY) * gram
+        ro_ref[0] = STAT_DECAY * rs_ref[0] + (1.0 - STAT_DECAY) * own_columns
+        precond = dot(lifted.astype(BF), right_block)
         renewed = w_ref[0] * (1.0 - RATE_MAT * DECAY_MAT) - RATE_MAT * precond
         wo_ref[0] = renewed
         eo_ref[0] = EMA_DECAY * e_ref[0] + (1.0 - EMA_DECAY) * renewed
@@ -799,12 +808,12 @@
     "attend0": [["place3", "place4"], ["place3", "place5", "place6"], ["place3"]],
     "mlp0": [["place5", "place6", "place7"], ["place5"]],
     "project0": [["place6", "place7"], ["place6"]],
-    "qkv1": [["place7", "right0", "right1"]],
-    "attend1": [["place7"]],
-    "mlp1": [["right0", "right1"]],
+    "qkv1": [["place7", "right0"]],
+    "attend1": [["place7", "right1"]],
+    "mlp1": [["right0"]],
     "project1": [["out1", "right0", "right1"]],
     "grad_mlp1": [["out1", "right1"]],
-    "attend_back1": [["out1", "mlp1"]],
+    "attend_back1": [["out1", "mlp1", "right1"]],
     "stream_back1": [["out1", "mlp1", "qkv1"]],
     "mlp_back0": [["mlp1"]],
     "grad_out0": [["out1", "mlp1", "qkv1"]],

time: 521 us -> 520 us (level)
  no operation moved by 1% of the time
where the time goes in v5:
time: 520 us; the launch traced here: 515 us
  Pallas kernels  173 us (33%)
  waiting for transfers between devices  168 us (32%)
  starting transfers between devices  102 us (20%)
  local copies, waits for them, and re-layouts  38.3 us (7%)
  other arithmetic  17.4 us (3%)
  between operations  16.5 us (3%)
    pallas_call x22, Pallas kernels, call(): pl.pallas_call(kernel, grid=grid, in_specs=in_specs, out_specs=out_specs,...  173 us
    ppermute x111, waiting for transfers between devices, swap(): lax.ppermute(array, 'dp', [(i, i ^ STEPS[axis][i % 2]) for i in range(DP)])  127 us
    ppermute x111, starting transfers between devices, swap(): lax.ppermute(array, 'dp', [(i, i ^ STEPS[axis][i % 2]) for i in range(DP)])  74.4 us
    ppermute x16, waiting for transfers between devices, hop(): return lax.ppermute(array, 'head', pairs)  31.1 us
    unnamed x326, local copies, waits for them, and re-layouts  29.4 us
    ppermute x16, starting transfers between devices, hop(): return lax.ppermute(array, 'head', pairs)  27.2 us
    all_gather x2, waiting for transfers between devices, gather_line(): lax.all_gather(array, 'head')  10.6 us
  transfers between devices with their start and end apart: 129, of which 42 were waited for; matrix products, arithmetic and copies ran while one was open for 3% of the time, Pallas kernels for 30%

profile of v5, /device:TPU:0, one launch (start us, length us, event | category | flops | bytes accessed | tf_op | source)
XLA Modules:
  0.0 515.0 jit_solution(12052349418659759076)
XLA Ops:
  14.8 8.7 %collective-permute-done.refs_1_.refs_17_.refs_33_ = bf16[3,96,768]{2,1,0:T(8,128)(2,1)S(1)} collective-permute-done((bf16[3,96,768]{2,1,0:T(8,128)(2,1)}, bf16[3,96,768]{2,1,0:T(8,128)(2,1)S(1)}, u32[]{:S(2)}, u32[]{:S(2)}) %collective-permute-start) | collective-permute-done | bytes 442400 | tf_op jit(solution)/shard_map/ppermute | solution.py:769
  42.2 10.6 %all-gather.5.cloned.1.call-done = bf16[12,96,768]{2,1,0:T(8,128)(2,1)} async-done(((bf16[3,96,768]{2,1,0:T(8,128)(2,1)}), bf16[12,96,768]{2,1,0:T(8,128)(2,1)}) %all-gather.5.cloned.1.call-update) | async-done | bytes 1769488 | tf_op jit(solution)/shard_map/all_gather | solution.py:863
  59.6 8.7 %collective-permute-done.14.refs_9_.refs_49_.refs_33_ = bf16[3,96,768]{2,1,0:T(8,128)(2,1)} collective-permute-done((bf16[3,96,768]{2,1,0:T(8,128)(2,1)S(1)}, bf16[3,96,768]{2,1,0:T(8,128)(2,1)}, u32[]{:S(2)}, u32[]{:S(2)}) %collective-permute-start.14) | collective-permute-done | bytes 442400 | tf_op jit(solution)/shard_map/ppermute | solution.py:769
  85.7 8.2 %qkv_in.2 = (bf16[624,768]{1,0:T(8,128)(2,1)S(1)}, bf16[624,2304]{1,0:T(8,128)(2,1)S(1)}, bf16[624,1536]{1,0:T(8,128)(2,1)S(1)}, f32[624,1536]{1,0:T(8,128)S(1)}) custom-call(bf16[624,768]{1,0:T(8,128)(2,1)S(1)} %bitcast.101, f32[1,768]{1,0:T(1,128)S(1)} %get-tuple-element.620.g_ref.c_ref, f32[2,1,768]{2,1,0:T(1,128)S(1)} %constant_dynamic-update-slice_fusion.c_ref, ...), custom_call_target="tpu_custom_call" | custom-call | flops 9900000256 | bytes 17630208 | tf_op jit(solution)/shard_map/qkv_in/pallas_call | solution.py:53
  108.8 5.4 %collective-permute-done.26.refs_9_ = bf16[3,96,768]{2,1,0:T(8,128)(2,1)S(1)} collective-permute-done((bf16[3,96,768]{2,1,0:T(8,128)(2,1)S(1)}, bf16[3,96,768]{2,1,0:T(8,128)(2,1)S(1)}, u32[]{:S(2)}, u32[]{:S(2)}) %collective-permute-start.26) | collective-permute-done | bytes 442400 | tf_op jit(solution)/shard_map/ppermute | solution.py:769
  118.0 9.2 %collective-permute-done.33.refs_25_.refs_17_ = bf16[3,96,768]{2,1,0:T(8,128)(2,1)S(1)} collective-permute-done((bf16[3,96,768]{2,1,0:T(8,128)(2,1)S(1)}, bf16[3,96,768]{2,1,0:T(8,128)(2,1)S(1)}, u32[]{:S(2)}, u32[]{:S(2)}) %collective-permute-start.33) | collective-permute-done | bytes 442400 | tf_op jit(solution)/shard_map/ppermute | solution.py:769
  134.9 10.1 %mlp_in.2 = (bf16[624,3072]{1,0:T(8,128)(2,1)S(1)}, bf16[624,3072]{1,0:T(8,128)(2,1)S(1)}) custom-call(bf16[624,768]{1,0:T(8,128)(2,1)S(1)} %get-tuple-element.495.h_ref.refs_0_, f32[1,3072]{1,0:T(1,128)S(1)} %get-tuple-element.622.b_ref, bf16[3,96,768]{2,1,0:T(8,128)(2,1)} %copy-done.36, bf16[3,96,768]{2,1,0:T(8,128)(2,1)} %copy-done.97, ...), custom_call_target="tpu_custom_call" | custom-call | flops 12099999744 | bytes 22794240 | tf_op jit(solution)/shard_map/mlp_in/pallas_call | solution.py:53
  152.8 8.0 %project.2.x_ref = f32[624,768]{1,0:T(8,128)S(1)} custom-call(bf16[624,768]{1,0:T(8,128)(2,1)S(1)} %bitcast.102, bf16[624,768]{1,0:T(8,128)(2,1)S(1)} %attend.2.o_ref.refs_2_, bf16[624,3072]{1,0:T(8,128)(2,1)S(1)} %get-tuple-element.354.a_ref.refs_4_, f32[1,768]{1,0:T(1,128)S(1)} %get-tuple-element.619.b_ref, ...), custom_call_target="tpu_custom_call" | custom-call | flops 8800000000 | bytes 21826560 | tf_op jit(solution)/shard_map/project/pallas_call | solution.py:53
  171.8 8.0 %qkv_in.3 = (bf16[624,768]{1,0:T(8,128)(2,1)S(1)}, bf16[624,2304]{1,0:T(8,128)(2,1)S(1)}, bf16[624,1536]{1,0:T(8,128)(2,1)S(1)}, f32[624,1536]{1,0:T(8,128)S(1)}) custom-call(f32[624,768]{1,0:T(8,128)S(1)} %project.2.x_ref, f32[1,768]{1,0:T(1,128)S(1)} %get-tuple-element.618.g_ref.c_ref, f32[2,1,768]{2,1,0:T(1,128)S(1)} %constant_dynamic-update-slice_fusion.2.c_ref, ...), custom_call_target="tpu_custom_call" | custom-call | flops 9900000256 | bytes 25666560 | tf_op jit(solution)/shard_map/qkv_in/pallas_call | solution.py:53
  190.3 10.6 %mlp_in.3 = (bf16[624,3072]{1,0:T(8,128)(2,1)S(1)}, bf16[624,3072]{1,0:T(8,128)(2,1)S(1)}) custom-call(bf16[624,768]{1,0:T(8,128)(2,1)S(1)} %get-tuple-element.433.h_ref.refs_0_, f32[1,3072]{1,0:T(1,128)S(1)} %get-tuple-element.621.b_ref, bf16[3,96,768]{2,1,0:T(8,128)(2,1)} %copy-done.36, bf16[3,96,768]{2,1,0:T(8,128)(2,1)} %copy-done.97, ...), custom_call_target="tpu_custom_call" | custom-call | flops 12099999744 | bytes 29872128 | tf_op jit(solution)/shard_map/mlp_in/pallas_call | solution.py:53
  201.0 7.6 %grad_out.2 = (bf16[5,96,768]{2,1,0:T(8,128)(2,1)}, bf16[5,96,768]{2,1,0:T(8,128)(2,1)}, bf16[5,96,768]{2,1,0:T(8,128)(2,1)}, bf16[5,96,768]{2,1,0:T(8,128)(2,1)}, bf16[4,5,96,768]{3,2,1,0:T(8,128)(2,1)}) custom-call(bf16[624,768]{1,0:T(8,128)(2,1)S(1)} %attend.3.refs_0_.o_ref, bf16[624,768]{1,0:T(8,128)(2,1)S(1)} %bitcast.104, ...), custom_call_target="tpu_custom_call" | custom-call | flops 8800000000 | bytes 12607488 | tf_op jit(solution)/shard_map/grad_out/pallas_call | solution.py:53
  211.5 8.1 %project.3 = bf16[624,768]{1,0:T(8,128)(2,1)S(1)} custom-call(f32[624,768]{1,0:T(8,128)S(1)} %project.2.x_ref, bf16[624,768]{1,0:T(8,128)(2,1)S(1)} %attend.3.refs_0_.o_ref, bf16[624,3072]{1,0:T(8,128)(2,1)S(1)} %get-tuple-element.391.refs_2_.a_ref, f32[1,768]{1,0:T(1,128)S(1)} %get-tuple-element.617.b_ref, ...), custom_call_target="tpu_custom_call" | custom-call | flops 8800000000 | bytes 21826560 | tf_op jit(solution)/shard_map/project/pallas_call | solution.py:53
  226.5 9.0 %mlp_back.2 = (bf16[624,768]{1,0:T(8,128)(2,1)}, bf16[624,768]{1,0:T(8,128)(2,1)S(1)}, bf16[624,3072]{1,0:T(8,128)(2,1)S(1)}, f32[1,768]{1,0:T(1,128)S(1)}, f32[1,3072]{1,0:T(1,128)S(1)}) custom-call(bf16[624,768]{1,0:T(8,128)(2,1)S(1)} %bitcast.106, bf16[624,3072]{1,0:T(8,128)(2,1)S(1)} %get-tuple-element.406.s_ref, ...), custom_call_target="tpu_custom_call" | custom-call | flops 9900000256 | bytes 24714240 | tf_op jit(solution)/shard_map/mlp_back/pallas_call | solution.py:53
  235.5 6.2 %grad_mlp.2 = (bf16[4,96,768]{2,1,0:T(8,128)(2,1)}, bf16[4,96,768]{2,1,0:T(8,128)(2,1)}, bf16[4,96,768]{2,1,0:T(8,128)(2,1)}, bf16[4,96,768]{2,1,0:T(8,128)(2,1)}, bf16[4,4,96,768]{3,2,1,0:T(8,128)(2,1)}) custom-call(bf16[624,768]{1,0:T(8,128)(2,1)S(1)} %get-tuple-element.433.h_ref.refs_0_, bf16[624,3072]{1,0:T(8,128)(2,1)S(1)} %get-tuple-element.409.refs_1_.du_ref), custom_call_target="tpu_custom_call" | custom-call | flops 7260000256 | bytes 9510912 | tf_op jit(solution)/shard_map/grad_mlp/pallas_call | solution.py:53
  241.7 5.4 %collective-permute-done.68.refs_11_ = bf16[3,96,768]{2,1,0:T(8,128)(2,1)S(1)} collective-permute-done((bf16[3,96,768]{2,1,0:T(8,128)(2,1)S(1)}, bf16[3,96,768]{2,1,0:T(8,128)(2,1)S(1)}, u32[]{:S(2)}, u32[]{:S(2)}) %collective-permute-start.68) | collective-permute-done | bytes 442400 | tf_op jit(solution)/shard_map/ppermute | solution.py:769
  249.4 8.4 %attend_back.2 = (bf16[624,2304]{1,0:T(8,128)(2,1)S(1)}, f32[2,1,768]{2,1,0:T(1,128)S(1)}) custom-call(bf16[624,768]{1,0:T(8,128)(2,1)S(1)} %get-tuple-element.420.do_ref, bf16[624,2304]{1,0:T(8,128)(2,1)S(1)} %get-tuple-element.374.z_ref, bf16[624,1536]{1,0:T(8,128)(2,1)S(1)} %get-tuple-element.421.u_ref, f32[624,1536]{1,0:T(8,128)S(1)} %get-tuple-element.422.i_ref, ...), custom_call_target="tpu_custom_call" | custom-call | flops 15399999488 | bytes 12472320 | tf_op jit(solution)/shard_map/attend_back/pallas_call | solution.py:53
  270.3 12.5 %stream_back.2 = (f32[624,768]{1,0:T(8,128)S(1)}, f32[1,768]{1,0:T(1,128)S(1)}) custom-call(bf16[624,768]{1,0:T(8,128)(2,1)S(1)} %bitcast.107, f32[624,768]{1,0:T(8,128)S(1)} %project.2.x_ref, f32[1,768]{1,0:T(1,128)S(1)} %get-tuple-element.618.g_ref.c_ref, bf16[624,3072]{1,0:T(8,128)(2,1)S(1)} %get-tuple-element.409.refs_1_.du_ref, ...), custom_call_target="tpu_custom_call" | custom-call | flops 13200000000 | bytes 39819264 | tf_op jit(solution)/shard_map/stream_back/pallas_call | solution.py:53
  290.0 8.4 %mlp_back.3 = (bf16[624,768]{1,0:T(8,128)(2,1)S(1)}, bf16[624,768]{1,0:T(8,128)(2,1)S(1)}, bf16[624,3072]{1,0:T(8,128)(2,1)S(1)}, f32[1,768]{1,0:T(1,128)S(1)}, f32[1,3072]{1,0:T(1,128)S(1)}) custom-call(f32[624,768]{1,0:T(8,128)S(1)} %get-tuple-element.511.g_ref, bf16[624,3072]{1,0:T(8,128)(2,1)S(1)} %copy-done.20, ...), custom_call_target="tpu_custom_call" | custom-call | flops 9900000256 | bytes 25672704 | tf_op jit(solution)/shard_map/mlp_back/pallas_call | solution.py:53
  307.6 9.4 %grad_out.3 = (bf16[6,96,768]{2,1,0:T(8,128)(2,1)}, bf16[6,96,768]{2,1,0:T(8,128)(2,1)}, bf16[6,96,768]{2,1,0:T(8,128)(2,1)}, bf16[6,96,768]{2,1,0:T(8,128)(2,1)}, bf16[4,6,96,768]{3,2,1,0:T(8,128)(2,1)}) custom-call(bf16[624,768]{1,0:T(8,128)(2,1)S(1)} %copy-done.28, bf16[624,3072]{1,0:T(8,128)(2,1)S(1)} %get-tuple-element.451.refs_1_.du_ref, ...), custom_call_target="tpu_custom_call" | custom-call | flops 10339999744 | bytes 18579456 | tf_op jit(solution)/shard_map/grad_out/pallas_call | solution.py:53
  330.9 6.8 %collective-permute-start.89 = (bf16[3,96,768]{2,1,0:T(8,128)(2,1)S(1)}, bf16[3,96,768]{2,1,0:T(8,128)(2,1)S(1)}, u32[]{:S(2)}, u32[]{:S(2)}) collective-permute-start(bf16[3,96,768]{2,1,0:T(8,128)(2,1)S(1)} %fusion.41), channel_id=1, source_target_pairs={{0,1},{3,2},{4,5},{7,6},{8,9},{11,10},{12,13},{15,14},{16,17},{19,... | collective-permute-start | bytes 1327112 | tf_op jit(solution)/shard_map/ppermute | solution.py:773
  338.7 8.5 %attend_back.3 = (bf16[624,2304]{1,0:T(8,128)(2,1)S(1)}, f32[2,1,768]{2,1,0:T(1,128)S(1)}) custom-call(bf16[624,768]{1,0:T(8,128)(2,1)S(1)} %get-tuple-element.483.do_ref, bf16[624,2304]{1,0:T(8,128)(2,1)S(1)} %copy-done.31, bf16[624,1536]{1,0:T(8,128)(2,1)S(1)} %copy-done.33, f32[624,1536]{1,0:T(8,128)S(1)} %copy-done.26, f32[2,1,768]{2,1,0:T(1,128)S(1)} %copy-done.8), custom_call_target="tpu_custom_call" | custom-call | flops 15399999488 | bytes 12472320 | tf_op jit(solution)/shard_map/attend_back/pallas_call | solution.py:53
  364.6 11.1 %collective-permute-done.95 = bf16[3,96,768]{2,1,0:T(8,128)(2,1)S(1)} collective-permute-done((bf16[3,96,768]{2,1,0:T(8,128)(2,1)S(1)}, bf16[3,96,768]{2,1,0:T(8,128)(2,1)S(1)}, u32[]{:S(2)}, u32[]{:S(2)}) %collective-permute-start.95) | collective-permute-done | bytes 442400 | tf_op jit(solution)/shard_map/ppermute | solution.py:769
  375.7 6.3 %collective-permute-done.96 = bf16[3,96,768]{2,1,0:T(8,128)(2,1)S(1)} collective-permute-done((bf16[3,96,768]{2,1,0:T(8,128)(2,1)S(1)}, bf16[3,96,768]{2,1,0:T(8,128)(2,1)S(1)}, u32[]{:S(2)}, u32[]{:S(2)}) %collective-permute-start.96) | collective-permute-done | bytes 442400 | tf_op jit(solution)/shard_map/ppermute | solution.py:769
  394.5 12.2 %stream_back.3 = (f32[624,768]{1,0:T(8,128)S(1)}, f32[1,768]{1,0:T(1,128)S(1)}) custom-call(f32[624,768]{1,0:T(8,128)S(1)} %copy-done.16, bf16[624,768]{1,0:T(8,128)(2,1)S(1)} %bitcast.103, f32[1,768]{1,0:T(1,128)S(1)} %copy-done.6, bf16[624,3072]{1,0:T(8,128)(2,1)S(1)} %copy-done.18, bf16[624,2304]{1,0:T(8,128)(2,1)S(1)} %copy-done.22, ...), custom_call_target="tpu_custom_call" | custom-call | flops 13200000000 | bytes 29202432 | tf_op jit(solution)/shard_map/stream_back/pallas_call | solution.py:53
  417.6 8.3 %collective-permute-done.101 = bf16[3,96,768]{2,1,0:T(8,128)(2,1)S(1)} collective-permute-done((bf16[3,96,768]{2,1,0:T(8,128)(2,1)S(1)}, bf16[3,96,768]{2,1,0:T(8,128)(2,1)S(1)}, u32[]{:S(2)}, u32[]{:S(2)}) %collective-permute-start.101) | collective-permute-done | bytes 442400 | tf_op jit(solution)/shard_map/ppermute | solution.py:773
  432.3 6.4 %collective-permute-done.107 = f32[2,4736]{1,0:T(2,128)S(1)} collective-permute-done((f32[2,4736]{1,0:T(2,128)S(1)}, f32[2,4736]{1,0:T(2,128)S(1)}, u32[]{:S(2)}, u32[]{:S(2)}) %collective-permute-start.107) | collective-permute-done | bytes 37920 | tf_op jit(solution)/shard_map/ppermute | solution.py:769
  438.7 6.0 %collective-permute-done.105 = bf16[3,96,768]{2,1,0:T(8,128)(2,1)S(1)} collective-permute-done((bf16[3,96,768]{2,1,0:T(8,128)(2,1)S(1)}, bf16[3,96,768]{2,1,0:T(8,128)(2,1)S(1)}, u32[]{:S(2)}, u32[]{:S(2)}) %collective-permute-start.105) | collective-permute-done | bytes 442400 | tf_op jit(solution)/shard_map/ppermute | solution.py:773
  450.6 5.7 %collective-permute-done.111 = f32[2,4736]{1,0:T(2,128)S(1)} collective-permute-done((f32[2,4736]{1,0:T(2,128)S(1)}, f32[2,4736]{1,0:T(2,128)S(1)}, u32[]{:S(2)}, u32[]{:S(2)}) %collective-permute-start.111) | collective-permute-done | bytes 37920 | tf_op jit(solution)/shard_map/ppermute | solution.py:769
  463.2 9.8 %collective-permute-done.116 = f32[2,4736]{1,0:T(2,128)S(1)} collective-permute-done((f32[2,4736]{1,0:T(2,128)S(1)}, f32[2,4736]{1,0:T(2,128)S(1)}, u32[]{:S(2)}, u32[]{:S(2)}) %collective-permute-start.116) | collective-permute-done | bytes 37920 | tf_op jit(solution)/shard_map/ppermute | solution.py:773
  480.9 5.6 %collective-permute-done.119.refs_1_ = bf16[3,96,768]{2,1,0:T(8,128)(2,1)S(1)} collective-permute-done((bf16[3,96,768]{2,1,0:T(8,128)(2,1)S(1)}, bf16[3,96,768]{2,1,0:T(8,128)(2,1)S(1)}, u32[]{:S(2)}, u32[]{:S(2)}) %collective-permute-start.119) | collective-permute-done | bytes 442400 | tf_op jit(solution)/shard_map/ppermute | solution.py:769
  488.1 8.7 %shampoo.2 = (f32[6,96,768]{2,1,0:T(8,128)}, f32[6,96,768]{2,1,0:T(8,128)}, f32[6,96,768]{2,1,0:T(8,128)}, f32[6,96,768]{2,1,0:T(8,128)}, f32[6,96,768]{2,1,0:T(8,128)}) custom-call(f32[3,96,768]{2,1,0:T(8,128)S(1)} %get-tuple-element.555.g_ref, f32[6,96,768]{2,1,0:T(8,128)S(1)} %copy-done.9, f32[6,96,768]{2,1,0:T(8,128)S(1)} %copy-done.10, ...), custom_call_target="tpu_custom_call" | custom-call | flops 12099999744 | bytes 25657344 | tf_op jit(solution)/shard_map/shampoo/pallas_call | solution.py:53
  499.5 8.4 %shampoo.3 = (f32[6,96,768]{2,1,0:T(8,128)}, f32[6,96,768]{2,1,0:T(8,128)}, f32[6,96,768]{2,1,0:T(8,128)}, f32[6,96,768]{2,1,0:T(8,128)}, f32[6,96,768]{2,1,0:T(8,128)}) custom-call(f32[3,96,768]{2,1,0:T(8,128)S(1)} %get-tuple-element.592.g_ref, ...), custom_call_target="tpu_custom_call", output_to_operand_aliasing={{0}: (22, {}), {1}: (23, {}), {2}: (24, {}), {3}: (25, {}),... | custom-call | flops 12099999744 | bytes 34504704 | tf_op jit(solution)/shard_map/shampoo/pallas_call | solution.py:53
  (653 shorter events, 232.4 us)
Async XLA Ops:
  7.2 45.6 %all-gather.5.cloned.1.call-start = ((), (), s32[]{:S(2)}) async-start(), calls=%async_computation | async-start | bytes 2211840 | tf_op jit(solution)/shard_map/all_gather | solution.py:863
  9.6 89.6 %all-gather.7.cloned.1.call-start = ((), (), s32[]{:S(2)}) async-start(), calls=%async_computation.1 | async-start | bytes 2211840 | tf_op jit(solution)/shard_map/all_gather | solution.py:863
  14.2 18.6 %collective-permute-start.5 = (bf16[3,96,768]{2,1,0:T(8,128)(2,1)S(1)}, bf16[3,96,768]{2,1,0:T(8,128)(2,1)S(1)}, u32[]{:S(2)}, u32[]{:S(2)}) collective-permute-start(bf16[3,96,768]{2,1,0:T(8,128)(2,1)S(1)} %get-tuple-element.615.refs_0_.refs_16_), channel_id=1, source_target_pairs={{0,8},{4,20},{8,0},{12,28},{16,24},{20,4},{24,16},{28,12},{1,9},{5... | collective-permute-start | bytes 1327112 | tf_op jit(solution)/shard_map/ppermute | solution.py:769
  14.8 18.1 %collective-permute-start.6 = (bf16[3,96,768]{2,1,0:T(8,128)(2,1)S(1)}, bf16[3,96,768]{2,1,0:T(8,128)(2,1)S(1)}, u32[]{:S(2)}, u32[]{:S(2)}) collective-permute-start(bf16[3,96,768]{2,1,0:T(8,128)(2,1)S(1)} %get-tuple-element.615.refs_0_.refs_16_), channel_id=1, source_target_pairs={{0,16},{4,12},{8,24},{12,4},{16,0},{20,28},{24,8},{28,20},{1,17},{... | collective-permute-start | bytes 1327112 | tf_op jit(solution)/shard_map/ppermute | solution.py:769
  14.8 20.7 %collective-permute-start.3 = (bf16[3,96,768]{2,1,0:T(8,128)(2,1)}, bf16[3,96,768]{2,1,0:T(8,128)(2,1)S(1)}, u32[]{:S(2)}, u32[]{:S(2)}) collective-permute-start(bf16[3,96,768]{2,1,0:T(8,128)(2,1)} %get-tuple-element.616.refs_0_.refs_16_.refs_32_), channel_id=1, source_target_pairs={{0,4},{4,0},{8,12},{12,8},{16,20},{20,16},{24,28},{28,24},{1,5},{5... | collective-permute-start | bytes 1327112 | tf_op jit(solution)/shard_map/ppermute | solution.py:769
  37.1 19.9 %collective-permute-start.10 = (bf16[3,96,768]{2,1,0:T(8,128)(2,1)S(1)}, bf16[3,96,768]{2,1,0:T(8,128)(2,1)}, u32[]{:S(2)}, u32[]{:S(2)}) collective-permute-start(bf16[3,96,768]{2,1,0:T(8,128)(2,1)S(1)} %collective-permute-done.1.refs_2_.refs_18_.refs_34_), channel_id=1, source_target_pairs={{0,4},{4,0},{8,12},{12,8},{16,20},{20,16},{24,28},{28,24},{1,5},{5... | collective-permute-start | bytes 1327112 | tf_op jit(solution)/shard_map/ppermute | solution.py:769
  37.4 21.0 %collective-permute-start.12 = (bf16[3,96,768]{2,1,0:T(8,128)(2,1)S(1)}, bf16[3,96,768]{2,1,0:T(8,128)(2,1)S(1)}, u32[]{:S(2)}, u32[]{:S(2)}) collective-permute-start(bf16[3,96,768]{2,1,0:T(8,128)(2,1)S(1)} %collective-permute-done.6.refs_2_.refs_18_), channel_id=1, source_target_pairs={{0,4},{4,0},{8,12},{12,8},{16,20},{20,16},{24,28},{28,24},{1,5},{5... | collective-permute-start | bytes 1327112 | tf_op jit(solution)/shard_map/ppermute | solution.py:769
  58.4 19.4 %collective-permute-start.19 = (bf16[3,96,768]{2,1,0:T(8,128)(2,1)S(1)}, bf16[3,96,768]{2,1,0:T(8,128)(2,1)}, u32[]{:S(2)}, u32[]{:S(2)}) collective-permute-start(bf16[3,96,768]{2,1,0:T(8,128)(2,1)S(1)} %get-tuple-element.611.refs_24_.refs_8_.refs_16_.refs_56_), channel_id=1, source_target_pairs={{0,8},{4,20},{8,0},{12,28},{16,24},{20,4},{24,16},{28,12},{1,9},{5... | collective-permute-start | bytes 1327112 | tf_op jit(solution)/shard_map/ppermute | solution.py:769
  59.1 18.7 %collective-permute-start.20 = (bf16[3,96,768]{2,1,0:T(8,128)(2,1)S(1)}, bf16[3,96,768]{2,1,0:T(8,128)(2,1)}, u32[]{:S(2)}, u32[]{:S(2)}) collective-permute-start(bf16[3,96,768]{2,1,0:T(8,128)(2,1)S(1)} %get-tuple-element.611.refs_24_.refs_8_.refs_16_.refs_56_), channel_id=1, source_target_pairs={{0,16},{4,12},{8,24},{12,4},{16,0},{20,28},{24,8},{28,20},{1,17},{... | collective-permute-start | bytes 1327112 | tf_op jit(solution)/shard_map/ppermute | solution.py:769
  101.0 16.5 %collective-permute-start.31 = (bf16[3,96,768]{2,1,0:T(8,128)(2,1)S(1)}, bf16[3,96,768]{2,1,0:T(8,128)(2,1)S(1)}, u32[]{:S(2)}, u32[]{:S(2)}) collective-permute-start(bf16[3,96,768]{2,1,0:T(8,128)(2,1)S(1)} %get-tuple-element.325.refs_8_), channel_id=1, source_target_pairs={{0,4},{4,0},{8,12},{12,8},{16,20},{20,16},{24,28},{28,24},{1,5},{5... | collective-permute-start | bytes 1327112 | tf_op jit(solution)/shard_map/ppermute | solution.py:769
  223.0 24.1 %collective-permute-start.66 = (bf16[5,96,768]{2,1,0:T(8,128)(2,1)S(1)}, bf16[5,96,768]{2,1,0:T(8,128)(2,1)S(1)}, u32[]{:S(2)}, u32[]{:S(2)}) collective-permute-start(bf16[5,96,768]{2,1,0:T(8,128)(2,1)S(1)} %get-tuple-element.411), channel_id=1, source_target_pairs={{0,16},{4,12},{8,24},{12,4},{16,0},{20,28},{24,8},{28,20},{1,17},{... | collective-permute-start | bytes 2211848 | tf_op jit(solution)/shard_map/ppermute | solution.py:769
  223.9 23.2 %collective-permute-start.67 = (bf16[5,96,768]{2,1,0:T(8,128)(2,1)S(1)}, bf16[5,96,768]{2,1,0:T(8,128)(2,1)S(1)}, u32[]{:S(2)}, u32[]{:S(2)}) collective-permute-start(bf16[5,96,768]{2,1,0:T(8,128)(2,1)S(1)} %get-tuple-element.412), channel_id=1, source_target_pairs={{0,16},{4,12},{8,24},{12,4},{16,0},{20,28},{24,8},{28,20},{1,17},{... | collective-permute-start | bytes 2211848 | tf_op jit(solution)/shard_map/ppermute | solution.py:769
  225.0 22.1 %collective-permute-start.68 = (bf16[3,96,768]{2,1,0:T(8,128)(2,1)S(1)}, bf16[3,96,768]{2,1,0:T(8,128)(2,1)S(1)}, u32[]{:S(2)}, u32[]{:S(2)}) collective-permute-start(bf16[3,96,768]{2,1,0:T(8,128)(2,1)S(1)} %collective-permute-done.64.refs_9_), channel_id=1, source_target_pairs={{0,16},{4,12},{8,24},{12,4},{16,0},{20,28},{24,8},{28,20},{1,17},{... | collective-permute-start | bytes 1327112 | tf_op jit(solution)/shard_map/ppermute | solution.py:769
  226.0 21.1 %collective-permute-start.69 = (bf16[3,96,768]{2,1,0:T(8,128)(2,1)S(1)}, bf16[3,96,768]{2,1,0:T(8,128)(2,1)S(1)}, u32[]{:S(2)}, u32[]{:S(2)}) collective-permute-start(bf16[3,96,768]{2,1,0:T(8,128)(2,1)S(1)} %copy-done.58), channel_id=1, source_target_pairs={{0,4},{4,0},{8,12},{12,8},{16,20},{20,16},{24,28},{28,24},{1,5},{5... | collective-permute-start | bytes 1327112 | tf_op jit(solution)/shard_map/ppermute | solution.py:769
  226.0 21.1 %collective-permute-start.70 = (bf16[3,96,768]{2,1,0:T(8,128)(2,1)S(1)}, bf16[3,96,768]{2,1,0:T(8,128)(2,1)S(1)}, u32[]{:S(2)}, u32[]{:S(2)}) collective-permute-start(bf16[3,96,768]{2,1,0:T(8,128)(2,1)S(1)} %collective-permute-done.64.refs_9_), channel_id=1, source_target_pairs={{0,4},{4,0},{8,12},{12,8},{16,20},{20,16},{24,28},{28,24},{1,5},{5... | collective-permute-start | bytes 1327112 | tf_op jit(solution)/shard_map/ppermute | solution.py:769
  265.8 18.7 %collective-permute-start.78 = (bf16[4,3,96,768]{3,2,1,0:T(8,128)(2,1)}, bf16[4,3,96,768]{3,2,1,0:T(8,128)(2,1)S(1)}, u32[]{:S(2)}, u32[]{:S(2)}) collective-permute-start(bf16[4,3,96,768]{3,2,1,0:T(8,128)(2,1)} %get-tuple-element.441), channel_id=1, source_target_pairs={{0,4},{4,0},{8,12},{12,8},{16,20},{20,16},{24,28},{28,24},{1,5},{5... | collective-permute-start | bytes 5308424 | tf_op jit(solution)/shard_map/ppermute | solution.py:769
  265.9 18.7 %collective-permute-start.75 = (bf16[5,96,768]{2,1,0:T(8,128)(2,1)S(1)}, bf16[5,96,768]{2,1,0:T(8,128)(2,1)S(1)}, u32[]{:S(2)}, u32[]{:S(2)}) collective-permute-start(bf16[5,96,768]{2,1,0:T(8,128)(2,1)S(1)} %fusion.13), channel_id=1, source_target_pairs={{0,1},{2,3},{4,5},{6,7},{8,9},{10,11},{12,13},{14,15},{16,17},{18,... | collective-permute-start | bytes 2211848 | tf_op jit(solution)/shard_map/ppermute | solution.py:773
  287.1 30.0 %collective-permute-start.80 = (bf16[5,96,768]{2,1,0:T(8,128)(2,1)S(1)}, bf16[5,96,768]{2,1,0:T(8,128)(2,1)S(1)}, u32[]{:S(2)}, u32[]{:S(2)}) collective-permute-start(bf16[5,96,768]{2,1,0:T(8,128)(2,1)S(1)} %add_convert_fusion.1), channel_id=1, source_target_pairs={{1,3},{5,7},{9,11},{13,15},{17,19},{21,23},{25,27},{29,31}} | collective-permute-start | bytes 2211848 | tf_op jit(solution)/shard_map/ppermute | solution.py:773
  287.8 29.2 %collective-permute-start.83 = (bf16[3,96,768]{2,1,0:T(8,128)(2,1)S(1)}, bf16[3,96,768]{2,1,0:T(8,128)(2,1)S(1)}, u32[]{:S(2)}, u32[]{:S(2)}) collective-permute-start(bf16[3,96,768]{2,1,0:T(8,128)(2,1)S(1)} %get-tuple-element.463), channel_id=1, source_target_pairs={{0,16},{4,12},{8,24},{12,4},{16,0},{20,28},{24,8},{28,20},{1,17},{... | collective-permute-start | bytes 1327112 | tf_op jit(solution)/shard_map/ppermute | solution.py:769
  288.8 28.3 %collective-permute-start.84 = (bf16[3,96,768]{2,1,0:T(8,128)(2,1)S(1)}, bf16[3,96,768]{2,1,0:T(8,128)(2,1)S(1)}, u32[]{:S(2)}, u32[]{:S(2)}) collective-permute-start(bf16[3,96,768]{2,1,0:T(8,128)(2,1)S(1)} %get-tuple-element.464), channel_id=1, source_target_pairs={{0,16},{4,12},{8,24},{12,4},{16,0},{20,28},{24,8},{28,20},{1,17},{... | collective-permute-start | bytes 1327112 | tf_op jit(solution)/shard_map/ppermute | solution.py:769
  329.4 19.0 %collective-permute-start.90 = (bf16[4,3,96,768]{3,2,1,0:T(8,128)(2,1)S(1)}, bf16[4,3,96,768]{3,2,1,0:T(8,128)(2,1)S(1)}, u32[]{:S(2)}, u32[]{:S(2)}) collective-permute-start(bf16[4,3,96,768]{3,2,1,0:T(8,128)(2,1)S(1)} %copy-done.94), channel_id=1, source_target_pairs={{0,4},{4,0},{8,12},{12,8},{16,20},{20,16},{24,28},{28,24},{1,5},{5... | collective-permute-start | bytes 5308424 | tf_op jit(solution)/shard_map/ppermute | solution.py:769
  329.4 19.0 %collective-permute-start.87 = (bf16[3,96,768]{2,1,0:T(8,128)(2,1)S(1)}, bf16[3,96,768]{2,1,0:T(8,128)(2,1)S(1)}, u32[]{:S(2)}, u32[]{:S(2)}) collective-permute-start(bf16[3,96,768]{2,1,0:T(8,128)(2,1)S(1)} %get-tuple-element.487), channel_id=1, source_target_pairs={{1,2},{5,6},{9,10},{13,14},{17,18},{21,22},{25,26},{29,30}} | collective-permute-start | bytes 1327112 | tf_op jit(solution)/shard_map/ppermute | solution.py:773
  330.2 17.0 %collective-permute-start.88 = (bf16[1,96,768]{2,1,0:T(8,128)(2,1)S(1)}, bf16[1,96,768]{2,1,0:T(8,128)(2,1)S(1)}, u32[]{:S(2)}, u32[]{:S(2)}) collective-permute-start(bf16[1,96,768]{2,1,0:T(8,128)(2,1)S(1)} %add_convert_fusion.6), channel_id=1, source_target_pairs={{1,3},{5,7},{9,11},{13,15},{17,19},{21,23},{25,27},{29,31}} | collective-permute-start | bytes 442376 | tf_op jit(solution)/shard_map/ppermute | solution.py:773
  330.9 17.5 %collective-permute-start.89 = (bf16[3,96,768]{2,1,0:T(8,128)(2,1)S(1)}, bf16[3,96,768]{2,1,0:T(8,128)(2,1)S(1)}, u32[]{:S(2)}, u32[]{:S(2)}) collective-permute-start(bf16[3,96,768]{2,1,0:T(8,128)(2,1)S(1)} %fusion.41), channel_id=1, source_target_pairs={{0,1},{3,2},{4,5},{7,6},{8,9},{11,10},{12,13},{15,14},{16,17},{19,... | collective-permute-start | bytes 1327112 | tf_op jit(solution)/shard_map/ppermute | solution.py:773
  337.7 17.6 %collective-permute-start.91 = (bf16[6,96,768]{2,1,0:T(8,128)(2,1)S(1)}, bf16[6,96,768]{2,1,0:T(8,128)(2,1)S(1)}, u32[]{:S(2)}, u32[]{:S(2)}) collective-permute-start(bf16[6,96,768]{2,1,0:T(8,128)(2,1)S(1)} %get-tuple-element.498), channel_id=1, source_target_pairs={{0,16},{4,12},{8,24},{12,4},{16,0},{20,28},{24,8},{28,20},{1,17},{... | collective-permute-start | bytes 2654216 | tf_op jit(solution)/shard_map/ppermute | solution.py:769
  361.4 21.2 %collective-permute-start.94 = (bf16[6,96,768]{2,1,0:T(8,128)(2,1)S(1)}, bf16[6,96,768]{2,1,0:T(8,128)(2,1)S(1)}, u32[]{:S(2)}, u32[]{:S(2)}) collective-permute-start(bf16[6,96,768]{2,1,0:T(8,128)(2,1)S(1)} %fusion.1), channel_id=1, source_target_pairs={{0,8},{4,20},{8,0},{12,28},{16,24},{20,4},{24,16},{28,12},{1,9},{5... | collective-permute-start | bytes 2654216 | tf_op jit(solution)/shard_map/ppermute | solution.py:769
  363.7 18.3 %collective-permute-start.96 = (bf16[3,96,768]{2,1,0:T(8,128)(2,1)S(1)}, bf16[3,96,768]{2,1,0:T(8,128)(2,1)S(1)}, u32[]{:S(2)}, u32[]{:S(2)}) collective-permute-start(bf16[3,96,768]{2,1,0:T(8,128)(2,1)S(1)} %get-tuple-element.505), channel_id=1, source_target_pairs={{0,16},{4,12},{8,24},{12,4},{16,0},{20,28},{24,8},{28,20},{1,17},{... | collective-permute-start | bytes 1327112 | tf_op jit(solution)/shard_map/ppermute | solution.py:769
  385.0 22.4 %collective-permute-start.99 = (bf16[4,3,96,768]{3,2,1,0:T(8,128)(2,1)}, bf16[4,3,96,768]{3,2,1,0:T(8,128)(2,1)}, u32[]{:S(2)}, u32[]{:S(2)}) collective-permute-start(bf16[4,3,96,768]{3,2,1,0:T(8,128)(2,1)} %get-tuple-element.515), channel_id=1, source_target_pairs={{0,4},{4,0},{8,12},{12,8},{16,20},{20,16},{24,28},{28,24},{1,5},{5... | collective-permute-start | bytes 5308424 | tf_op jit(solution)/shard_map/ppermute | solution.py:769
  385.5 21.9 %collective-permute-start.97 = (bf16[6,96,768]{2,1,0:T(8,128)(2,1)}, bf16[6,96,768]{2,1,0:T(8,128)(2,1)}, u32[]{:S(2)}, u32[]{:S(2)}) collective-permute-start(bf16[6,96,768]{2,1,0:T(8,128)(2,1)} %fusion.6), channel_id=1, source_target_pairs={{3,2},{0,1},{7,6},{4,5},{11,10},{8,9},{15,14},{12,13},{19,18},{16,... | collective-permute-start | bytes 2654216 | tf_op jit(solution)/shard_map/ppermute | solution.py:773
  388.4 18.4 %collective-permute-start.98 = (bf16[3,96,768]{2,1,0:T(8,128)(2,1)}, bf16[3,96,768]{2,1,0:T(8,128)(2,1)}, u32[]{:S(2)}, u32[]{:S(2)}) collective-permute-start(bf16[3,96,768]{2,1,0:T(8,128)(2,1)} %fusion.36), channel_id=1, source_target_pairs={{0,8},{4,20},{8,0},{12,28},{16,24},{20,4},{24,16},{28,12},{1,9},{5... | collective-permute-start | bytes 1327112 | tf_op jit(solution)/shard_map/ppermute | solution.py:769
  409.1 18.2 %collective-permute-start.100 = (bf16[6,96,768]{2,1,0:T(8,128)(2,1)S(1)}, bf16[6,96,768]{2,1,0:T(8,128)(2,1)S(1)}, u32[]{:S(2)}, u32[]{:S(2)}) collective-permute-start(bf16[6,96,768]{2,1,0:T(8,128)(2,1)S(1)} %add_convert_fusion), channel_id=1, source_target_pairs={{2,1},{6,5},{10,9},{14,13},{18,17},{22,21},{26,25},{30,29}} | collective-permute-start | bytes 2654216 | tf_op jit(solution)/shard_map/ppermute | solution.py:773
  427.4 17.2 %collective-permute-start.105 = (bf16[3,96,768]{2,1,0:T(8,128)(2,1)S(1)}, bf16[3,96,768]{2,1,0:T(8,128)(2,1)S(1)}, u32[]{:S(2)}, u32[]{:S(2)}) collective-permute-start(bf16[3,96,768]{2,1,0:T(8,128)(2,1)S(1)} %add_convert_fusion.3), channel_id=1, source_target_pairs={{2,0},{6,4},{10,8},{14,12},{18,16},{22,20},{26,24},{30,28}} | collective-permute-start | bytes 1327112 | tf_op jit(solution)/shard_map/ppermute | solution.py:773
  (259 other events, 2898.2 us)
Sparse Core Ops, SparseCore 0:
  9.8 43.0 all-gather.4
  54.4 39.1 all-gather.6

commit v6 on v5

--- a/solution.py
+++ b/solution.py
@@ -847,10 +847,9 @@
 
     def __init__(self, weights, right_root):
         self.parts, self.chains, self.asked, self.sent = {}, {}, {}, {}
-        own = weights.astype(BF)
-        right_root = right_root.astype(BF)
-        self.plan = [PlaneGather(own[:HALF]), PlaneGather(own[HALF:])] + [PlaneGather(None) for _ in range(6)]
-        self.right = [PlaneGather(right_root[:HALF]), PlaneGather(right_root[HALF:])]
+        own, right_root = ([part[:HALF].astype(BF), part[HALF:].astype(BF)] for part in (weights, right_root))
+        self.plan = [PlaneGather(own[0]), PlaneGather(own[1])] + [PlaneGather(None) for _ in range(6)]
+        self.right = [PlaneGather(right_root[0]), PlaneGather(right_root[1])]
         for at, part in enumerate(self.plan):
             self.chains[f"place{at}"] = part.steps()
         for side in (0, 1):

time: 520 us -> 520 us (level)
  no operation moved by 1% of the time
where the time goes in v6:
time: 520 us; the launch traced here: 515 us
  Pallas kernels  173 us (33%)
  waiting for transfers between devices  168 us (32%)
  starting transfers between devices  102 us (20%)
  local copies, waits for them, and re-layouts  38.3 us (7%)
  other arithmetic  17.4 us (3%)
  between operations  16.5 us (3%)
    pallas_call x22, Pallas kernels, call(): pl.pallas_call(kernel, grid=grid, in_specs=in_specs, out_specs=out_specs,...  173 us
    ppermute x111, waiting for transfers between devices, swap(): lax.ppermute(array, 'dp', [(i, i ^ STEPS[axis][i % 2]) for i in range(DP)])  127 us
    ppermute x111, starting transfers between devices, swap(): lax.ppermute(array, 'dp', [(i, i ^ STEPS[axis][i % 2]) for i in range(DP)])  74.4 us
    ppermute x16, waiting for transfers between devices, hop(): return lax.ppermute(array, 'head', pairs)  31.1 us
    unnamed x326, local copies, waits for them, and re-layouts  29.4 us
    ppermute x16, starting transfers between devices, hop(): return lax.ppermute(array, 'head', pairs)  27.2 us
    all_gather x2, waiting for transfers between devices, gather_line(): lax.all_gather(array, 'head')  10.6 us
  transfers between devices with their start and end apart: 129, of which 42 were waited for; matrix products, arithmetic and copies ran while one was open for 3% of the time, Pallas kernels for 30%

profile of v6, /device:TPU:0, one launch (start us, length us, event | category | flops | bytes accessed | tf_op | source)
XLA Modules:
  0.0 515.0 jit_solution(12052349418659759076)
XLA Ops:
  14.8 8.7 %collective-permute-done.refs_1_.refs_17_.refs_33_ = bf16[3,96,768]{2,1,0:T(8,128)(2,1)S(1)} collective-permute-done((bf16[3,96,768]{2,1,0:T(8,128)(2,1)}, bf16[3,96,768]{2,1,0:T(8,128)(2,1)S(1)}, u32[]{:S(2)}, u32[]{:S(2)}) %collective-permute-start) | collective-permute-done | bytes 442400 | tf_op jit(solution)/shard_map/ppermute | solution.py:769
  42.2 10.6 %all-gather.5.cloned.1.call-done = bf16[12,96,768]{2,1,0:T(8,128)(2,1)} async-done(((bf16[3,96,768]{2,1,0:T(8,128)(2,1)}), bf16[12,96,768]{2,1,0:T(8,128)(2,1)}) %all-gather.5.cloned.1.call-update) | async-done | bytes 1769488 | tf_op jit(solution)/shard_map/all_gather | solution.py:862
  59.6 8.7 %collective-permute-done.14.refs_9_.refs_49_.refs_33_ = bf16[3,96,768]{2,1,0:T(8,128)(2,1)} collective-permute-done((bf16[3,96,768]{2,1,0:T(8,128)(2,1)S(1)}, bf16[3,96,768]{2,1,0:T(8,128)(2,1)}, u32[]{:S(2)}, u32[]{:S(2)}) %collective-permute-start.14) | collective-permute-done | bytes 442400 | tf_op jit(solution)/shard_map/ppermute | solution.py:769
  85.7 8.2 %qkv_in.2 = (bf16[624,768]{1,0:T(8,128)(2,1)S(1)}, bf16[624,2304]{1,0:T(8,128)(2,1)S(1)}, bf16[624,1536]{1,0:T(8,128)(2,1)S(1)}, f32[624,1536]{1,0:T(8,128)S(1)}) custom-call(bf16[624,768]{1,0:T(8,128)(2,1)S(1)} %bitcast.101, f32[1,768]{1,0:T(1,128)S(1)} %get-tuple-element.620.g_ref.c_ref, f32[2,1,768]{2,1,0:T(1,128)S(1)} %constant_dynamic-update-slice_fusion.c_ref, ...), custom_call_target="tpu_custom_call" | custom-call | flops 9900000256 | bytes 17630208 | tf_op jit(solution)/shard_map/qkv_in/pallas_call | solution.py:53
  108.8 5.4 %collective-permute-done.26.refs_9_ = bf16[3,96,768]{2,1,0:T(8,128)(2,1)S(1)} collective-permute-done((bf16[3,96,768]{2,1,0:T(8,128)(2,1)S(1)}, bf16[3,96,768]{2,1,0:T(8,128)(2,1)S(1)}, u32[]{:S(2)}, u32[]{:S(2)}) %collective-permute-start.26) | collective-permute-done | bytes 442400 | tf_op jit(solution)/shard_map/ppermute | solution.py:769
  118.0 9.2 %collective-permute-done.33.refs_25_.refs_17_ = bf16[3,96,768]{2,1,0:T(8,128)(2,1)S(1)} collective-permute-done((bf16[3,96,768]{2,1,0:T(8,128)(2,1)S(1)}, bf16[3,96,768]{2,1,0:T(8,128)(2,1)S(1)}, u32[]{:S(2)}, u32[]{:S(2)}) %collective-permute-start.33) | collective-permute-done | bytes 442400 | tf_op jit(solution)/shard_map/ppermute | solution.py:769
  134.9 10.1 %mlp_in.2 = (bf16[624,3072]{1,0:T(8,128)(2,1)S(1)}, bf16[624,3072]{1,0:T(8,128)(2,1)S(1)}) custom-call(bf16[624,768]{1,0:T(8,128)(2,1)S(1)} %get-tuple-element.495.h_ref.refs_0_, f32[1,3072]{1,0:T(1,128)S(1)} %get-tuple-element.622.b_ref, bf16[3,96,768]{2,1,0:T(8,128)(2,1)} %copy-done.36, bf16[3,96,768]{2,1,0:T(8,128)(2,1)} %copy-done.97, ...), custom_call_target="tpu_custom_call" | custom-call | flops 12099999744 | bytes 22794240 | tf_op jit(solution)/shard_map/mlp_in/pallas_call | solution.py:53
  152.8 8.0 %project.2.x_ref = f32[624,768]{1,0:T(8,128)S(1)} custom-call(bf16[624,768]{1,0:T(8,128)(2,1)S(1)} %bitcast.102, bf16[624,768]{1,0:T(8,128)(2,1)S(1)} %attend.2.o_ref.refs_2_, bf16[624,3072]{1,0:T(8,128)(2,1)S(1)} %get-tuple-element.354.a_ref.refs_4_, f32[1,768]{1,0:T(1,128)S(1)} %get-tuple-element.619.b_ref, ...), custom_call_target="tpu_custom_call" | custom-call | flops 8800000000 | bytes 21826560 | tf_op jit(solution)/shard_map/project/pallas_call | solution.py:53
  171.8 8.0 %qkv_in.3 = (bf16[624,768]{1,0:T(8,128)(2,1)S(1)}, bf16[624,2304]{1,0:T(8,128)(2,1)S(1)}, bf16[624,1536]{1,0:T(8,128)(2,1)S(1)}, f32[624,1536]{1,0:T(8,128)S(1)}) custom-call(f32[624,768]{1,0:T(8,128)S(1)} %project.2.x_ref, f32[1,768]{1,0:T(1,128)S(1)} %get-tuple-element.618.g_ref.c_ref, f32[2,1,768]{2,1,0:T(1,128)S(1)} %constant_dynamic-update-slice_fusion.2.c_ref, ...), custom_call_target="tpu_custom_call" | custom-call | flops 9900000256 | bytes 25666560 | tf_op jit(solution)/shard_map/qkv_in/pallas_call | solution.py:53
  190.3 10.6 %mlp_in.3 = (bf16[624,3072]{1,0:T(8,128)(2,1)S(1)}, bf16[624,3072]{1,0:T(8,128)(2,1)S(1)}) custom-call(bf16[624,768]{1,0:T(8,128)(2,1)S(1)} %get-tuple-element.433.h_ref.refs_0_, f32[1,3072]{1,0:T(1,128)S(1)} %get-tuple-element.621.b_ref, bf16[3,96,768]{2,1,0:T(8,128)(2,1)} %copy-done.36, bf16[3,96,768]{2,1,0:T(8,128)(2,1)} %copy-done.97, ...), custom_call_target="tpu_custom_call" | custom-call | flops 12099999744 | bytes 29872128 | tf_op jit(solution)/shard_map/mlp_in/pallas_call | solution.py:53
  201.0 7.6 %grad_out.2 = (bf16[5,96,768]{2,1,0:T(8,128)(2,1)}, bf16[5,96,768]{2,1,0:T(8,128)(2,1)}, bf16[5,96,768]{2,1,0:T(8,128)(2,1)}, bf16[5,96,768]{2,1,0:T(8,128)(2,1)}, bf16[4,5,96,768]{3,2,1,0:T(8,128)(2,1)}) custom-call(bf16[624,768]{1,0:T(8,128)(2,1)S(1)} %attend.3.refs_0_.o_ref, bf16[624,768]{1,0:T(8,128)(2,1)S(1)} %bitcast.104, ...), custom_call_target="tpu_custom_call" | custom-call | flops 8800000000 | bytes 12607488 | tf_op jit(solution)/shard_map/grad_out/pallas_call | solution.py:53
  211.5 8.1 %project.3 = bf16[624,768]{1,0:T(8,128)(2,1)S(1)} custom-call(f32[624,768]{1,0:T(8,128)S(1)} %project.2.x_ref, bf16[624,768]{1,0:T(8,128)(2,1)S(1)} %attend.3.refs_0_.o_ref, bf16[624,3072]{1,0:T(8,128)(2,1)S(1)} %get-tuple-element.391.refs_2_.a_ref, f32[1,768]{1,0:T(1,128)S(1)} %get-tuple-element.617.b_ref, ...), custom_call_target="tpu_custom_call" | custom-call | flops 8800000000 | bytes 21826560 | tf_op jit(solution)/shard_map/project/pallas_call | solution.py:53
  226.5 9.0 %mlp_back.2 = (bf16[624,768]{1,0:T(8,128)(2,1)}, bf16[624,768]{1,0:T(8,128)(2,1)S(1)}, bf16[624,3072]{1,0:T(8,128)(2,1)S(1)}, f32[1,768]{1,0:T(1,128)S(1)}, f32[1,3072]{1,0:T(1,128)S(1)}) custom-call(bf16[624,768]{1,0:T(8,128)(2,1)S(1)} %bitcast.106, bf16[624,3072]{1,0:T(8,128)(2,1)S(1)} %get-tuple-element.406.s_ref, ...), custom_call_target="tpu_custom_call" | custom-call | flops 9900000256 | bytes 24714240 | tf_op jit(solution)/shard_map/mlp_back/pallas_call | solution.py:53
  235.5 6.2 %grad_mlp.2 = (bf16[4,96,768]{2,1,0:T(8,128)(2,1)}, bf16[4,96,768]{2,1,0:T(8,128)(2,1)}, bf16[4,96,768]{2,1,0:T(8,128)(2,1)}, bf16[4,96,768]{2,1,0:T(8,128)(2,1)}, bf16[4,4,96,768]{3,2,1,0:T(8,128)(2,1)}) custom-call(bf16[624,768]{1,0:T(8,128)(2,1)S(1)} %get-tuple-element.433.h_ref.refs_0_, bf16[624,3072]{1,0:T(8,128)(2,1)S(1)} %get-tuple-element.409.refs_1_.du_ref), custom_call_target="tpu_custom_call" | custom-call | flops 7260000256 | bytes 9510912 | tf_op jit(solution)/shard_map/grad_mlp/pallas_call | solution.py:53
  241.7 5.4 %collective-permute-done.68.refs_11_ = bf16[3,96,768]{2,1,0:T(8,128)(2,1)S(1)} collective-permute-done((bf16[3,96,768]{2,1,0:T(8,128)(2,1)S(1)}, bf16[3,96,768]{2,1,0:T(8,128)(2,1)S(1)}, u32[]{:S(2)}, u32[]{:S(2)}) %collective-permute-start.68) | collective-permute-done | bytes 442400 | tf_op jit(solution)/shard_map/ppermute | solution.py:769
  249.4 8.4 %attend_back.2 = (bf16[624,2304]{1,0:T(8,128)(2,1)S(1)}, f32[2,1,768]{2,1,0:T(1,128)S(1)}) custom-call(bf16[624,768]{1,0:T(8,128)(2,1)S(1)} %get-tuple-element.420.do_ref, bf16[624,2304]{1,0:T(8,128)(2,1)S(1)} %get-tuple-element.374.z_ref, bf16[624,1536]{1,0:T(8,128)(2,1)S(1)} %get-tuple-element.421.u_ref, f32[624,1536]{1,0:T(8,128)S(1)} %get-tuple-element.422.i_ref, ...), custom_call_target="tpu_custom_call" | custom-call | flops 15399999488 | bytes 12472320 | tf_op jit(solution)/shard_map/attend_back/pallas_call | solution.py:53
  270.3 12.5 %stream_back.2 = (f32[624,768]{1,0:T(8,128)S(1)}, f32[1,768]{1,0:T(1,128)S(1)}) custom-call(bf16[624,768]{1,0:T(8,128)(2,1)S(1)} %bitcast.107, f32[624,768]{1,0:T(8,128)S(1)} %project.2.x_ref, f32[1,768]{1,0:T(1,128)S(1)} %get-tuple-element.618.g_ref.c_ref, bf16[624,3072]{1,0:T(8,128)(2,1)S(1)} %get-tuple-element.409.refs_1_.du_ref, ...), custom_call_target="tpu_custom_call" | custom-call | flops 13200000000 | bytes 39819264 | tf_op jit(solution)/shard_map/stream_back/pallas_call | solution.py:53
  290.0 8.4 %mlp_back.3 = (bf16[624,768]{1,0:T(8,128)(2,1)S(1)}, bf16[624,768]{1,0:T(8,128)(2,1)S(1)}, bf16[624,3072]{1,0:T(8,128)(2,1)S(1)}, f32[1,768]{1,0:T(1,128)S(1)}, f32[1,3072]{1,0:T(1,128)S(1)}) custom-call(f32[624,768]{1,0:T(8,128)S(1)} %get-tuple-element.511.g_ref, bf16[624,3072]{1,0:T(8,128)(2,1)S(1)} %copy-done.20, ...), custom_call_target="tpu_custom_call" | custom-call | flops 9900000256 | bytes 25672704 | tf_op jit(solution)/shard_map/mlp_back/pallas_call | solution.py:53
  307.6 9.4 %grad_out.3 = (bf16[6,96,768]{2,1,0:T(8,128)(2,1)}, bf16[6,96,768]{2,1,0:T(8,128)(2,1)}, bf16[6,96,768]{2,1,0:T(8,128)(2,1)}, bf16[6,96,768]{2,1,0:T(8,128)(2,1)}, bf16[4,6,96,768]{3,2,1,0:T(8,128)(2,1)}) custom-call(bf16[624,768]{1,0:T(8,128)(2,1)S(1)} %copy-done.28, bf16[624,3072]{1,0:T(8,128)(2,1)S(1)} %get-tuple-element.451.refs_1_.du_ref, ...), custom_call_target="tpu_custom_call" | custom-call | flops 10339999744 | bytes 18579456 | tf_op jit(solution)/shard_map/grad_out/pallas_call | solution.py:53
  330.9 6.8 %collective-permute-start.89 = (bf16[3,96,768]{2,1,0:T(8,128)(2,1)S(1)}, bf16[3,96,768]{2,1,0:T(8,128)(2,1)S(1)}, u32[]{:S(2)}, u32[]{:S(2)}) collective-permute-start(bf16[3,96,768]{2,1,0:T(8,128)(2,1)S(1)} %fusion.41), channel_id=1, source_target_pairs={{0,1},{3,2},{4,5},{7,6},{8,9},{11,10},{12,13},{15,14},{16,17},{19,... | collective-permute-start | bytes 1327112 | tf_op jit(solution)/shard_map/ppermute | solution.py:773
  338.7 8.5 %attend_back.3 = (bf16[624,2304]{1,0:T(8,128)(2,1)S(1)}, f32[2,1,768]{2,1,0:T(1,128)S(1)}) custom-call(bf16[624,768]{1,0:T(8,128)(2,1)S(1)} %get-tuple-element.483.do_ref, bf16[624,2304]{1,0:T(8,128)(2,1)S(1)} %copy-done.31, bf16[624,1536]{1,0:T(8,128)(2,1)S(1)} %copy-done.33, f32[624,1536]{1,0:T(8,128)S(1)} %copy-done.26, f32[2,1,768]{2,1,0:T(1,128)S(1)} %copy-done.8), custom_call_target="tpu_custom_call" | custom-call | flops 15399999488 | bytes 12472320 | tf_op jit(solution)/shard_map/attend_back/pallas_call | solution.py:53
  364.6 11.1 %collective-permute-done.95 = bf16[3,96,768]{2,1,0:T(8,128)(2,1)S(1)} collective-permute-done((bf16[3,96,768]{2,1,0:T(8,128)(2,1)S(1)}, bf16[3,96,768]{2,1,0:T(8,128)(2,1)S(1)}, u32[]{:S(2)}, u32[]{:S(2)}) %collective-permute-start.95) | collective-permute-done | bytes 442400 | tf_op jit(solution)/shard_map/ppermute | solution.py:769
  375.7 6.3 %collective-permute-done.96 = bf16[3,96,768]{2,1,0:T(8,128)(2,1)S(1)} collective-permute-done((bf16[3,96,768]{2,1,0:T(8,128)(2,1)S(1)}, bf16[3,96,768]{2,1,0:T(8,128)(2,1)S(1)}, u32[]{:S(2)}, u32[]{:S(2)}) %collective-permute-start.96) | collective-permute-done | bytes 442400 | tf_op jit(solution)/shard_map/ppermute | solution.py:769
  394.5 12.2 %stream_back.3 = (f32[624,768]{1,0:T(8,128)S(1)}, f32[1,768]{1,0:T(1,128)S(1)}) custom-call(f32[624,768]{1,0:T(8,128)S(1)} %copy-done.16, bf16[624,768]{1,0:T(8,128)(2,1)S(1)} %bitcast.103, f32[1,768]{1,0:T(1,128)S(1)} %copy-done.6, bf16[624,3072]{1,0:T(8,128)(2,1)S(1)} %copy-done.18, bf16[624,2304]{1,0:T(8,128)(2,1)S(1)} %copy-done.22, ...), custom_call_target="tpu_custom_call" | custom-call | flops 13200000000 | bytes 29202432 | tf_op jit(solution)/shard_map/stream_back/pallas_call | solution.py:53
  417.6 8.3 %collective-permute-done.101 = bf16[3,96,768]{2,1,0:T(8,128)(2,1)S(1)} collective-permute-done((bf16[3,96,768]{2,1,0:T(8,128)(2,1)S(1)}, bf16[3,96,768]{2,1,0:T(8,128)(2,1)S(1)}, u32[]{:S(2)}, u32[]{:S(2)}) %collective-permute-start.101) | collective-permute-done | bytes 442400 | tf_op jit(solution)/shard_map/ppermute | solution.py:773
  432.3 6.4 %collective-permute-done.107 = f32[2,4736]{1,0:T(2,128)S(1)} collective-permute-done((f32[2,4736]{1,0:T(2,128)S(1)}, f32[2,4736]{1,0:T(2,128)S(1)}, u32[]{:S(2)}, u32[]{:S(2)}) %collective-permute-start.107) | collective-permute-done | bytes 37920 | tf_op jit(solution)/shard_map/ppermute | solution.py:769
  438.7 6.0 %collective-permute-done.105 = bf16[3,96,768]{2,1,0:T(8,128)(2,1)S(1)} collective-permute-done((bf16[3,96,768]{2,1,0:T(8,128)(2,1)S(1)}, bf16[3,96,768]{2,1,0:T(8,128)(2,1)S(1)}, u32[]{:S(2)}, u32[]{:S(2)}) %collective-permute-start.105) | collective-permute-done | bytes 442400 | tf_op jit(solution)/shard_map/ppermute | solution.py:773
  450.6 5.7 %collective-permute-done.111 = f32[2,4736]{1,0:T(2,128)S(1)} collective-permute-done((f32[2,4736]{1,0:T(2,128)S(1)}, f32[2,4736]{1,0:T(2,128)S(1)}, u32[]{:S(2)}, u32[]{:S(2)}) %collective-permute-start.111) | collective-permute-done | bytes 37920 | tf_op jit(solution)/shard_map/ppermute | solution.py:769
  463.2 9.8 %collective-permute-done.116 = f32[2,4736]{1,0:T(2,128)S(1)} collective-permute-done((f32[2,4736]{1,0:T(2,128)S(1)}, f32[2,4736]{1,0:T(2,128)S(1)}, u32[]{:S(2)}, u32[]{:S(2)}) %collective-permute-start.116) | collective-permute-done | bytes 37920 | tf_op jit(solution)/shard_map/ppermute | solution.py:773
  480.9 5.6 %collective-permute-done.119.refs_1_ = bf16[3,96,768]{2,1,0:T(8,128)(2,1)S(1)} collective-permute-done((bf16[3,96,768]{2,1,0:T(8,128)(2,1)S(1)}, bf16[3,96,768]{2,1,0:T(8,128)(2,1)S(1)}, u32[]{:S(2)}, u32[]{:S(2)}) %collective-permute-start.119) | collective-permute-done | bytes 442400 | tf_op jit(solution)/shard_map/ppermute | solution.py:769
  488.1 8.7 %shampoo.2 = (f32[6,96,768]{2,1,0:T(8,128)}, f32[6,96,768]{2,1,0:T(8,128)}, f32[6,96,768]{2,1,0:T(8,128)}, f32[6,96,768]{2,1,0:T(8,128)}, f32[6,96,768]{2,1,0:T(8,128)}) custom-call(f32[3,96,768]{2,1,0:T(8,128)S(1)} %get-tuple-element.555.g_ref, f32[6,96,768]{2,1,0:T(8,128)S(1)} %copy-done.9, f32[6,96,768]{2,1,0:T(8,128)S(1)} %copy-done.10, ...), custom_call_target="tpu_custom_call" | custom-call | flops 12099999744 | bytes 25657344 | tf_op jit(solution)/shard_map/shampoo/pallas_call | solution.py:53
  499.5 8.4 %shampoo.3 = (f32[6,96,768]{2,1,0:T(8,128)}, f32[6,96,768]{2,1,0:T(8,128)}, f32[6,96,768]{2,1,0:T(8,128)}, f32[6,96,768]{2,1,0:T(8,128)}, f32[6,96,768]{2,1,0:T(8,128)}) custom-call(f32[3,96,768]{2,1,0:T(8,128)S(1)} %get-tuple-element.592.g_ref, ...), custom_call_target="tpu_custom_call", output_to_operand_aliasing={{0}: (22, {}), {1}: (23, {}), {2}: (24, {}), {3}: (25, {}),... | custom-call | flops 12099999744 | bytes 34504704 | tf_op jit(solution)/shard_map/shampoo/pallas_call | solution.py:53
  (653 shorter events, 232.4 us)
Async XLA Ops:
  7.2 45.6 %all-gather.5.cloned.1.call-start = ((), (), s32[]{:S(2)}) async-start(), calls=%async_computation | async-start | bytes 2211840 | tf_op jit(solution)/shard_map/all_gather | solution.py:862
  9.6 89.6 %all-gather.7.cloned.1.call-start = ((), (), s32[]{:S(2)}) async-start(), calls=%async_computation.1 | async-start | bytes 2211840 | tf_op jit(solution)/shard_map/all_gather | solution.py:862
  14.2 18.6 %collective-permute-start.5 = (bf16[3,96,768]{2,1,0:T(8,128)(2,1)S(1)}, bf16[3,96,768]{2,1,0:T(8,128)(2,1)S(1)}, u32[]{:S(2)}, u32[]{:S(2)}) collective-permute-start(bf16[3,96,768]{2,1,0:T(8,128)(2,1)S(1)} %get-tuple-element.615.refs_0_.refs_16_), channel_id=1, source_target_pairs={{0,8},{4,20},{8,0},{12,28},{16,24},{20,4},{24,16},{28,12},{1,9},{5... | collective-permute-start | bytes 1327112 | tf_op jit(solution)/shard_map/ppermute | solution.py:769
  14.8 18.1 %collective-permute-start.6 = (bf16[3,96,768]{2,1,0:T(8,128)(2,1)S(1)}, bf16[3,96,768]{2,1,0:T(8,128)(2,1)S(1)}, u32[]{:S(2)}, u32[]{:S(2)}) collective-permute-start(bf16[3,96,768]{2,1,0:T(8,128)(2,1)S(1)} %get-tuple-element.615.refs_0_.refs_16_), channel_id=1, source_target_pairs={{0,16},{4,12},{8,24},{12,4},{16,0},{20,28},{24,8},{28,20},{1,17},{... | collective-permute-start | bytes 1327112 | tf_op jit(solution)/shard_map/ppermute | solution.py:769
  14.8 20.7 %collective-permute-start.3 = (bf16[3,96,768]{2,1,0:T(8,128)(2,1)}, bf16[3,96,768]{2,1,0:T(8,128)(2,1)S(1)}, u32[]{:S(2)}, u32[]{:S(2)}) collective-permute-start(bf16[3,96,768]{2,1,0:T(8,128)(2,1)} %get-tuple-element.616.refs_0_.refs_16_.refs_32_), channel_id=1, source_target_pairs={{0,4},{4,0},{8,12},{12,8},{16,20},{20,16},{24,28},{28,24},{1,5},{5... | collective-permute-start | bytes 1327112 | tf_op jit(solution)/shard_map/ppermute | solution.py:769
  37.1 19.9 %collective-permute-start.10 = (bf16[3,96,768]{2,1,0:T(8,128)(2,1)S(1)}, bf16[3,96,768]{2,1,0:T(8,128)(2,1)}, u32[]{:S(2)}, u32[]{:S(2)}) collective-permute-start(bf16[3,96,768]{2,1,0:T(8,128)(2,1)S(1)} %collective-permute-done.1.refs_2_.refs_18_.refs_34_), channel_id=1, source_target_pairs={{0,4},{4,0},{8,12},{12,8},{16,20},{20,16},{24,28},{28,24},{1,5},{5... | collective-permute-start | bytes 1327112 | tf_op jit(solution)/shard_map/ppermute | solution.py:769
  37.4 21.0 %collective-permute-start.12 = (bf16[3,96,768]{2,1,0:T(8,128)(2,1)S(1)}, bf16[3,96,768]{2,1,0:T(8,128)(2,1)S(1)}, u32[]{:S(2)}, u32[]{:S(2)}) collective-permute-start(bf16[3,96,768]{2,1,0:T(8,128)(2,1)S(1)} %collective-permute-done.6.refs_2_.refs_18_), channel_id=1, source_target_pairs={{0,4},{4,0},{8,12},{12,8},{16,20},{20,16},{24,28},{28,24},{1,5},{5... | collective-permute-start | bytes 1327112 | tf_op jit(solution)/shard_map/ppermute | solution.py:769
  58.4 19.4 %collective-permute-start.19 = (bf16[3,96,768]{2,1,0:T(8,128)(2,1)S(1)}, bf16[3,96,768]{2,1,0:T(8,128)(2,1)}, u32[]{:S(2)}, u32[]{:S(2)}) collective-permute-start(bf16[3,96,768]{2,1,0:T(8,128)(2,1)S(1)} %get-tuple-element.611.refs_24_.refs_8_.refs_16_.refs_56_), channel_id=1, source_target_pairs={{0,8},{4,20},{8,0},{12,28},{16,24},{20,4},{24,16},{28,12},{1,9},{5... | collective-permute-start | bytes 1327112 | tf_op jit(solution)/shard_map/ppermute | solution.py:769
  59.1 18.7 %collective-permute-start.20 = (bf16[3,96,768]{2,1,0:T(8,128)(2,1)S(1)}, bf16[3,96,768]{2,1,0:T(8,128)(2,1)}, u32[]{:S(2)}, u32[]{:S(2)}) collective-permute-start(bf16[3,96,768]{2,1,0:T(8,128)(2,1)S(1)} %get-tuple-element.611.refs_24_.refs_8_.refs_16_.refs_56_), channel_id=1, source_target_pairs={{0,16},{4,12},{8,24},{12,4},{16,0},{20,28},{24,8},{28,20},{1,17},{... | collective-permute-start | bytes 1327112 | tf_op jit(solution)/shard_map/ppermute | solution.py:769
  101.0 16.5 %collective-permute-start.31 = (bf16[3,96,768]{2,1,0:T(8,128)(2,1)S(1)}, bf16[3,96,768]{2,1,0:T(8,128)(2,1)S(1)}, u32[]{:S(2)}, u32[]{:S(2)}) collective-permute-start(bf16[3,96,768]{2,1,0:T(8,128)(2,1)S(1)} %get-tuple-element.325.refs_8_), channel_id=1, source_target_pairs={{0,4},{4,0},{8,12},{12,8},{16,20},{20,16},{24,28},{28,24},{1,5},{5... | collective-permute-start | bytes 1327112 | tf_op jit(solution)/shard_map/ppermute | solution.py:769
  223.0 24.1 %collective-permute-start.66 = (bf16[5,96,768]{2,1,0:T(8,128)(2,1)S(1)}, bf16[5,96,768]{2,1,0:T(8,128)(2,1)S(1)}, u32[]{:S(2)}, u32[]{:S(2)}) collective-permute-start(bf16[5,96,768]{2,1,0:T(8,128)(2,1)S(1)} %get-tuple-element.411), channel_id=1, source_target_pairs={{0,16},{4,12},{8,24},{12,4},{16,0},{20,28},{24,8},{28,20},{1,17},{... | collective-permute-start | bytes 2211848 | tf_op jit(solution)/shard_map/ppermute | solution.py:769
  223.9 23.2 %collective-permute-start.67 = (bf16[5,96,768]{2,1,0:T(8,128)(2,1)S(1)}, bf16[5,96,768]{2,1,0:T(8,128)(2,1)S(1)}, u32[]{:S(2)}, u32[]{:S(2)}) collective-permute-start(bf16[5,96,768]{2,1,0:T(8,128)(2,1)S(1)} %get-tuple-element.412), channel_id=1, source_target_pairs={{0,16},{4,12},{8,24},{12,4},{16,0},{20,28},{24,8},{28,20},{1,17},{... | collective-permute-start | bytes 2211848 | tf_op jit(solution)/shard_map/ppermute | solution.py:769
  225.0 22.1 %collective-permute-start.68 = (bf16[3,96,768]{2,1,0:T(8,128)(2,1)S(1)}, bf16[3,96,768]{2,1,0:T(8,128)(2,1)S(1)}, u32[]{:S(2)}, u32[]{:S(2)}) collective-permute-start(bf16[3,96,768]{2,1,0:T(8,128)(2,1)S(1)} %collective-permute-done.64.refs_9_), channel_id=1, source_target_pairs={{0,16},{4,12},{8,24},{12,4},{16,0},{20,28},{24,8},{28,20},{1,17},{... | collective-permute-start | bytes 1327112 | tf_op jit(solution)/shard_map/ppermute | solution.py:769
  226.0 21.1 %collective-permute-start.69 = (bf16[3,96,768]{2,1,0:T(8,128)(2,1)S(1)}, bf16[3,96,768]{2,1,0:T(8,128)(2,1)S(1)}, u32[]{:S(2)}, u32[]{:S(2)}) collective-permute-start(bf16[3,96,768]{2,1,0:T(8,128)(2,1)S(1)} %copy-done.58), channel_id=1, source_target_pairs={{0,4},{4,0},{8,12},{12,8},{16,20},{20,16},{24,28},{28,24},{1,5},{5... | collective-permute-start | bytes 1327112 | tf_op jit(solution)/shard_map/ppermute | solution.py:769
  226.0 21.1 %collective-permute-start.70 = (bf16[3,96,768]{2,1,0:T(8,128)(2,1)S(1)}, bf16[3,96,768]{2,1,0:T(8,128)(2,1)S(1)}, u32[]{:S(2)}, u32[]{:S(2)}) collective-permute-start(bf16[3,96,768]{2,1,0:T(8,128)(2,1)S(1)} %collective-permute-done.64.refs_9_), channel_id=1, source_target_pairs={{0,4},{4,0},{8,12},{12,8},{16,20},{20,16},{24,28},{28,24},{1,5},{5... | collective-permute-start | bytes 1327112 | tf_op jit(solution)/shard_map/ppermute | solution.py:769
  265.8 18.7 %collective-permute-start.78 = (bf16[4,3,96,768]{3,2,1,0:T(8,128)(2,1)}, bf16[4,3,96,768]{3,2,1,0:T(8,128)(2,1)S(1)}, u32[]{:S(2)}, u32[]{:S(2)}) collective-permute-start(bf16[4,3,96,768]{3,2,1,0:T(8,128)(2,1)} %get-tuple-element.441), channel_id=1, source_target_pairs={{0,4},{4,0},{8,12},{12,8},{16,20},{20,16},{24,28},{28,24},{1,5},{5... | collective-permute-start | bytes 5308424 | tf_op jit(solution)/shard_map/ppermute | solution.py:769
  265.9 18.7 %collective-permute-start.75 = (bf16[5,96,768]{2,1,0:T(8,128)(2,1)S(1)}, bf16[5,96,768]{2,1,0:T(8,128)(2,1)S(1)}, u32[]{:S(2)}, u32[]{:S(2)}) collective-permute-start(bf16[5,96,768]{2,1,0:T(8,128)(2,1)S(1)} %fusion.13), channel_id=1, source_target_pairs={{0,1},{2,3},{4,5},{6,7},{8,9},{10,11},{12,13},{14,15},{16,17},{18,... | collective-permute-start | bytes 2211848 | tf_op jit(solution)/shard_map/ppermute | solution.py:773
  287.1 30.0 %collective-permute-start.80 = (bf16[5,96,768]{2,1,0:T(8,128)(2,1)S(1)}, bf16[5,96,768]{2,1,0:T(8,128)(2,1)S(1)}, u32[]{:S(2)}, u32[]{:S(2)}) collective-permute-start(bf16[5,96,768]{2,1,0:T(8,128)(2,1)S(1)} %add_convert_fusion.1), channel_id=1, source_target_pairs={{1,3},{5,7},{9,11},{13,15},{17,19},{21,23},{25,27},{29,31}} | collective-permute-start | bytes 2211848 | tf_op jit(solution)/shard_map/ppermute | solution.py:773
  287.8 29.2 %collective-permute-start.83 = (bf16[3,96,768]{2,1,0:T(8,128)(2,1)S(1)}, bf16[3,96,768]{2,1,0:T(8,128)(2,1)S(1)}, u32[]{:S(2)}, u32[]{:S(2)}) collective-permute-start(bf16[3,96,768]{2,1,0:T(8,128)(2,1)S(1)} %get-tuple-element.463), channel_id=1, source_target_pairs={{0,16},{4,12},{8,24},{12,4},{16,0},{20,28},{24,8},{28,20},{1,17},{... | collective-permute-start | bytes 1327112 | tf_op jit(solution)/shard_map/ppermute | solution.py:769
  288.8 28.3 %collective-permute-start.84 = (bf16[3,96,768]{2,1,0:T(8,128)(2,1)S(1)}, bf16[3,96,768]{2,1,0:T(8,128)(2,1)S(1)}, u32[]{:S(2)}, u32[]{:S(2)}) collective-permute-start(bf16[3,96,768]{2,1,0:T(8,128)(2,1)S(1)} %get-tuple-element.464), channel_id=1, source_target_pairs={{0,16},{4,12},{8,24},{12,4},{16,0},{20,28},{24,8},{28,20},{1,17},{... | collective-permute-start | bytes 1327112 | tf_op jit(solution)/shard_map/ppermute | solution.py:769
  329.4 19.0 %collective-permute-start.90 = (bf16[4,3,96,768]{3,2,1,0:T(8,128)(2,1)S(1)}, bf16[4,3,96,768]{3,2,1,0:T(8,128)(2,1)S(1)}, u32[]{:S(2)}, u32[]{:S(2)}) collective-permute-start(bf16[4,3,96,768]{3,2,1,0:T(8,128)(2,1)S(1)} %copy-done.94), channel_id=1, source_target_pairs={{0,4},{4,0},{8,12},{12,8},{16,20},{20,16},{24,28},{28,24},{1,5},{5... | collective-permute-start | bytes 5308424 | tf_op jit(solution)/shard_map/ppermute | solution.py:769
  329.4 19.0 %collective-permute-start.87 = (bf16[3,96,768]{2,1,0:T(8,128)(2,1)S(1)}, bf16[3,96,768]{2,1,0:T(8,128)(2,1)S(1)}, u32[]{:S(2)}, u32[]{:S(2)}) collective-permute-start(bf16[3,96,768]{2,1,0:T(8,128)(2,1)S(1)} %get-tuple-element.487), channel_id=1, source_target_pairs={{1,2},{5,6},{9,10},{13,14},{17,18},{21,22},{25,26},{29,30}} | collective-permute-start | bytes 1327112 | tf_op jit(solution)/shard_map/ppermute | solution.py:773
  330.2 17.0 %collective-permute-start.88 = (bf16[1,96,768]{2,1,0:T(8,128)(2,1)S(1)}, bf16[1,96,768]{2,1,0:T(8,128)(2,1)S(1)}, u32[]{:S(2)}, u32[]{:S(2)}) collective-permute-start(bf16[1,96,768]{2,1,0:T(8,128)(2,1)S(1)} %add_convert_fusion.6), channel_id=1, source_target_pairs={{1,3},{5,7},{9,11},{13,15},{17,19},{21,23},{25,27},{29,31}} | collective-permute-start | bytes 442376 | tf_op jit(solution)/shard_map/ppermute | solution.py:773
  330.9 17.5 %collective-permute-start.89 = (bf16[3,96,768]{2,1,0:T(8,128)(2,1)S(1)}, bf16[3,96,768]{2,1,0:T(8,128)(2,1)S(1)}, u32[]{:S(2)}, u32[]{:S(2)}) collective-permute-start(bf16[3,96,768]{2,1,0:T(8,128)(2,1)S(1)} %fusion.41), channel_id=1, source_target_pairs={{0,1},{3,2},{4,5},{7,6},{8,9},{11,10},{12,13},{15,14},{16,17},{19,... | collective-permute-start | bytes 1327112 | tf_op jit(solution)/shard_map/ppermute | solution.py:773
  337.7 17.6 %collective-permute-start.91 = (bf16[6,96,768]{2,1,0:T(8,128)(2,1)S(1)}, bf16[6,96,768]{2,1,0:T(8,128)(2,1)S(1)}, u32[]{:S(2)}, u32[]{:S(2)}) collective-permute-start(bf16[6,96,768]{2,1,0:T(8,128)(2,1)S(1)} %get-tuple-element.498), channel_id=1, source_target_pairs={{0,16},{4,12},{8,24},{12,4},{16,0},{20,28},{24,8},{28,20},{1,17},{... | collective-permute-start | bytes 2654216 | tf_op jit(solution)/shard_map/ppermute | solution.py:769
  361.4 21.2 %collective-permute-start.94 = (bf16[6,96,768]{2,1,0:T(8,128)(2,1)S(1)}, bf16[6,96,768]{2,1,0:T(8,128)(2,1)S(1)}, u32[]{:S(2)}, u32[]{:S(2)}) collective-permute-start(bf16[6,96,768]{2,1,0:T(8,128)(2,1)S(1)} %fusion.1), channel_id=1, source_target_pairs={{0,8},{4,20},{8,0},{12,28},{16,24},{20,4},{24,16},{28,12},{1,9},{5... | collective-permute-start | bytes 2654216 | tf_op jit(solution)/shard_map/ppermute | solution.py:769
  363.7 18.3 %collective-permute-start.96 = (bf16[3,96,768]{2,1,0:T(8,128)(2,1)S(1)}, bf16[3,96,768]{2,1,0:T(8,128)(2,1)S(1)}, u32[]{:S(2)}, u32[]{:S(2)}) collective-permute-start(bf16[3,96,768]{2,1,0:T(8,128)(2,1)S(1)} %get-tuple-element.505), channel_id=1, source_target_pairs={{0,16},{4,12},{8,24},{12,4},{16,0},{20,28},{24,8},{28,20},{1,17},{... | collective-permute-start | bytes 1327112 | tf_op jit(solution)/shard_map/ppermute | solution.py:769
  385.0 22.4 %collective-permute-start.99 = (bf16[4,3,96,768]{3,2,1,0:T(8,128)(2,1)}, bf16[4,3,96,768]{3,2,1,0:T(8,128)(2,1)}, u32[]{:S(2)}, u32[]{:S(2)}) collective-permute-start(bf16[4,3,96,768]{3,2,1,0:T(8,128)(2,1)} %get-tuple-element.515), channel_id=1, source_target_pairs={{0,4},{4,0},{8,12},{12,8},{16,20},{20,16},{24,28},{28,24},{1,5},{5... | collective-permute-start | bytes 5308424 | tf_op jit(solution)/shard_map/ppermute | solution.py:769
  385.5 21.9 %collective-permute-start.97 = (bf16[6,96,768]{2,1,0:T(8,128)(2,1)}, bf16[6,96,768]{2,1,0:T(8,128)(2,1)}, u32[]{:S(2)}, u32[]{:S(2)}) collective-permute-start(bf16[6,96,768]{2,1,0:T(8,128)(2,1)} %fusion.6), channel_id=1, source_target_pairs={{3,2},{0,1},{7,6},{4,5},{11,10},{8,9},{15,14},{12,13},{19,18},{16,... | collective-permute-start | bytes 2654216 | tf_op jit(solution)/shard_map/ppermute | solution.py:773
  388.4 18.4 %collective-permute-start.98 = (bf16[3,96,768]{2,1,0:T(8,128)(2,1)}, bf16[3,96,768]{2,1,0:T(8,128)(2,1)}, u32[]{:S(2)}, u32[]{:S(2)}) collective-permute-start(bf16[3,96,768]{2,1,0:T(8,128)(2,1)} %fusion.36), channel_id=1, source_target_pairs={{0,8},{4,20},{8,0},{12,28},{16,24},{20,4},{24,16},{28,12},{1,9},{5... | collective-permute-start | bytes 1327112 | tf_op jit(solution)/shard_map/ppermute | solution.py:769
  409.1 18.2 %collective-permute-start.100 = (bf16[6,96,768]{2,1,0:T(8,128)(2,1)S(1)}, bf16[6,96,768]{2,1,0:T(8,128)(2,1)S(1)}, u32[]{:S(2)}, u32[]{:S(2)}) collective-permute-start(bf16[6,96,768]{2,1,0:T(8,128)(2,1)S(1)} %add_convert_fusion), channel_id=1, source_target_pairs={{2,1},{6,5},{10,9},{14,13},{18,17},{22,21},{26,25},{30,29}} | collective-permute-start | bytes 2654216 | tf_op jit(solution)/shard_map/ppermute | solution.py:773
  427.4 17.2 %collective-permute-start.105 = (bf16[3,96,768]{2,1,0:T(8,128)(2,1)S(1)}, bf16[3,96,768]{2,1,0:T(8,128)(2,1)S(1)}, u32[]{:S(2)}, u32[]{:S(2)}) collective-permute-start(bf16[3,96,768]{2,1,0:T(8,128)(2,1)S(1)} %add_convert_fusion.3), channel_id=1, source_target_pairs={{2,0},{6,4},{10,8},{14,12},{18,16},{22,20},{26,24},{30,28}} | collective-permute-start | bytes 1327112 | tf_op jit(solution)/shard_map/ppermute | solution.py:773
  (259 other events, 2898.2 us)
Sparse Core Ops, SparseCore 0:
  9.8 43.0 all-gather.4
  54.4 39.1 all-gather.6
